TPU v7x, 128 devices: a whole 4x4x4 slice. The times are simulated.
128 devices in a mesh: gx: 8 (over y_hi, z), gy: 16 (over x, y_lo, core).
Axes of the slice: x: 4, y: 4 (y_hi: 2, y_lo: 2; y = y_hi * 2 + y_lo), z: 4, core: 2. Of those that a mesh axis runs over, the one named last changes fastest.
Arguments:
- well_cell: int32 [65536], P(('gx', 'gy')), may hold values from 0 to 4194303, as said below
- well_test: int32 [65536], P(('gx', 'gy')), may hold values from 0 to 3
- well_value: float32 [65536], P(('gx', 'gy')), may hold values from -6 to 6
- cond_class: int32 [32, 64, 2048], P('gx', None, 'gy'), may hold values from 0 to 15
- class_value: float32 [16], replicated, may hold values from 0.1 to 3
- zone_id: int32 [32, 64, 2048], P('gx', None, 'gy'), may hold values from 0 to 98303
- drawdown: bfloat16 [4, 32, 64, 2048], P(None, 'gx', None, 'gy'), may hold values from -6 to 6
- centroid: float32 [3, 98304], replicated, may hold values from 0 to 1
Outputs:
- prior_product: bfloat16 [4, 98304], P(None, ('gx', 'gy'))
Inputs may be any that keep to these rules, and one draw needn't show every extreme that they name: `well_cell`: rows s * 512 to (s + 1) * 512 - 1 belong to device s (gx first). At most 16 of one device's rows lie in the cells of any one device, and in every draw some device holds 16 rows of every device's block.
All inputs are finite; a program needn't handle non-finite values.
Results may differ from a plain program's by a relative error of at most 0.0065.
Values may be sent and summed in bfloat16 or wider, within the bound.
A program may use at most 192 MiB of HBM per device.

v0:
```python
import jax
import jax.numpy as jnp
from jax import lax
from jax.sharding import PartitionSpec as P

SWEEPS = 12
ZONES = 98304


storage = 0.02
lam_low = 0.02
lam_high = 36.02
corr_len = 0.1


def padded_2(value, sides, width):
    for axis, dim in sides:
        size, length = (lax.axis_size(axis), value.shape[dim])
        up = [(i, (i + 1) % size) for i in range(size - 1)]
        down = [(j, i) for i, j in up]
        last = lax.slice_in_dim(value, length - width, length, axis=dim)
        initial = lax.slice_in_dim(value, 0, width, axis=dim)
        before = lax.ppermute(last, axis, up)
        after = lax.ppermute(initial, axis, down)
        value = jnp.concatenate([before, value, after], axis=dim)
    return value


def cheb_setup():
    middle = 0.5 * (lam_high + lam_low)
    spread = 0.5 * (lam_high - lam_low)
    ratio_mid = middle / spread
    current = 1.0 / ratio_mid
    factors = []
    for counter in range(SWEEPS - 1):
        updated = 1.0 / (2.0 * ratio_mid - current)
        factors.append((updated * current, 2.0 * updated / spread))
        current = updated
    return (middle, factors)


def apply_operator(padded, cond_pad):
    centre = padded[..., 1:-1, 1:-1, 1:-1]
    cond_mid = cond_pad[..., 1:-1, 1:-1, 1:-1]
    result = storage * centre
    pairs = [
        (padded[..., 2:, 1:-1, 1:-1], cond_pad[..., 2:, 1:-1, 1:-1]),
        (padded[..., :-2, 1:-1, 1:-1], cond_pad[..., :-2, 1:-1, 1:-1]),
        (padded[..., 1:-1, 2:, 1:-1], cond_pad[..., 1:-1, 2:, 1:-1]),
        (padded[..., 1:-1, :-2, 1:-1], cond_pad[..., 1:-1, :-2, 1:-1]),
        (padded[..., 1:-1, 1:-1, 2:], cond_pad[..., 1:-1, 1:-1, 2:]),
        (padded[..., 1:-1, 1:-1, :-2], cond_pad[..., 1:-1, 1:-1, :-2]),
    ]
    for beside, cond_side in pairs:
        result = result + 0.5 * (cond_mid + cond_side) * (centre - beside)
    return result


def pad_layers(values):
    widths = [(0, 0)] * values.ndim
    widths[-2] = (1, 1)
    return jnp.pad(values, widths)


def covariance(col_pts, row_pts):
    squared = (col_pts[0][:, None] - row_pts[0][None, :]) ** 2
    squared = squared + (col_pts[1][:, None] - row_pts[1][None, :]) ** 2
    squared = squared + (col_pts[2][:, None] - row_pts[2][None, :]) ** 2
    return jnp.exp(-jnp.sqrt(squared) / corr_len).astype(jnp.bfloat16)


def per_device(
    well_cell, well_test, well_value, cond_class, class_value, zone_id, drawdown, centroid
):
    size_gx = lax.axis_size("gx")
    size_gy = lax.axis_size("gy")
    tests, width_x, layers, width_y = drawdown.shape
    cells_dev = width_x * layers * width_y
    index_gx = lax.axis_index("gx")
    index_gy = lax.axis_index("gy")
    my_device = index_gx * size_gy + index_gy
    classes = jnp.arange(class_value.shape[0], dtype=jnp.int32)
    conduct = jnp.sum(
        jnp.where(
            cond_class[None] == classes[:, None, None, None], class_value[:, None, None, None], 0.0
        ),
        axis=0,
    )
    grid_y = width_y * size_gy
    plane_size = layers * grid_y
    glob_x = well_cell // plane_size
    remain = well_cell % plane_size
    glob_z = remain // grid_y
    glob_y = remain % grid_y
    owner_dev = glob_x // width_x * size_gy + glob_y // width_y
    local_cell = (glob_x % width_x * layers + glob_z) * width_y + glob_y % width_y
    cell_code = well_test * cells_dev + local_cell
    packed = jnp.stack([owner_dev.astype(jnp.float32), cell_code.astype(jnp.float32), well_value])
    whole = lax.all_gather(packed, ("gx", "gy"), axis=1, tiled=True)
    mine = whole[0].astype(jnp.int32) == my_device
    codes = jnp.where(mine, whole[1].astype(jnp.int32), 0)
    amounts = jnp.where(mine, whole[2], 0.0)
    source = (
        jnp.zeros((tests * cells_dev,), jnp.float32)
        .at[codes]
        .add(amounts)
        .reshape(tests, width_x, layers, width_y)
    )
    middle, factors = cheb_setup()
    keep_table = jnp.asarray([pair[0] for pair in factors] + [0.0], jnp.float32)
    new_table = jnp.asarray([pair[1] for pair in factors] + [0.0], jnp.float32)
    solution = jnp.zeros_like(source)
    direction = source / middle
    cond_pad = pad_layers(padded_2(conduct, (("gx", 0), ("gy", 2)), 1))

    def sweep_each(counter, carry):
        solution_now, residual_now, direction_now = carry
        rimmed = padded_2(direction_now, (("gx", 1), ("gy", 3)), 1)
        applied = apply_operator(pad_layers(rimmed), cond_pad)
        solution_now = solution_now + direction_now
        residual_now = residual_now - applied
        direction_now = keep_table[counter] * direction_now + new_table[counter] * residual_now
        return (solution_now, residual_now, direction_now)

    solution, residual, direction = lax.fori_loop(
        0, SWEEPS, sweep_each, (solution, source, direction)
    )
    sensitive = conduct[None] * drawdown.astype(jnp.float32) * solution
    zone_flat = zone_id.reshape(-1)
    partial_value = jax.vmap(
        lambda test_row: jax.ops.segment_sum(test_row, zone_flat, num_segments=ZONES)
    )(sensitive.reshape(tests, cells_dev))
    zone_share = ZONES // (size_gx * size_gy)
    rows_len = ZONES // size_gx
    cols_len = ZONES // size_gy
    share = lax.psum_scatter(partial_value, ("gx", "gy"), scatter_dimension=1, tiled=True)
    zone_cols = lax.all_gather(share.astype(jnp.bfloat16), "gx", axis=1, tiled=True)
    col_pts = lax.dynamic_index_in_dim(
        centroid.reshape(3, size_gx, size_gy, zone_share), index_gy, 2, keepdims=False
    ).reshape(3, cols_len)
    row_pts = lax.dynamic_slice_in_dim(centroid, index_gx * rows_len, rows_len, 1)
    block_len = min(1024, rows_len)

    def tile_product(start):
        block_pts = lax.dynamic_slice_in_dim(row_pts, start, block_len, 1)
        return jnp.dot(
            zone_cols, covariance(col_pts, block_pts), preferred_element_type=jnp.float32
        )

    pieces = lax.map(tile_product, jnp.arange(rows_len // block_len, dtype=jnp.int32) * block_len)
    partial_out = jnp.moveaxis(pieces, 0, 1).reshape(tests, rows_len)
    return lax.psum_scatter(partial_out, "gy", scatter_dimension=1, tiled=True).astype(jnp.bfloat16)


def solution(mesh):
    return jax.shard_map(
        per_device,
        mesh=mesh,
        in_specs=(
            P(("gx", "gy")),
            P(("gx", "gy")),
            P(("gx", "gy")),
            P("gx", None, "gy"),
            P(),
            P("gx", None, "gy"),
            P(None, "gx", None, "gy"),
            P(),
        ),
        out_specs=P(None, ("gx", "gy")),
        check_vma=False,
    )
```

profile of v0, /device:TPU:1, one launch (start us, length us, event | category | flops | bytes accessed | tf_op | source)
XLA Modules:
  0.0 2328.2 jit_solution(9613533928649428960)
XLA Ops:
  9.1 5.0 collective-permute-start.5
  15.5 180.3 %all_gather.6 = f32[3,65536]{1,0:T(4,128)S(1)} all-gather(f32[3,512]{1,0:T(4,128)S(1)} %pad_maximum_fusion.13), channel_id=1, replica_groups=mesh['gx'=8,'gy'=16] {'gx','gy'}, dimensions={1}, use_global_device_ids=true | all-gather | bytes 792576 | tf_op jit(solution)/shard_map/all_gather | solution.py:99
  196.9 448.7 %scatter_custom_fusion = f32[131072]{0:T(1024)S(1)} fusion(s32[65536]{0:T(1024)S(1)} %bitcast.84, f32[65536]{0:T(1024)S(1)} %bitcast.85, f32[]{:T(128)} %constant.174.clone.1), kind=kCustom, calls=%fused_computation.67 | custom fusion | flops 65536 | bytes 524292 | tf_op jit(solution)/shard_map/scatter-add | solution.py:106
  660.5 389.4 %while.32 = (s32[]{:T(128)}, f32[4,4,64,128]{2,0,3,1:T(4,128)}, f32[4,4,64,128]{2,0,3,1:T(4,128)}, f32[4,4,64,128]{2,0,3,1:T(4,128)}, f32[4,64,128]{1,2,0:T(8,12...) while((s32[]{:T(128)}, f32[4,4,64,128]{2,0,3,1:T(4,128)}, ...), condition=%wide.region_3.4_spmd.clone.clone, body=%wide.region_2.3_spmd.sunk.clone.clone.sunk | while | flops 5645059 | bytes 22811596 | solution.py:125
  681.9 5.4 multiply_add_fusion.2
  710.4 5.4 multiply_add_fusion.2
  740.5 5.4 multiply_add_fusion.2
  760.9 4.5 collective-permute-start.2
  771.4 5.4 multiply_add_fusion.2
  791.3 5.0 collective-permute-start.2
  802.2 5.4 multiply_add_fusion.2
  810.6 5.3 collective-permute-start
  824.8 5.5 collective-permute-start.2
  836.3 5.4 multiply_add_fusion.2
  844.6 6.4 collective-permute-start
  860.3 4.9 collective-permute-start.2
  871.1 5.4 multiply_add_fusion.2
  879.5 6.3 collective-permute-start
  895.1 4.6 collective-permute-start.2
  905.6 5.4 multiply_add_fusion.2
  913.9 7.0 collective-permute-start
  940.1 5.4 multiply_add_fusion.2
  948.4 6.9 collective-permute-start
  964.4 4.2 collective-permute-start.2
  974.6 5.4 multiply_add_fusion.2
  982.9 6.9 collective-permute-start
  998.8 4.2 collective-permute-start.2
  1009.0 5.4 multiply_add_fusion.2
  1017.4 6.9 collective-permute-start
  1043.5 5.4 multiply_add_fusion.2
  1052.4 8.4 copy.40
  1060.8 194.2 %scatter_custom_fusion.1 = f32[4,98304]{0,1:T(8,128)} fusion(s32[32768]{0:T(1024)} %bitcast.93, f32[32768,4]{1,0:T(8,128)} %copy.40, f32[]{:T(128)} %constant.174.clone.1), kind=kCustom, calls=%fused_computation.47 | custom fusion | flops 131072 | bytes 1573376 | tf_op jit(solution)/shard_map/vmap()/scatter-add | solution.py:131
  1256.8 723.1 %reduce-scatter.5.cloned.1.call-done = f32[4,768]{0,1:T(8,128)} async-done(((f32[4,98304]{0,1:T(8,128)}), f32[4,768]{0,1:T(8,128)}) %reduce-scatter.5.cloned.1.call-update) | async-done | bytes 12304 | tf_op jit(solution)/shard_map/reduce_scatter | solution.py:136
  1980.9 33.5 %all_gather.7 = bf16[4,6144]{0,1:T(8,128)(2,1)S(1)} all-gather(bf16[4,768]{0,1:T(8,128)(2,1)S(1)} %convert_element_type.56), channel_id=1, replica_groups=mesh['gx'=8,'gy'=16] {'gx'}, dimensions={1}, use_global_device_ids=true | all-gather | bytes 55296 | tf_op jit(solution)/shard_map/all_gather | solution.py:137
  2015.2 219.2 %while.31 = (s32[]{:T(128)}, f32[12,4,1024]{2,1,0:T(4,128)S(1)}, f32[3,6144]{1,0:T(4,128)S(1)}, s32[12]{0:T(128)S(1)}, f32[3,12288]{1,0:T(4,128)S(1)}, /*index=5...) while((s32[]{:T(128)}, f32[12,4,1024]{2,1,0:T(4,128)S(1)}, ...), condition=%wide.region_7.8_spmd, body=%wide.region_6.7_spmd.sunk | while | flops 119537672 | bytes 323779 | solution.py:150
  2018.0 15.4 fusion.59
  2036.3 15.4 fusion.59
  2054.6 15.4 fusion.59
  2072.8 15.4 fusion.59
  2091.1 15.4 fusion.59
  2109.4 15.4 fusion.59
  2127.6 15.4 fusion.59
  2145.9 15.4 fusion.59
  2164.2 15.4 fusion.59
  2182.4 15.4 fusion.59
  2200.7 15.4 fusion.59
  2219.0 15.4 fusion.59
  2238.4 80.8 %reduce-scatter.7.cloned.1.call-done = f32[768,4]{1,0:T(8,128)} async-done(((f32[12288,4]{1,0:T(8,128)}), f32[768,4]{1,0:T(8,128)}) %reduce-scatter.7.cloned.1.call-update) | async-done | bytes 12304
  (533 shorter events, 285.0 us)
Async XLA Ops:
  6.5 1973.4 %reduce-scatter.5.cloned.1.call-start = ((), (), s32[]{:S(2)}) async-start(), calls=%async_computation.2 | async-start | bytes 50724864 | tf_op jit(solution)/shard_map/reduce_scatter | solution.py:136
  7.8 637.9 %collective-permute-start.4 = (f32[1,64,128]{2,1,0:T(8,128)S(1)}, f32[1,64,128]{2,1,0:T(8,128)S(1)}, u32[]{:S(2)}, u32[]{:S(2)}) collective-permute-start(f32[1,64,128]{2,1,0:T(8,128)S(1)} %get-tuple-element.423), channel_id=1, source_target_pairs={{16,0},{32,16},{48,32},{64,48},{80,64},{96,80},{112,96},{17,1},{33... | collective-permute-start | bytes 98312 | tf_op jit(solution)/shard_map/ppermute | solution.py:24
  9.1 636.6 %collective-permute-start.5 = (f32[1,64,128]{2,1,0:T(8,128)S(1)}, f32[1,64,128]{2,1,0:T(8,128)S(1)}, u32[]{:S(2)}, u32[]{:S(2)}) collective-permute-start(f32[1,64,128]{2,1,0:T(8,128)S(1)} %get-tuple-element.422), channel_id=1, source_target_pairs={{0,16},{16,32},{32,48},{48,64},{64,80},{80,96},{96,112},{1,17},{17... | collective-permute-start | bytes 98312 | tf_op jit(solution)/shard_map/ppermute | solution.py:23
  645.8 9.1 collective-permute-start.6
  647.7 7.2 collective-permute-start.7
  662.4 7.0 collective-permute-start
  663.7 10.1 collective-permute-start.1
  673.9 6.5 collective-permute-start.2
  690.3 7.4 collective-permute-start
  692.0 10.1 collective-permute-start.1
  702.2 6.5 collective-permute-start.2
  704.4 5.0 collective-permute-start.3
  718.7 8.2 collective-permute-start
  722.0 9.3 collective-permute-start.1
  731.3 7.3 collective-permute-start.2
  748.8 8.0 collective-permute-start
  751.9 8.9 collective-permute-start.1
  760.9 8.6 collective-permute-start.2
  765.4 5.0 collective-permute-start.3
  779.7 7.5 collective-permute-start
  782.3 8.9 collective-permute-start.1
  791.3 9.1 collective-permute-start.2
  796.3 5.0 collective-permute-start.3
  810.6 10.2 collective-permute-start
  815.8 8.9 collective-permute-start.1
  824.8 9.6 collective-permute-start.2
  844.6 11.4 collective-permute-start
  851.0 9.2 collective-permute-start.1
  860.3 9.0 collective-permute-start.2
  879.5 11.3 collective-permute-start
  885.8 9.2 collective-permute-start.1
  895.1 8.7 collective-permute-start.2
  899.6 5.0 collective-permute-start.3
  913.9 11.9 collective-permute-start
  920.9 8.9 collective-permute-start.1
  929.9 8.3 collective-permute-start.2
  934.1 5.0 collective-permute-start.3
  948.4 11.9 collective-permute-start
  955.4 8.9 collective-permute-start.1
  964.4 8.3 collective-permute-start.2
  968.6 5.0 collective-permute-start.3
  982.9 11.9 collective-permute-start
  989.8 8.9 collective-permute-start.1
  998.8 8.3 collective-permute-start.2
  1017.4 11.9 collective-permute-start
  1024.3 8.9 collective-permute-start.1
  1033.3 8.3 collective-permute-start.2
  1255.0 1064.2 %reduce-scatter.7.cloned.1.call-start = ((), (), s32[]{:S(2)}) async-start(), calls=%async_computation.3 | async-start | bytes 6684672
  (118 other events, 434.7 us)
Sparse Core Ops, SparseCore 0:
  1255.1 724.7 reduce-scatter.4
  2238.5 80.6 reduce-scatter.6
where the time goes:
time: 2340 us; the launch traced here: 2330 us
  waiting for transfers between devices  833 us (36%)
  other arithmetic  811 us (35%)
  blocking collectives  214 us (9%)
  matrix products  185 us (8%)
  starting transfers between devices  156 us (7%)
  local copies, waits for them, and re-layouts  87.9 us (4%)
  loops' own time  26.5 us (1%)
    reduce_scatter x1, waiting for transfers between devices, per_device(): lax.psum_scatter(partial_value, ('gx', 'gy'), scatter_dimension=1, tiled=...  723 us
    scatter-add x1, other arithmetic, per_device(): source = jnp.zeros((tests * cells_dev,), jnp.float32).at[codes].add(amoun...  449 us
    scatter-add x1, other arithmetic, per_device(): jax.ops.segment_sum(test_row, zone_flat, num_segments=ZONES)  194 us
    dot_general x12, matrix products, tile_product(): jnp.dot(zone_cols, covariance(col_pts, block_pts), preferred_element_type...  185 us
    all_gather x1, blocking collectives, per_device(): whole = lax.all_gather(packed, ('gx', 'gy'), axis=1, tiled=True)  180 us
    ppermute x26, starting transfers between devices, padded_2(): before = lax.ppermute(last, axis, up)  113 us
    unnamed x3, waiting for transfers between devices  80.8 us
    add x12, other arithmetic, sweep_each(): keep_table[counter] * direction_now + new_table[counter] * residual_now  65 us
  transfers between devices with their start and end apart: 54, of which 28 were waited for; matrix products, arithmetic and copies ran while one was open for 24% of the time, Pallas kernels for 0%

commit v1 on v0

v1 whole, which is shorter than its diff:
```python
import functools

import jax
import jax.numpy as jnp
from jax import lax
from jax.experimental import pallas as pl
from jax.experimental.pallas import tpu as pltpu
from jax.sharding import PartitionSpec as P

MESH = pl.DeviceIdType.MESH
NT = (((1,), (1,)), ((), ()))
VMEM = pl.BlockSpec(memory_space=pltpu.VMEM)
F32 = jnp.float32
BF16 = jnp.bfloat16
MIB = 2**20

SWEEPS = 12
TESTS = 4
CX, NZ, CY = 4, 64, 128
N_GX, N_GY = 8, 16
DEVICES = N_GX * N_GY
NCLASS = 16
CAP = 16
ZONES = 98304
SHARE = ZONES // DEVICES
GROUPS = 16
MEMBERS = DEVICES // GROUPS
GROUP = ZONES // GROUPS
PLANES = TESTS * CX

storage = 0.02
lam_low = 0.02
lam_high = 36.02
corr_len = 0.1
LOG2E = 1.4426950408889634


def cheb_setup():
    middle = 0.5 * (lam_high + lam_low)
    spread = 0.5 * (lam_high - lam_low)
    ratio_mid = middle / spread
    current = 1.0 / ratio_mid
    factors = []
    for counter in range(SWEEPS - 1):
        updated = 1.0 / (2.0 * ratio_mid - current)
        factors.append((updated * current, 2.0 * updated / spread))
        current = updated
    return (middle, factors)


def my_index():
    return lax.axis_index("gx") * N_GY + lax.axis_index("gy")


def coords(dev):
    return (dev // N_GY, dev % N_GY)


def greet(devs):
    barrier = pltpu.get_barrier_semaphore()
    for dev in devs:
        pl.semaphore_signal(barrier, inc=1, device_id=dev, device_id_type=MESH)
    pl.semaphore_wait(barrier, len(devs))


def greet_all(me):
    barrier = pltpu.get_barrier_semaphore()

    def each(k, _):
        dev = lax.rem(me + k, DEVICES)
        pl.semaphore_signal(barrier, inc=1, device_id=coords(dev), device_id_type=MESH)
        return 0

    lax.fori_loop(1, DEVICES, each, 0)
    pl.semaphore_wait(barrier, DEVICES - 1)


def send_to_all(me, send, recv, send_sem, recv_sem):
    def each(k, _):
        dev = lax.rem(me + k, DEVICES)
        pltpu.make_async_remote_copy(
            src_ref=send.at[dev],
            dst_ref=recv.at[me],
            send_sem=send_sem,
            recv_sem=recv_sem,
            device_id=coords(dev),
            device_id_type=MESH,
        ).start()
        return 0

    lax.fori_loop(1, DEVICES, each, 0)
    recv[me] = send[me]
    rest = pl.ds(0, DEVICES - 1)
    pltpu.make_async_copy(recv.at[rest], recv.at[rest], recv_sem).wait()
    pltpu.make_async_copy(send.at[rest], send.at[rest], send_sem).wait()


def wells_kernel(cell_ref, test_ref, value_ref, src_ref, rows, send, recv, send_sem, recv_sem):
    me = my_index()
    cell, test, value = cell_ref[...], test_ref[...], value_ref[...]
    n_rows = cell.shape[1]
    y = cell % (CY * N_GY)
    z = cell // (CY * N_GY) % NZ
    x = cell // (CY * N_GY * NZ)
    owner = x // CX * N_GY + y // CY
    z_row = z % 8 * 8 + z // 8
    high = (test * CX + x % CX) * 32 + z_row % 32
    code = (high * 256 + z_row // 32 * CY + y % CY).astype(F32)
    hot = jnp.where(
        lax.broadcasted_iota(jnp.int32, (DEVICES, n_rows), 0) == owner, 1.0, 0.0
    )
    earlier = jnp.where(
        lax.broadcasted_iota(jnp.int32, (n_rows, n_rows), 0)
        < lax.broadcasted_iota(jnp.int32, (n_rows, n_rows), 1),
        1.0,
        0.0,
    )
    hot16 = hot.astype(BF16)
    count = jnp.dot(hot16, earlier.astype(BF16), preferred_element_type=F32)
    rank = jnp.sum(hot * count, axis=0, keepdims=True).astype(jnp.int32)
    slot = lax.broadcasted_iota(jnp.int32, (128, n_rows), 0)
    part = jnp.where(slot == rank, code, jnp.where(slot == rank + CAP, value, 0.0))
    part = jnp.where(rank < CAP, part, 0.0)
    total = None
    for _ in range(3):
        piece = part.astype(BF16)
        part = part - piece.astype(F32)
        term = lax.dot_general(hot16, piece, NT, preferred_element_type=F32)
        total = term if total is None else total + term
    rows[...] = total
    for dev in range(DEVICES):
        send[dev] = rows[dev : dev + 1, :]

    greet_all(me)
    send_to_all(me, send, recv, send_sem, recv_sem)

    for dev in range(DEVICES):
        rows[dev : dev + 1, :] = recv[dev]
    lane = lax.broadcasted_iota(jnp.int32, (16, 128), 1)
    codes = jnp.zeros((16, 128), F32)
    values = jnp.zeros((16, 128), F32)
    for g in range(8):
        block = rows[16 * g : 16 * g + 16, :]
        here = lane // CAP == g
        codes = jnp.where(here, pltpu.roll(block, CAP * g, 1) if g else block, codes)
        values = jnp.where(here, pltpu.roll(block, (CAP * g - CAP) % 128, 1), values)
    codes = codes.astype(jnp.int32)
    highs, lows = codes // 256, codes % 256
    first = values.astype(BF16).astype(F32)
    second = values - first
    row_high = lax.broadcasted_iota(jnp.int32, (512, 128), 0)
    row_low = lax.broadcasted_iota(jnp.int32, (256, 128), 0)
    left, right_a, right_b = [], [], []
    for r in range(16):
        left.append(jnp.where(row_high == highs[r : r + 1], 1.0, 0.0).astype(BF16))
        same = row_low == lows[r : r + 1]
        right_a.append(jnp.where(same, first[r : r + 1], 0.0).astype(BF16))
        right_b.append(jnp.where(same, second[r : r + 1], 0.0).astype(BF16))
    left = jnp.concatenate(left, axis=1)
    acc = lax.dot_general(
        left, jnp.concatenate(right_a, axis=1), NT, preferred_element_type=F32
    ) + lax.dot_general(left, jnp.concatenate(right_b, axis=1), NT, preferred_element_type=F32)
    for p in range(PLANES):
        for half in range(2):
            src_ref[p, 32 * half : 32 * half + 32, :] = acc[
                32 * p : 32 * p + 32, 128 * half : 128 * half + 128
            ]


def wells_call(cell, test, value):
    return pl.pallas_call(
        wells_kernel,
        out_shape=jax.ShapeDtypeStruct((PLANES, NZ, CY), F32),
        in_specs=[VMEM] * 3,
        out_specs=VMEM,
        scratch_shapes=[
            pltpu.VMEM((DEVICES, 128), F32),
            pltpu.VMEM((DEVICES, 1, 128), F32),
            pltpu.VMEM((DEVICES, 1, 128), F32),
            pltpu.SemaphoreType.DMA,
            pltpu.SemaphoreType.DMA,
        ],
        compiler_params=pltpu.CompilerParams(
            collective_id=0, has_side_effects=True, vmem_limit_bytes=48 * MIB
        ),
    )(cell, test, value)


def roll_to(value, shift):
    shift = shift % 128
    return pltpu.roll(value, shift, 1) if shift else value


def sweeps_kernel(
    class_ref,
    class_value_ref,
    src_ref,
    draw_ref,
    out_ref,
    cond_nat,
    cond,
    coef,
    dirs,
    resid,
    sol,
    cx_recv,
    cy_send,
    cy_recv,
    dx_send,
    dx_recv,
    dy_send,
    dy_recv,
    cond_send_sem,
    cond_recv_sem,
    send_sem,
    recv_sem,
):
    gx, gy = lax.axis_index("gx"), lax.axis_index("gy")
    x_down, x_up = (lax.rem(gx + N_GX - 1, N_GX), gy), (lax.rem(gx + 1, N_GX), gy)
    y_down, y_up = (gx, lax.rem(gy + N_GY - 1, N_GY)), (gx, lax.rem(gy + 1, N_GY))
    lane = lax.broadcasted_iota(jnp.int32, (8, 128), 1)
    sub = lax.broadcasted_iota(jnp.int32, (8, 128), 0)
    first_lane, last_lane = lane == 0, lane == 127

    def tile(j):
        return slice(8 * j, 8 * j + 8)

    for x in range(CX):
        cls = class_ref[x]
        acc = jnp.zeros((NZ, CY), F32)
        for k in range(NCLASS):
            acc = jnp.where(cls == k, class_value_ref[k], acc)
        cond_nat[x] = acc
    for x in range(CX):
        for j in range(8):
            cond[x, tile(j), :] = cond_nat[x, pl.ds(j, 8, stride=8), :]

    def packed(get):
        parts = [jnp.zeros((8, 128), F32)] * 2
        for x in range(CX):
            for j in range(8):
                q = 2 * x + 32 * (j % 4)
                here = (lane == q) | (lane == q + 1)
                parts[j // 4] = jnp.where(here, roll_to(get(x, j), q + 1), parts[j // 4])
        return parts

    def met(low, high):
        return jnp.where(lane % 2 == 1, high, roll_to(low, 2))

    greet([x_down, x_up, y_down, y_up])

    def exchange(x_src, x_dst, y_src, y_dst, s_sem, r_sem):
        out = []
        for n, (src, dst, dev) in enumerate(
            (
                (x_src(0), x_dst(1), x_down),
                (x_src(1), x_dst(0), x_up),
                (y_src, y_dst(1), y_down),
                (y_src, y_dst(0), y_up),
            )
        ):
            out.append(
                pltpu.make_async_remote_copy(
                    src_ref=src,
                    dst_ref=dst,
                    send_sem=s_sem(n),
                    recv_sem=r_sem(n),
                    device_id=dev,
                    device_id_type=MESH,
                )
            )
        return out

    pack = packed(lambda x, j: cond[x, tile(j), :])
    for half in range(2):
        cy_send[half] = pack[half]
    cond_copies = exchange(
        lambda side: cond.at[side * (CX - 1)],
        lambda side: cx_recv.at[side],
        cy_send,
        lambda side: cy_recv.at[side],
        lambda n: cond_send_sem.at[n],
        lambda n: cond_recv_sem.at[n],
    )
    for copy in cond_copies:
        copy.start()

    def copies(par):
        return exchange(
            lambda side: dx_send.at[par, side],
            lambda side: dx_recv.at[par, side],
            dy_send.at[par],
            lambda side: dy_recv.at[par, side],
            lambda n: send_sem.at[par, n],
            lambda n: recv_sem.at[par, n],
        )

    middle, factors = cheb_setup()

    def stage(par, t, get):
        for side, x in ((0, 0), (1, CX - 1)):
            for j in range(0, 8, 2):
                both = jnp.concatenate([get(x, j), get(x, j + 1)], axis=0)
                dx_send[par, side, t, 8 * j : 8 * j + 16, :] = both.astype(BF16)
        parts = packed(get)
        for half in range(2):
            old = dy_send[par, half]
            dy_send[par, half] = jnp.where(
                lane % 32 // 8 == t, pltpu.roll(parts[half], 8 * t, 1), old
            )

    for par in range(2):
        for half in range(2):
            dy_send[par, half] = jnp.zeros((8, 128), F32)

    def begin(t, _):
        for x in range(CX):
            p = CX * t + x
            value = src_ref[p]
            resid[p] = value
            dirs[0, p] = value / middle
            sol[p] = jnp.zeros((NZ, CY), F32)
        stage(0, t, lambda x, j: dirs[0, CX * t + x, tile(j), :])
        return 0

    lax.fori_loop(0, TESTS, begin, 0)
    for copy in copies(0):
        copy.start()
    for copy in cond_copies:
        copy.wait()

    beside = [met(cy_recv[0, half], cy_recv[1, half]) for half in range(2)]
    for x in range(CX):
        for j in range(8):
            c = cond[x, tile(j), :]
            q = 2 * x + 32 * (j % 4)
            halo = roll_to(beside[j // 4], -(q + 2))
            zero = jnp.zeros((8, 128), F32)
            off_y_up = last_lane & (gy == N_GY - 1)
            off_y_down = first_lane & (gy == 0)
            sides = []
            if x < CX - 1:
                sides.append((cond[x + 1, tile(j), :], None))
            else:
                sides.append((cx_recv[1, tile(j), :], (lane >= 0) & (gx == N_GX - 1)))
            if x > 0:
                sides.append((cond[x - 1, tile(j), :], None))
            else:
                sides.append((cx_recv[0, tile(j), :], (lane >= 0) & (gx == 0)))
            if j < 7:
                sides.append((cond[x, tile(j + 1), :], None))
            else:
                sides.append((pltpu.roll(cond[x, tile(0), :], 7, 0), sub == 7))
            if j > 0:
                sides.append((cond[x, tile(j - 1), :], None))
            else:
                sides.append((pltpu.roll(cond[x, tile(7), :], 1, 0), sub == 0))
            sides.append((jnp.where(last_lane, halo, roll_to(c, 127)), off_y_up))
            sides.append((jnp.where(first_lane, halo, roll_to(c, 1)), off_y_down))
            diag = storage
            for n, (near, off) in enumerate(sides):
                if off is not None:
                    near = jnp.where(off, zero, near)
                face = 0.5 * (c + near)
                diag = diag + face
                coef[n, x, tile(j), :] = face if off is None else jnp.where(off, zero, face)
            coef[6, x, tile(j), :] = diag

    keeps = [pair[0] for pair in factors]
    news = [pair[1] for pair in factors]

    def sweep(k, _):
        par = lax.rem(k, 2)
        nxt = 1 - par
        keep, new = jnp.float32(keeps[0]), jnp.float32(news[0])
        for n in range(1, SWEEPS - 1):
            keep = jnp.where(k == n, jnp.float32(keeps[n]), keep)
            new = jnp.where(k == n, jnp.float32(news[n]), new)
        for copy in copies(par):
            copy.wait()
        near_y = [met(dy_recv[par, 0, half], dy_recv[par, 1, half]) for half in range(2)]

        def one_test(t, _):
            halos = [pltpu.roll(near_y[half], lax.rem(128 - 8 * t, 128), 1) for half in range(2)]
            made = {}
            low = [dx_recv[par, 0, t, 8 * j : 8 * j + 16, :].astype(F32) for j in range(0, 8, 2)]
            high = [dx_recv[par, 1, t, 8 * j : 8 * j + 16, :].astype(F32) for j in range(0, 8, 2)]
            for x in range(CX):
                p = CX * t + x
                v = [dirs[par, p, tile(j), :] for j in range(8)]
                for j in range(8):
                    q = 2 * x + 32 * (j % 4)
                    halo = roll_to(halos[j // 4], -(q + 2))
                    half = slice(8 * (j % 2), 8 * (j % 2) + 8)
                    near = [
                        dirs[par, p + 1, tile(j), :] if x < CX - 1 else high[j // 2][half],
                        dirs[par, p - 1, tile(j), :] if x > 0 else low[j // 2][half],
                        v[j + 1] if j < 7 else pltpu.roll(v[0], 7, 0),
                        v[j - 1] if j > 0 else pltpu.roll(v[7], 1, 0),
                        jnp.where(last_lane, halo, roll_to(v[j], 127)),
                        jnp.where(first_lane, halo, roll_to(v[j], 1)),
                    ]
                    applied = coef[6, x, tile(j), :] * v[j]
                    for n in range(6):
                        applied = applied - coef[n, x, tile(j), :] * near[n]
                    left = resid[p, tile(j), :] - applied
                    resid[p, tile(j), :] = left
                    sol[p, tile(j), :] += v[j]
                    fresh = keep * v[j] + new * left
                    dirs[nxt, p, tile(j), :] = fresh
                    made[x, j] = fresh
            stage(nxt, t, lambda x, j: made[x, j])
            return 0

        lax.fori_loop(0, TESTS, one_test, 0)

        @pl.when(k < SWEEPS - 2)
        def _():
            for copy in copies(nxt):
                copy.start()

        return 0

    lax.fori_loop(0, SWEEPS - 1, sweep, 0)
    last = (SWEEPS - 1) % 2

    def finish(p, _):
        for j in range(8):
            resid[p, pl.ds(j, 8, stride=8), :] = sol[p, tile(j), :] + dirs[last, p, tile(j), :]
        x = lax.rem(p, CX)
        out_ref[p] = cond_nat[x] * draw_ref[p].astype(F32) * resid[p]
        return 0

    lax.fori_loop(0, PLANES, finish, 0)


def sweeps_call(classes, class_value, source, drawdown):
    block = (PLANES, NZ, CY)
    return pl.pallas_call(
        sweeps_kernel,
        out_shape=jax.ShapeDtypeStruct(block, F32),
        in_specs=[VMEM, pl.BlockSpec(memory_space=pltpu.SMEM), VMEM, VMEM],
        out_specs=VMEM,
        scratch_shapes=[
            pltpu.VMEM((CX, NZ, CY), F32),
            pltpu.VMEM((CX, NZ, CY), F32),
            pltpu.VMEM((7, CX, NZ, CY), F32),
            pltpu.VMEM((2,) + block, F32),
            pltpu.VMEM(block, F32),
            pltpu.VMEM(block, F32),
            pltpu.VMEM((2, NZ, CY), F32),
            pltpu.VMEM((2, 8, 128), F32),
            pltpu.VMEM((2, 2, 8, 128), F32),
            pltpu.VMEM((2, 2, TESTS, NZ, CY), BF16),
            pltpu.VMEM((2, 2, TESTS, NZ, CY), BF16),
            pltpu.VMEM((2, 2, 8, 128), F32),
            pltpu.VMEM((2, 2, 2, 8, 128), F32),
            pltpu.SemaphoreType.DMA((4,)),
            pltpu.SemaphoreType.DMA((4,)),
            pltpu.SemaphoreType.DMA((2, 4)),
            pltpu.SemaphoreType.DMA((2, 4)),
        ],
        compiler_params=pltpu.CompilerParams(
            collective_id=1, has_side_effects=True, vmem_limit_bytes=48 * MIB
        ),
    )(classes, class_value, source, drawdown)


def groups_of(gx, gy):
    tail = gx == N_GX - 1
    low = jnp.where(tail, gy % 8, gy)
    high = jnp.where(tail, gy % 8 + 8, (gy + gx + 1) % GROUPS)
    return low, high, tail & (gy >= 8)


def takers_of(group):
    out = []
    for k in range(N_GX - 1):
        out.append(((k, group), 0))
        out.append(((k, (group + GROUPS - k - 1) % GROUPS), 1))
    place = group // 8
    out.append(((N_GX - 1, group % 8), place))
    out.append(((N_GX - 1, group % 8 + 8), place))
    return out


ROWS_STEP = 8


def zones_kernel(
    zone_ref, sens_ref, out_ref, owner_of, left, right, acc, send, recv, mine, sem, got_sem, put_sem
):
    me = my_index()
    gx, gy = lax.axis_index("gx"), lax.axis_index("gy")
    owner_of[...] = (
        (lax.broadcasted_iota(jnp.int32, (TESTS * DEVICES, 128), 0) // TESTS)
        .astype(F32)
        .astype(BF16)
    )
    acc[...] = jnp.zeros_like(acc)
    inner = lax.broadcasted_iota(jnp.int32, (256, 128), 0).astype(F32).astype(BF16)
    sub = lax.broadcasted_iota(jnp.int32, (8, 128), 0) % TESTS

    def spread(row, times):
        return jnp.concatenate([jnp.broadcast_to(row, (16, 128)).astype(BF16)] * times, axis=0)

    def step(i, _):
        at = pl.ds(pl.multiple_of(i * ROWS_STEP, ROWS_STEP), ROWS_STEP)
        zone = zone_ref[at, :].astype(F32)
        owner = ((zone + 0.5) * (1.0 / SHARE)).astype(jnp.int32).astype(F32)
        place = zone - owner * SHARE
        values = [sens_ref[t, at, :] for t in range(TESTS)]
        for r in range(ROWS_STEP):
            row = slice(r, r + 1)
            four = jnp.broadcast_to(values[0][row], (8, 128))
            for t in range(1, TESTS):
                four = jnp.where(sub == t, jnp.broadcast_to(values[t][row], (8, 128)), four)
            four = jnp.concatenate([four, four], axis=0).astype(BF16)
            cols = slice(128 * r, 128 * r + 128)
            left[:, cols] = jnp.where(
                owner_of[...] == spread(owner[row], TESTS * DEVICES // 16),
                jnp.concatenate([four] * (TESTS * DEVICES // 16), axis=0),
                jnp.zeros((), BF16),
            )
            for part in range(SHARE // 256):
                right[256 * part : 256 * part + 256, cols] = jnp.where(
                    inner == spread(place[row] - 256.0 * part, 16),
                    jnp.ones((), BF16),
                    jnp.zeros((), BF16),
                )
        acc[...] += lax.dot_general(left[...], right[...], NT, preferred_element_type=F32)
        return 0

    lax.fori_loop(0, CX * NZ // ROWS_STEP, step, 0)
    for dev in range(DEVICES):
        send[dev] = acc[TESTS * dev : TESTS * dev + TESTS, :]

    greet_all(me)
    send_to_all(me, send, recv, sem.at[0], sem.at[1])

    def add(s, total):
        for n in range(8):
            total = total + recv[8 * s + n]
        return total

    total = lax.fori_loop(0, DEVICES // 8, add, jnp.zeros((TESTS, SHARE), F32))
    mine[...] = total.astype(BF16).astype(F32)

    group, member = me // MEMBERS, me % MEMBERS

    def put(n, dev, place):
        return pltpu.make_async_remote_copy(
            src_ref=mine,
            dst_ref=out_ref.at[place, member],
            send_sem=put_sem.at[n],
            recv_sem=got_sem.at[place, member],
            device_id=dev,
            device_id_type=MESH,
        )

    takers = takers_of(group)
    for n, (dev, place) in enumerate(takers):
        self_here = dev[0] * N_GY + dev[1] == me

        @pl.when(jnp.logical_not(self_here))
        def _():
            put(n, dev, place).start()

        @pl.when(self_here)
        def _():
            out_ref[place, member] = mine[...]

    low, high, _ = groups_of(gx, gy)
    for place, held in ((0, low), (1, high)):
        for m in range(MEMBERS):

            @pl.when(held * MEMBERS + m != me)
            def _():
                pltpu.make_async_copy(
                    out_ref.at[place, m], out_ref.at[place, m], got_sem.at[place, m]
                ).wait()

    for n, (dev, place) in enumerate(takers):

        @pl.when(dev[0] * N_GY + dev[1] != me)
        def _():
            put(n, dev, place).wait_send()


def zones_call(zone, sens):
    rows = TESTS * DEVICES
    width = ROWS_STEP * 128
    return pl.pallas_call(
        zones_kernel,
        out_shape=jax.ShapeDtypeStruct((2, MEMBERS, TESTS, SHARE), F32),
        in_specs=[VMEM] * 2,
        out_specs=VMEM,
        scratch_shapes=[
            pltpu.VMEM((rows, 128), BF16),
            pltpu.VMEM((rows, width), BF16),
            pltpu.VMEM((SHARE, width), BF16),
            pltpu.VMEM((rows, SHARE), F32),
            pltpu.VMEM((DEVICES, TESTS, SHARE), F32),
            pltpu.VMEM((DEVICES, TESTS, SHARE), F32),
            pltpu.VMEM((TESTS, SHARE), F32),
            pltpu.SemaphoreType.DMA((2,)),
            pltpu.SemaphoreType.DMA((2, MEMBERS)),
            pltpu.SemaphoreType.DMA((16,)),
        ],
        compiler_params=pltpu.CompilerParams(
            collective_id=2, has_side_effects=True, vmem_limit_bytes=48 * MIB
        ),
    )(zone, sens)


BLOCK = 1024
STRIP = 64


def cov_kernel(diag_ref, pts_ref, sums_ref, out_ref, z_ref, rows_ref, tile_ref):
    blocks = GROUP // BLOCK
    diag = diag_ref[0]
    out_ref[...] = jnp.zeros_like(out_ref)
    for g in range(2):
        for m in range(MEMBERS):
            both = jnp.concatenate([sums_ref[g, m], jnp.zeros((TESTS, SHARE), F32)], axis=0)
            z_ref[g, :, SHARE * m : SHARE * m + SHARE] = both.astype(BF16)

    def tile(cg, c):
        cols = [pts_ref[cg, k : k + 1, pl.ds(pl.multiple_of(c * BLOCK, BLOCK), BLOCK)] for k in range(3)]

        def body(i, _):
            r0 = pl.multiple_of(i * STRIP, STRIP)
            squared = None
            for k in range(3):
                near = jnp.concatenate([rows_ref[k, pl.ds(r0, STRIP), :]] * (BLOCK // 128), axis=1)
                gap = near - cols[k]
                squared = gap * gap if squared is None else squared + gap * gap
            squared = jnp.maximum(squared, 1e-30)
            dist = squared * lax.rsqrt(squared)
            tile_ref[pl.ds(r0, STRIP), :] = jnp.exp2(-dist).astype(BF16)
            return 0

        lax.fori_loop(0, BLOCK // STRIP, body, 0, unroll=True)

    def phase(rg, _):
        cg = jnp.where(diag == 1, rg, 1)

        def row_block(r, _):
            rs = pl.ds(pl.multiple_of(r * BLOCK, BLOCK), BLOCK)
            for k in range(3):
                rows_ref[k] = jnp.broadcast_to(pts_ref[rg, k : k + 1, rs], (128, BLOCK)).T
            near = z_ref[rg, :, rs]

            def col_block(c, acc):
                tile(cg, c)
                cs = pl.ds(pl.multiple_of(c * BLOCK, BLOCK), BLOCK)
                acc = acc + lax.dot_general(
                    z_ref[cg, :, cs], tile_ref[...], NT, preferred_element_type=F32
                )

                @pl.when(jnp.logical_not((diag == 1) & (c == r)))
                def _():
                    out_ref[cg, :, cs] += jnp.dot(near, tile_ref[...], preferred_element_type=F32)

                return acc

            first = jnp.where(diag == 1, r, 0)
            acc = lax.fori_loop(first, blocks, col_block, jnp.zeros((8, BLOCK), F32))
            out_ref[rg, :, rs] += acc
            return 0

        lax.fori_loop(0, blocks, row_block, 0)
        return 0

    lax.fori_loop(0, 1 + diag, phase, 0)


def cov_call(diag, pts, sums):
    return pl.pallas_call(
        cov_kernel,
        out_shape=jax.ShapeDtypeStruct((2, 8, GROUP), F32),
        in_specs=[pl.BlockSpec(memory_space=pltpu.SMEM), VMEM, VMEM],
        out_specs=VMEM,
        scratch_shapes=[
            pltpu.VMEM((2, 8, GROUP), BF16),
            pltpu.VMEM((3, BLOCK, 128), F32),
            pltpu.VMEM((BLOCK, BLOCK), BF16),
        ],
        compiler_params=pltpu.CompilerParams(vmem_limit_bytes=48 * MIB),
    )(diag, pts, sums)


def reduce_kernel(part_ref, out_ref, send, recv, send_sem, recv_sem):
    me = my_index()
    gx, gy = lax.axis_index("gx"), lax.axis_index("gy")
    low, high, diag = groups_of(gx, gy)
    group, member = me // MEMBERS, me % MEMBERS
    for g in range(2):
        for m in range(MEMBERS):
            send[g, m] = part_ref[g, 0:TESTS, SHARE * m : SHARE * m + SHARE]

    takers = takers_of(group)
    barrier = pltpu.get_barrier_semaphore()
    for place, held in ((0, low), (1, high)):
        for m in range(MEMBERS):
            owner = held * MEMBERS + m

            @pl.when(owner != me)
            def _():
                pl.semaphore_signal(barrier, inc=1, device_id=coords(owner), device_id_type=MESH)

    for dev, _ in takers:

        @pl.when(dev[0] * N_GY + dev[1] != me)
        def _():
            pl.semaphore_signal(barrier, inc=1, device_id=dev, device_id_type=MESH)

    self_here = (low == group) | (high == group)
    pl.semaphore_wait(barrier, 32 - 2 * self_here.astype(jnp.int32))

    def put(place, m, held, slot):
        return pltpu.make_async_remote_copy(
            src_ref=send.at[place, m],
            dst_ref=recv.at[slot],
            send_sem=send_sem.at[place, m],
            recv_sem=recv_sem.at[slot],
            device_id=coords(held * MEMBERS + m),
            device_id_type=MESH,
        )

    sides = (
        (0, low, jnp.where(diag, low, high)),
        (1, high, jnp.where(diag, high, low)),
    )
    for place, held, slot in sides:
        for m in range(MEMBERS):

            @pl.when(held * MEMBERS + m != me)
            def _():
                put(place, m, held, slot).start()

            @pl.when(held * MEMBERS + m == me)
            def _():
                recv[slot] = send[place, m]

    own_slot = jnp.where(
        low == group, jnp.where(diag, low, high), jnp.where(diag, high, low)
    )
    for slot in range(GROUPS):

        @pl.when(jnp.logical_not(self_here & (own_slot == slot)))
        def _():
            pltpu.make_async_copy(recv.at[slot], recv.at[slot], recv_sem.at[slot]).wait()

    total = recv[0]
    for slot in range(1, GROUPS):
        total = total + recv[slot]
    out_ref[...] = total.astype(BF16)
    for place, held, slot in sides:
        for m in range(MEMBERS):

            @pl.when(held * MEMBERS + m != me)
            def _():
                put(place, m, held, slot).wait_send()


def reduce_call(parts):
    return pl.pallas_call(
        reduce_kernel,
        out_shape=jax.ShapeDtypeStruct((TESTS, SHARE), BF16),
        in_specs=[VMEM],
        out_specs=VMEM,
        scratch_shapes=[
            pltpu.VMEM((2, MEMBERS, TESTS, SHARE), F32),
            pltpu.VMEM((GROUPS, TESTS, SHARE), F32),
            pltpu.SemaphoreType.DMA((2, MEMBERS)),
            pltpu.SemaphoreType.DMA((GROUPS,)),
        ],
        compiler_params=pltpu.CompilerParams(
            collective_id=3, has_side_effects=True, vmem_limit_bytes=32 * MIB
        ),
    )(parts)


def per_device(
    well_cell, well_test, well_value, cond_class, class_value, zone_id, drawdown, centroid
):
    gx, gy = lax.axis_index("gx"), lax.axis_index("gy")
    low, high, diag = groups_of(gx, gy)
    pts = jnp.stack(
        [lax.dynamic_slice_in_dim(centroid, held * GROUP, GROUP, 1) for held in (low, high)]
    ) * (LOG2E / corr_len)
    source = wells_call(well_cell[None], well_test[None], well_value[None])
    sens = sweeps_call(cond_class, class_value, source, drawdown.reshape(PLANES, NZ, CY))
    sums = zones_call(zone_id.reshape(CX * NZ, CY), sens.reshape(TESTS, CX * NZ, CY))
    parts = cov_call(diag.astype(jnp.int32)[None], pts, sums)
    return reduce_call(parts)


def solution(mesh):
    return jax.shard_map(
        per_device,
        mesh=mesh,
        in_specs=(
            P(("gx", "gy")),
            P(("gx", "gy")),
            P(("gx", "gy")),
            P("gx", None, "gy"),
            P(),
            P("gx", None, "gy"),
            P(None, "gx", None, "gy"),
            P(),
        ),
        out_specs=P(None, ("gx", "gy")),
        check_vma=False,
    )
```

time: 2340 us -> 318 us (0.14)
  waiting for transfers between devices: 833 us -> 0 us
  other arithmetic: 811 us -> 0.07 us
  Pallas kernels: 0 us -> 313 us
  blocking collectives: 214 us -> 0 us
  matrix products: 185 us -> 0 us
  starting transfers between devices: 156 us -> 0 us
  local copies, waits for them, and re-layouts: 87.9 us -> 5.22 us
  loops' own time: 26.5 us -> 0 us
    reduce_scatter x1 -> x0, waiting for transfers between devices: 723 us -> none  [per_device(): lax.psum_scatter(partial_value, ('gx', 'gy'), scatter_dimension=1, tiled=...]
    scatter-add x2 -> x0, other arithmetic: 643 us -> none  [the longest x1 449 us: per_device(): source = jnp.zeros((tests * cells_dev,), jnp.float32).at[codes].add(amoun...]
    pallas_call x0 -> x5, Pallas kernels: none -> 313 us  [the longest x1 97.9 us: sweeps_call(): pl.pallas_call(sweeps_kernel, out_shape=jax.ShapeDtypeStruct(block, F32),...]
    all_gather x2 -> x0, blocking collectives: 214 us -> none  [the longest x1 180 us: per_device(): whole = lax.all_gather(packed, ('gx', 'gy'), axis=1, tiled=True)]
    dot_general x12 -> x0, matrix products: 185 us -> none  [tile_product(): jnp.dot(zone_cols, covariance(col_pts, block_pts), preferred_element_type...]
    ppermute x52 -> x0, starting transfers between devices: 156 us -> none  [the longest x26 113 us: padded_2(): before = lax.ppermute(last, axis, up)]
    unnamed x3 -> x0, waiting for transfers between devices: 80.8 us -> none
    add x13 -> x0, other arithmetic: 65.2 us -> none  [the longest x12 65 us: sweep_each(): keep_table[counter] * direction_now + new_table[counter] * residual_now]
  transfers between devices with their start and end apart: 54 -> 0, of which waited for: 28 -> 0; matrix products, arithmetic and copies ran while one was open for 24% -> 0% of each run, Pallas kernels for 0% -> 0%
where the time goes in v1:
time: 318 us
  Pallas kernels  313 us (98%)
  local copies, waits for them, and re-layouts  5.22 us (2%)
    pallas_call x1, Pallas kernels, sweeps_call(): pl.pallas_call(sweeps_kernel, out_shape=jax.ShapeDtypeStruct(block, F32),...  97.9 us
    pallas_call x1, Pallas kernels, cov_call(): pl.pallas_call(cov_kernel, out_shape=jax.ShapeDtypeStruct((2, 8, GROUP),...  91.6 us
    pallas_call x1, Pallas kernels, zones_call(): pl.pallas_call(zones_kernel, out_shape=jax.ShapeDtypeStruct((2, MEMBERS,...  76 us
    pallas_call x1, Pallas kernels, reduce_call(): pl.pallas_call(reduce_kernel, out_shape=jax.ShapeDtypeStruct((TESTS, SHAR...  28 us
    pallas_call x1, Pallas kernels, wells_call(): pl.pallas_call(wells_kernel, out_shape=jax.ShapeDtypeStruct((PLANES, NZ,...  19.1 us

profile of v1, /device:TPU:1, one launch (start us, length us, event | category | flops | bytes accessed | tf_op | source)
XLA Modules:
  0.0 317.9 jit_solution(1866880580837959894)
XLA Ops:
  0.0 0.0 copy-start
  0.0 0.0 copy-start.1
  0.0 1.0 dynamic-slice_bitcast_fusion.1
  1.0 0.1 maximum_multiply_fusion.pts_ref
  1.1 0.0 copy-start.3
  1.1 0.7 copy-done.3
  1.8 0.0 copy-start.4
  1.8 0.7 copy-done.4
  2.5 0.0 copy-start.5
  2.5 0.7 copy-done.5
  3.2 19.1 %shard_map.82.src_ref = f32[16,64,128]{2,1,0:T(8,128)S(1)} custom-call(s32[1,512]{1,0:T(1,128)S(1)} %bitcast.14, s32[1,512]{1,0:T(1,128)S(1)} %bitcast.15, f32[1,512]{1,0:T(1,128)S(1)} %bitcast.16), custom_call_target="tpu_custom_call" | custom-call | tf_op jit(solution)/shard_map/pallas_call | solution.py:171
  22.3 0.0 copy-done
  22.3 0.0 copy-start.2
  22.3 0.9 copy-done.2
  23.2 0.0 copy-start.6
  23.2 0.7 copy-done.6
  23.9 97.9 %shard_map.83 = f32[16,64,128]{2,1,0:T(8,128)S(1)} custom-call(s32[4,64,128]{2,1,0:T(8,128)S(1)} %copy-done.2, f32[16]{0:T(128)S(1)} %copy-done.6, f32[16,64,128]{2,1,0:T(8,128)S(1)} %shard_map.82.src_ref, bf16[16,64,128]{2,1,0:T(8,128)(2,1)S(1)} %bitcast.12), custom_call_target="tpu_custom_call" | custom-call | tf_op jit(solution)/shard_map/pallas_call | solution.py:439
  121.8 0.0 copy-done.1
  121.8 76.0 %shard_map.84.sums_ref = f32[2,8,4,768]{3,2,1,0:T(4,128)S(1)} custom-call(s32[256,128]{1,0:T(8,128)S(1)} %bitcast.13, f32[4,256,128]{2,1,0:T(8,128)S(1)} %bitcast.11), custom_call_target="tpu_custom_call" | custom-call | tf_op jit(solution)/shard_map/pallas_call | solution.py:593
  197.7 91.6 %shard_map.85.part_ref = f32[2,8,6144]{2,1,0:T(8,128)S(1)} custom-call(s32[1]{0:T(128)} %bitcast.diag_ref, f32[2,3,6144]{2,1,0:T(4,128)S(1)} %maximum_multiply_fusion.pts_ref, f32[2,8,4,768]{3,2,1,0:T(4,128)S(1)} %shard_map.84.sums_ref), custom_call_target="tpu_custom_call" | custom-call | tf_op jit(solution)/shard_map/pallas_call | solution.py:680
  289.3 28.0 %shard_map.86 = bf16[4,768]{1,0:T(4,128)(2,1)S(1)} custom-call(f32[2,8,6144]{2,1,0:T(8,128)S(1)} %shard_map.85.part_ref), custom_call_target="tpu_custom_call" | custom-call | tf_op jit(solution)/shard_map/pallas_call | solution.py:769
  317.3 0.6 copy.10
Async XLA Ops:
  0.0 22.3 %copy-start = (bf16[4,4,64,128]{3,2,1,0:T(8,128)(2,1)S(1)}, bf16[4,4,64,128]{3,2,1,0:T(8,128)(2,1)}, u32[]{:S(2)}) copy-start(bf16[4,4,64,128]{3,2,1,0:T(8,128)(2,1)} %param.14) | copy-start | bytes 786436
  0.0 121.8 %copy-start.1 = (s32[4,64,128]{2,1,0:T(8,128)S(1)}, s32[4,64,128]{2,1,0:T(8,128)}, u32[]{:S(2)}) copy-start(s32[4,64,128]{2,1,0:T(8,128)} %param.13) | copy-start | bytes 393220
  1.1 0.7 copy-start.3
  1.8 0.7 copy-start.4
  2.5 0.7 copy-start.5
  22.3 0.9 copy-start.2
  23.2 0.7 copy-start.6

commit v2 on v1

v2 whole, which is shorter than its diff:
```python
import functools

import jax
import jax.numpy as jnp
from jax import lax
from jax.experimental import pallas as pl
from jax.experimental.pallas import tpu as pltpu
from jax.sharding import PartitionSpec as P

MESH = pl.DeviceIdType.MESH
NT = (((1,), (1,)), ((), ()))
VMEM = pl.BlockSpec(memory_space=pltpu.VMEM)
F32 = jnp.float32
BF16 = jnp.bfloat16
MIB = 2**20

SWEEPS = 12
TESTS = 4
CX, NZ, CY = 4, 64, 128
N_GX, N_GY = 8, 16
DEVICES = N_GX * N_GY
NCLASS = 16
CAP = 16
ZONES = 98304
SHARE = ZONES // DEVICES
GROUPS = 16
MEMBERS = DEVICES // GROUPS
GROUP = ZONES // GROUPS
HALF = CY // 2
RIM = 16
XL, YL = 8, 3
HIGHS = 4 * YL * NZ
SLOTS = 16 * CAP

storage = 0.02
lam_low = 0.02
lam_high = 36.02
corr_len = 0.1
LOG2E = 1.4426950408889634


def cheb_setup():
    middle = 0.5 * (lam_high + lam_low)
    spread = 0.5 * (lam_high - lam_low)
    ratio_mid = middle / spread
    current = 1.0 / ratio_mid
    factors = []
    for counter in range(SWEEPS - 1):
        updated = 1.0 / (2.0 * ratio_mid - current)
        factors.append((updated * current, 2.0 * updated / spread))
        current = updated
    return (middle, factors)


def my_index():
    return lax.axis_index("gx") * N_GY + lax.axis_index("gy")


def coords(dev):
    return (dev // N_GY, dev % N_GY)


def greet(devs):
    barrier = pltpu.get_barrier_semaphore()
    for dev in devs:
        pl.semaphore_signal(barrier, inc=1, device_id=dev, device_id_type=MESH)
    pl.semaphore_wait(barrier, len(devs))


def greet_all(me):
    barrier = pltpu.get_barrier_semaphore()

    def each(k, _):
        dev = lax.rem(me + k, DEVICES)
        pl.semaphore_signal(barrier, inc=1, device_id=coords(dev), device_id_type=MESH)
        return 0

    lax.fori_loop(1, DEVICES, each, 0)
    pl.semaphore_wait(barrier, DEVICES - 1)


def send_to_all(me, send, recv, send_sem, recv_sem):
    def each(k, _):
        dev = lax.rem(me + k, DEVICES)
        pltpu.make_async_remote_copy(
            src_ref=send.at[dev],
            dst_ref=recv.at[me],
            send_sem=send_sem,
            recv_sem=recv_sem,
            device_id=coords(dev),
            device_id_type=MESH,
        ).start()
        return 0

    lax.fori_loop(1, DEVICES, each, 0)
    recv[me] = send[me]
    rest = pl.ds(0, DEVICES - 1)
    pltpu.make_async_copy(recv.at[rest], recv.at[rest], recv_sem).wait()
    pltpu.make_async_copy(send.at[rest], send.at[rest], send_sem).wait()


def share_kernel(
    cell_ref,
    test_ref,
    value_ref,
    class_ref,
    wells_ref,
    cls_ref,
    edge_ref,
    rows,
    send,
    mine,
    edges,
    wells_sem,
    cls_sem,
    edge_sem,
):
    me = my_index()
    gx, gy = lax.axis_index("gx"), lax.axis_index("gy")
    lane = lax.broadcasted_iota(jnp.int32, (32, 128), 1)
    classes = class_ref[...].reshape(CX * NZ, CY).astype(F32)
    mine[...] = classes.astype(BF16)
    for side, first in ((0, 0), (1, CY - RIM)):
        pack = jnp.zeros((32, 128), F32)
        for g in range(8):
            here = (lane >= RIM * g) & (lane < RIM * g + RIM)
            pack = jnp.where(here, roll_to(classes[32 * g : 32 * g + 32], RIM * g - first), pack)
        edges[side] = pack.astype(BF16)
    edge_ref[...] = jnp.zeros_like(edge_ref)

    cell, test, value = cell_ref[...], test_ref[...], value_ref[...]
    n_rows = 2 * cell.shape[1]
    y = cell % (CY * N_GY)
    z = cell // (CY * N_GY) % NZ
    x = cell // (CY * N_GY * NZ)
    block = y // HALF
    within = y % HALF
    step = jnp.where(within < RIM, -1, jnp.where(within >= HALF - RIM, 1, 0))
    other = block + step
    valid = (step != 0) & (other >= 0) & (other < 2 * N_GY)

    def twice(first, second):
        return jnp.concatenate([first, second], axis=1)

    block, y, z, x = twice(block, other), twice(y, y), twice(z, z), twice(x, x)
    test, value = twice(test, test), twice(value, value)
    owner = (block % 2 * 4 + test) * N_GY + block // 2
    owner = twice(owner[:, : n_rows // 2], jnp.where(valid, owner[:, n_rows // 2 :], -1))
    y_loc = y - (block * HALF - RIM)
    x_low = x % XL
    high = ((x_low % 4 * YL + y_loc % YL) * 8 + z % 8) * 8 + z // 8
    low = x_low // 4 * 128 + x // XL * 32 + y_loc // YL
    code = (high * 256 + low).astype(F32)
    hot = jnp.where(
        lax.broadcasted_iota(jnp.int32, (DEVICES, n_rows), 0) == owner, 1.0, 0.0
    )
    earlier = jnp.where(
        lax.broadcasted_iota(jnp.int32, (n_rows, n_rows), 0)
        < lax.broadcasted_iota(jnp.int32, (n_rows, n_rows), 1),
        1.0,
        0.0,
    )
    hot16 = hot.astype(BF16)
    count = jnp.dot(hot16, earlier.astype(BF16), preferred_element_type=F32)
    rank = jnp.sum(hot * count, axis=0, keepdims=True).astype(jnp.int32)
    slot = lax.broadcasted_iota(jnp.int32, (SLOTS, n_rows), 0)
    part = jnp.concatenate(
        [jnp.where(slot == rank, code, 0.0), jnp.where(slot == rank, value, 0.0)], axis=0
    )
    total = None
    for _ in range(3):
        piece = part.astype(BF16)
        part = part - piece.astype(F32)
        term = lax.dot_general(hot16, piece, NT, preferred_element_type=F32)
        total = term if total is None else total + term
    for k in range(4):
        rows[k] = total[:, 128 * k : 128 * k + 128]
    for dev in range(DEVICES):
        for k in range(4):
            send[dev, k : k + 1, :] = rows[k, dev : dev + 1, :]

    greet_all(me)

    def cls_copy(k):
        return pltpu.make_async_remote_copy(
            src_ref=mine,
            dst_ref=cls_ref.at[gx],
            send_sem=cls_sem.at[0],
            recv_sem=cls_sem.at[1],
            device_id=(lax.rem(gx + k, N_GX), gy),
            device_id_type=MESH,
        )

    for k in range(1, N_GX):
        cls_copy(k).start()

    def edge_copy(side, k):
        return pltpu.make_async_remote_copy(
            src_ref=edges.at[side],
            dst_ref=edge_ref.at[gx],
            send_sem=edge_sem.at[side],
            recv_sem=edge_sem.at[2],
            device_id=(k + 4 * (1 - side), lax.rem(gy + N_GY - 1 + 2 * side, N_GY)),
            device_id_type=MESH,
        )

    @pl.when(gy > 0)
    def _():
        for k in range(4):
            edge_copy(0, k).start()

    @pl.when(gy < N_GY - 1)
    def _():
        for k in range(4):
            edge_copy(1, k).start()

    cls_ref[gx] = mine[...]
    send_to_all(me, send, wells_ref, wells_sem.at[0], wells_sem.at[1])
    seven = pl.ds(0, N_GX - 1)
    pltpu.make_async_copy(cls_ref.at[seven], cls_ref.at[seven], cls_sem.at[1]).wait()
    pltpu.make_async_copy(cls_ref.at[seven], cls_ref.at[seven], cls_sem.at[0]).wait()
    four = pl.ds(0, 4)

    @pl.when(gy > 0)
    def _():
        pltpu.make_async_copy(edge_ref.at[four], edge_ref.at[four], edge_sem.at[0]).wait()

    @pl.when(gy < N_GY - 1)
    def _():
        pltpu.make_async_copy(edge_ref.at[four], edge_ref.at[four], edge_sem.at[1]).wait()

    upper = gx >= 4

    @pl.when((upper & (gy < N_GY - 1)) | (jnp.logical_not(upper) & (gy > 0)))
    def _():
        pltpu.make_async_copy(edge_ref, edge_ref, edge_sem.at[2]).wait()


def share_call(cell, test, value, classes):
    return pl.pallas_call(
        share_kernel,
        out_shape=(
            jax.ShapeDtypeStruct((DEVICES, 4, 128), F32),
            jax.ShapeDtypeStruct((N_GX, CX * NZ, CY), BF16),
            jax.ShapeDtypeStruct((N_GX, 32, 128), BF16),
        ),
        in_specs=[VMEM] * 4,
        out_specs=(VMEM,) * 3,
        scratch_shapes=[
            pltpu.VMEM((4, DEVICES, 128), F32),
            pltpu.VMEM((DEVICES, 4, 128), F32),
            pltpu.VMEM((CX * NZ, CY), BF16),
            pltpu.VMEM((2, 32, 128), BF16),
            pltpu.SemaphoreType.DMA((2,)),
            pltpu.SemaphoreType.DMA((2,)),
            pltpu.SemaphoreType.DMA((3,)),
        ],
        compiler_params=pltpu.CompilerParams(
            collective_id=0, has_side_effects=True, vmem_limit_bytes=48 * MIB
        ),
    )(cell, test, value, classes)


def roll_to(value, shift):
    shift = shift % 128
    return pltpu.roll(value, shift, 1) if shift else value


def sweeps_kernel(
    wells_ref,
    cls_ref,
    edge_ref,
    class_value_ref,
    out_ref,
    rows,
    plane,
    cond,
    face_x,
    face_y,
    face_z,
    extra,
    dirs,
    resid,
    sol,
    flux,
    acc,
):
    gx, gy = lax.axis_index("gx"), lax.axis_index("gy")
    half = gx // 4
    lane = lax.broadcasted_iota(jnp.int32, (8, 128), 1)
    sub = lax.broadcasted_iota(jnp.int32, (8, 128), 0)
    x_high, y_high = lane // 32, lane % 32

    def tile(j):
        return slice(8 * j, 8 * j + 8)

    from_lane = lax.broadcasted_iota(jnp.int32, (128, 128), 0)
    to_lane = lax.broadcasted_iota(jnp.int32, (128, 128), 1)
    local = (from_lane + jnp.where(half == 0, RIM, HALF + RIM)) % 128
    picks = [
        jnp.where(local == YL * (to_lane % 32) + low, 1.0, 0.0).astype(BF16) for low in range(YL)
    ]
    lane32 = lax.broadcasted_iota(jnp.int32, (32, 128), 1)
    rim_at = jnp.where(half == 0, CY - RIM, 0)
    in_rim = (lane32 >= rim_at) & (lane32 < rim_at + RIM)
    group64 = lax.broadcasted_iota(jnp.int32, (NZ, 128), 1) // 32

    def whole(x):
        o = x // CX
        own = cls_ref[o, NZ * (x % CX) : NZ * (x % CX) + NZ, :].astype(F32)
        side = edge_ref[o].astype(F32)
        parts = []
        for g in (2 * (x % CX), 2 * (x % CX) + 1):
            moved = pltpu.roll(side, lax.rem(rim_at + 128 - RIM * g, 128), 1)
            parts.append(jnp.where(in_rim, moved, own[32 * (g % 2) : 32 * (g % 2) + 32]))
        return jnp.concatenate(parts, axis=0).astype(BF16)

    for x_low in range(XL):
        blocks = jnp.concatenate([whole(XL * h + x_low) for h in range(4)], axis=0)
        for y_low in range(YL):
            moved = jnp.dot(blocks, picks[y_low], preferred_element_type=F32)
            merged = moved[0:NZ]
            for h in range(1, 4):
                merged = jnp.where(group64 == h, moved[NZ * h : NZ * h + NZ], merged)
            value = jnp.zeros((NZ, 128), F32)
            for k in range(NCLASS):
                value = jnp.where(merged == float(k), class_value_ref[k], value)
            plane[...] = value
            for j in range(8):
                cond[x_low, y_low, tile(j), :] = plane[pl.ds(j, 8, stride=8), :]

    zero = jnp.zeros((8, 128), F32)
    first_y = jnp.where((gy == 0) & (half == 0), RIM, -1)
    last_y = jnp.where((gy == N_GY - 1) & (half == 1), RIM + HALF - 1, -2)

    def faces(x_low, _):
        for y_low in range(YL):
            y_loc = YL * y_high + y_low
            for j in range(8):
                c = cond[x_low, y_low, tile(j), :]
                more = jnp.full((8, 128), storage, F32)
                end = x_low == XL - 1
                near = cond[jnp.where(end, 0, x_low + 1), y_low, tile(j), :]
                near = jnp.where(end, pltpu.roll(near, 96, 1), near)
                off = end & (x_high == 3)
                face_x[x_low, y_low, tile(j), :] = jnp.where(off, zero, 0.5 * (c + near))
                more = more + jnp.where(off, 0.5 * c, zero)
                more = more + jnp.where((x_low == 0) & (x_high == 0), 0.5 * c, zero)
                if y_low < YL - 1:
                    near = cond[x_low, y_low + 1, tile(j), :]
                    off = y_loc + 1 == first_y
                else:
                    near = pltpu.roll(cond[x_low, 0, tile(j), :], 127, 1)
                    off = (y_loc + 1 == first_y) | (y_high == 31)
                off = off | (y_loc == last_y)
                face_y[x_low, y_low, tile(j), :] = jnp.where(off, zero, 0.5 * (c + near))
                more = more + jnp.where((y_loc == first_y) | (y_loc == last_y), 0.5 * c, zero)
                if j < 7:
                    face_z[x_low, y_low, tile(j), :] = 0.5 * (c + cond[x_low, y_low, tile(j + 1), :])
                else:
                    near = pltpu.roll(cond[x_low, y_low, tile(0), :], 7, 0)
                    face_z[x_low, y_low, tile(j), :] = jnp.where(sub == 7, zero, 0.5 * (c + near))
                    more = more + jnp.where(sub == 7, 0.5 * c, zero)
                if j == 0:
                    more = more + jnp.where(sub == 0, 0.5 * c, zero)
                extra[x_low, y_low, tile(j), :] = more
        return 0

    lax.fori_loop(0, XL, faces, 0)

    for dev in range(DEVICES):
        for k in range(4):
            rows[k, dev : dev + 1, :] = wells_ref[dev, k : k + 1, :]
    lane16 = lax.broadcasted_iota(jnp.int32, (16, 128), 1)
    row_high = lax.broadcasted_iota(jnp.int32, (HIGHS, 128), 0)
    row_low = lax.broadcasted_iota(jnp.int32, (256, 128), 0)
    acc[...] = jnp.zeros_like(acc)

    def level(n, _):
        row, at = n // 8, n % 8 * CAP
        codes = jnp.zeros((16, 128), F32)
        values = jnp.zeros((16, 128), F32)
        for g in range(8):
            here = lane16 // CAP == g
            turn = lax.rem(CAP * g + 128 - at, 128)
            block = rows[row, 16 * g : 16 * g + 16, :]
            codes = jnp.where(here, pltpu.roll(block, turn, 1), codes)
            block = rows[2 + row, 16 * g : 16 * g + 16, :]
            values = jnp.where(here, pltpu.roll(block, turn, 1), values)

        @pl.when(jnp.max(jnp.abs(values)) > 0.0)
        def _():
            whole_codes = codes.astype(jnp.int32)
            highs, lows = whole_codes // 256, whole_codes % 256
            first = values.astype(BF16).astype(F32)
            second = values - first
            left, right_a, right_b = [], [], []
            for r in range(16):
                left.append(jnp.where(row_high == highs[r : r + 1], 1.0, 0.0).astype(BF16))
                same = row_low == lows[r : r + 1]
                right_a.append(jnp.where(same, first[r : r + 1], 0.0).astype(BF16))
                right_b.append(jnp.where(same, second[r : r + 1], 0.0).astype(BF16))
            left = jnp.concatenate(left, axis=1)
            acc[...] += lax.dot_general(
                left, jnp.concatenate(right_a, axis=1), NT, preferred_element_type=F32
            ) + lax.dot_general(
                left, jnp.concatenate(right_b, axis=1), NT, preferred_element_type=F32
            )

        return 0

    lax.fori_loop(0, SLOTS // CAP, level, 0)

    middle, factors = cheb_setup()
    for x_low in range(XL):
        for y_low in range(YL):
            at = NZ * (x_low % 4 * YL + y_low)
            value = acc[at : at + NZ, x_low // 4 * 128 : x_low // 4 * 128 + 128]
            resid[x_low, y_low] = value
            dirs[0, x_low, y_low] = value / middle
            sol[x_low, y_low] = jnp.zeros((NZ, 128), F32)

    keeps = [pair[0] for pair in factors]
    news = [pair[1] for pair in factors]

    def sweep(k, _):
        par = lax.rem(k, 2)
        nxt = 1 - par
        keep, new = jnp.float32(keeps[0]), jnp.float32(news[0])
        for n in range(1, SWEEPS - 1):
            keep = jnp.where(k == n, jnp.float32(keeps[n]), keep)
            new = jnp.where(k == n, jnp.float32(news[n]), new)
        for y_low in range(YL):
            for j in range(8):
                over = face_x[XL - 1, y_low, tile(j), :] * (
                    pltpu.roll(dirs[par, 0, y_low, tile(j), :], 96, 1)
                    - dirs[par, XL - 1, y_low, tile(j), :]
                )
                flux[XL - 1, y_low, tile(j), :] = over
                flux[XL, y_low, tile(j), :] = pltpu.roll(over, 32, 1)
        for x_low in range(XL):
            behind = XL if x_low == 0 else x_low - 1
            v = [[dirs[par, x_low, y_low, tile(j), :] for y_low in range(YL)] for j in range(8)]
            z_old = []
            for y_low in range(YL):
                z_old.append(
                    pltpu.roll(
                        face_z[x_low, y_low, tile(7), :]
                        * (pltpu.roll(v[0][y_low], 7, 0) - v[7][y_low]),
                        1,
                        0,
                    )
                )
            for j in range(8):
                fy = [
                    face_y[x_low, y_low, tile(j), :]
                    * (
                        (v[j][y_low + 1] if y_low < YL - 1 else pltpu.roll(v[j][0], 127, 1))
                        - v[j][y_low]
                    )
                    for y_low in range(YL)
                ]
                for y_low in range(YL):
                    here = v[j][y_low]
                    at = (x_low, y_low, tile(j))
                    if x_low < XL - 1:
                        fx = face_x[at] * (dirs[par, x_low + 1, y_low, tile(j), :] - here)
                        flux[at] = fx
                    else:
                        fx = flux[at]
                    above = v[j + 1][y_low] if j < 7 else pltpu.roll(v[0][y_low], 7, 0)
                    fz = face_z[at] * (above - here)
                    fy_old = fy[y_low - 1] if y_low else pltpu.roll(fy[YL - 1], 1, 1)
                    gain = (fx - flux[behind, y_low, tile(j), :]) + (fy[y_low] - fy_old)
                    gain = gain + (fz - z_old[y_low])
                    z_old[y_low] = fz
                    left = resid[at] + (gain - extra[at] * here)
                    resid[at] = left
                    sol[at] = sol[at] + here
                    dirs[nxt, x_low, y_low, tile(j), :] = keep * here + new * left
        return 0

    lax.fori_loop(0, SWEEPS - 1, sweep, 0)
    last = (SWEEPS - 1) % 2

    row = lax.broadcasted_iota(jnp.int32, (YL * 128, 256), 0)
    col = lax.broadcasted_iota(jnp.int32, (YL * 128, 256), 1)
    put = jnp.where(
        (row % 128 // 32 == col // HALF)
        & (YL * (row % 32) + row // 128 == col % HALF + RIM),
        1.0,
        0.0,
    ).astype(BF16)
    left_half = lax.broadcasted_iota(jnp.int32, (NZ, 128), 1) < HALF
    for odd in range(2):
        wide = []
        for x_low in range(4 * odd, 4 * odd + 4):
            field = jnp.concatenate(
                [sol[x_low, y_low] + dirs[last, x_low, y_low] for y_low in range(YL)], axis=1
            )
            first = field.astype(BF16)
            second = (field - first.astype(F32)).astype(BF16)
            wide.append(
                jnp.dot(first, put, preferred_element_type=F32)
                + jnp.dot(second, put, preferred_element_type=F32)
            )
        for h in range(4):
            lanes = slice(128 * (h // 2), 128 * (h // 2) + 128)
            for n in range(2):
                a, b = wide[n][:, lanes], wide[n + 2][:, lanes]
                if h % 2 == 0:
                    both = jnp.where(left_half, a, pltpu.roll(b, 64, 1))
                else:
                    both = jnp.where(left_half, pltpu.roll(a, 64, 1), b)
                for j in range(8):
                    out_ref[2 * h + odd, pl.ds(NZ * n + j, 8, stride=8), :] = both[tile(j)]


def sweeps_call(wells, classes, edges, class_value):
    block = (XL, YL, NZ, 128)
    return pl.pallas_call(
        sweeps_kernel,
        out_shape=jax.ShapeDtypeStruct((N_GX, 2 * NZ, 128), F32),
        in_specs=[VMEM] * 3 + [pl.BlockSpec(memory_space=pltpu.SMEM)],
        out_specs=VMEM,
        scratch_shapes=[
            pltpu.VMEM((4, DEVICES, 128), F32),
            pltpu.VMEM((NZ, 128), F32),
            pltpu.VMEM(block, F32),
            pltpu.VMEM(block, F32),
            pltpu.VMEM(block, F32),
            pltpu.VMEM(block, F32),
            pltpu.VMEM(block, F32),
            pltpu.VMEM((2,) + block, F32),
            pltpu.VMEM(block, F32),
            pltpu.VMEM(block, F32),
            pltpu.VMEM((XL + 1, YL, NZ, 128), F32),
            pltpu.VMEM((HIGHS, 256), F32),
        ],
        compiler_params=pltpu.CompilerParams(vmem_limit_bytes=48 * MIB),
    )(wells, classes, edges, class_value)


def groups_of(gx, gy):
    tail = gx == N_GX - 1
    low = jnp.where(tail, gy % 8, gy)
    high = jnp.where(tail, gy % 8 + 8, (gy + gx + 1) % GROUPS)
    return low, high, tail & (gy >= 8)


def takers_of(group):
    out = []
    for k in range(N_GX - 1):
        out.append(((k, group), 0))
        out.append(((k, (group + GROUPS - k - 1) % GROUPS), 1))
    place = group // 8
    out.append(((N_GX - 1, group % 8), place))
    out.append(((N_GX - 1, group % 8 + 8), place))
    return out


ROWS_STEP = 8


def zones_kernel(
    zone_ref,
    adj_ref,
    class_ref,
    class_value_ref,
    draw_ref,
    out_ref,
    adj,
    sens_ref,
    owner_of,
    left,
    right,
    acc,
    send,
    recv,
    mine,
    sem,
    got_sem,
    put_sem,
    adj_sem,
):
    me = my_index()
    gx, gy = lax.axis_index("gx"), lax.axis_index("gy")
    greet_all(me)

    def back(k):
        dev = lax.rem(gx + k, N_GX)
        return pltpu.make_async_remote_copy(
            src_ref=adj_ref.at[dev],
            dst_ref=adj.at[gx],
            send_sem=adj_sem.at[0],
            recv_sem=adj_sem.at[1],
            device_id=(dev, gy),
            device_id_type=MESH,
        )

    for k in range(1, N_GX):
        back(k).start()
    adj[gx] = adj_ref[gx]
    left_half = lax.broadcasted_iota(jnp.int32, (NZ, 128), 1) < HALF
    owner_of[...] = (
        (lax.broadcasted_iota(jnp.int32, (TESTS * DEVICES, 128), 0) // TESTS)
        .astype(F32)
        .astype(BF16)
    )
    acc[...] = jnp.zeros_like(acc)
    inner = lax.broadcasted_iota(jnp.int32, (256, 128), 0).astype(F32).astype(BF16)
    sub = lax.broadcasted_iota(jnp.int32, (8, 128), 0) % TESTS
    conduct = []
    for x in range(CX):
        cls = class_ref[NZ * x : NZ * x + NZ, :]
        value = jnp.zeros((NZ, CY), F32)
        for k in range(NCLASS):
            value = jnp.where(cls == k, class_value_ref[k], value)
        conduct.append(value)
    seven = pl.ds(0, N_GX - 1)
    pltpu.make_async_copy(adj.at[seven], adj.at[seven], adj_sem.at[1]).wait()
    for t in range(TESTS):
        for n in range(2):
            a, b = adj[t, NZ * n : NZ * n + NZ, :], adj[4 + t, NZ * n : NZ * n + NZ, :]
            for x, field in (
                (n, jnp.where(left_half, a, pltpu.roll(b, 64, 1))),
                (n + 2, jnp.where(left_half, pltpu.roll(a, 64, 1), b)),
            ):
                at = slice(NZ * x, NZ * x + NZ)
                sens_ref[t, at, :] = conduct[x] * draw_ref[t, at, :].astype(F32) * field

    def spread(row, times):
        return jnp.concatenate([jnp.broadcast_to(row, (16, 128)).astype(BF16)] * times, axis=0)

    def step(i, _):
        at = pl.ds(pl.multiple_of(i * ROWS_STEP, ROWS_STEP), ROWS_STEP)
        zone = zone_ref[at, :].astype(F32)
        owner = ((zone + 0.5) * (1.0 / SHARE)).astype(jnp.int32).astype(F32)
        place = zone - owner * SHARE
        values = [sens_ref[t, at, :] for t in range(TESTS)]
        for r in range(ROWS_STEP):
            row = slice(r, r + 1)
            four = jnp.broadcast_to(values[0][row], (8, 128))
            for t in range(1, TESTS):
                four = jnp.where(sub == t, jnp.broadcast_to(values[t][row], (8, 128)), four)
            four = jnp.concatenate([four, four], axis=0).astype(BF16)
            cols = slice(128 * r, 128 * r + 128)
            left[:, cols] = jnp.where(
                owner_of[...] == spread(owner[row], TESTS * DEVICES // 16),
                jnp.concatenate([four] * (TESTS * DEVICES // 16), axis=0),
                jnp.zeros((), BF16),
            )
            for part in range(SHARE // 256):
                right[256 * part : 256 * part + 256, cols] = jnp.where(
                    inner == spread(place[row] - 256.0 * part, 16),
                    jnp.ones((), BF16),
                    jnp.zeros((), BF16),
                )
        acc[...] += lax.dot_general(left[...], right[...], NT, preferred_element_type=F32)
        return 0

    lax.fori_loop(0, CX * NZ // ROWS_STEP, step, 0)
    for dev in range(DEVICES):
        send[dev] = acc[TESTS * dev : TESTS * dev + TESTS, :]

    send_to_all(me, send, recv, sem.at[0], sem.at[1])
    pltpu.make_async_copy(adj.at[seven], adj.at[seven], adj_sem.at[0]).wait()

    def add(s, total):
        for n in range(8):
            total = total + recv[8 * s + n]
        return total

    total = lax.fori_loop(0, DEVICES // 8, add, jnp.zeros((TESTS, SHARE), F32))
    mine[...] = total.astype(BF16).astype(F32)

    group, member = me // MEMBERS, me % MEMBERS

    def put(n, dev, place):
        return pltpu.make_async_remote_copy(
            src_ref=mine,
            dst_ref=out_ref.at[place, member],
            send_sem=put_sem.at[n],
            recv_sem=got_sem.at[place, member],
            device_id=dev,
            device_id_type=MESH,
        )

    takers = takers_of(group)
    for n, (dev, place) in enumerate(takers):
        self_here = dev[0] * N_GY + dev[1] == me

        @pl.when(jnp.logical_not(self_here))
        def _():
            put(n, dev, place).start()

        @pl.when(self_here)
        def _():
            out_ref[place, member] = mine[...]

    low, high, _ = groups_of(gx, gy)
    for place, held in ((0, low), (1, high)):
        for m in range(MEMBERS):

            @pl.when(held * MEMBERS + m != me)
            def _():
                pltpu.make_async_copy(
                    out_ref.at[place, m], out_ref.at[place, m], got_sem.at[place, m]
                ).wait()

    for n, (dev, place) in enumerate(takers):

        @pl.when(dev[0] * N_GY + dev[1] != me)
        def _():
            put(n, dev, place).wait_send()


def zones_call(zone, adjoint, classes, class_value, drawdown):
    rows = TESTS * DEVICES
    width = ROWS_STEP * 128
    return pl.pallas_call(
        zones_kernel,
        out_shape=jax.ShapeDtypeStruct((2, MEMBERS, TESTS, SHARE), F32),
        in_specs=[VMEM] * 3 + [pl.BlockSpec(memory_space=pltpu.SMEM), VMEM],
        out_specs=VMEM,
        scratch_shapes=[
            pltpu.VMEM((N_GX, 2 * NZ, 128), F32),
            pltpu.VMEM((TESTS, CX * NZ, CY), F32),
            pltpu.VMEM((rows, 128), BF16),
            pltpu.VMEM((rows, width), BF16),
            pltpu.VMEM((SHARE, width), BF16),
            pltpu.VMEM((rows, SHARE), F32),
            pltpu.VMEM((DEVICES, TESTS, SHARE), F32),
            pltpu.VMEM((DEVICES, TESTS, SHARE), F32),
            pltpu.VMEM((TESTS, SHARE), F32),
            pltpu.SemaphoreType.DMA((2,)),
            pltpu.SemaphoreType.DMA((2, MEMBERS)),
            pltpu.SemaphoreType.DMA((16,)),
            pltpu.SemaphoreType.DMA((2,)),
        ],
        compiler_params=pltpu.CompilerParams(
            collective_id=2, has_side_effects=True, vmem_limit_bytes=48 * MIB
        ),
    )(zone, adjoint, classes, class_value, drawdown)


BLOCK = 1024
STRIP = 64


def cov_kernel(diag_ref, pts_ref, sums_ref, out_ref, z_ref, rows_ref, tile_ref):
    blocks = GROUP // BLOCK
    diag = diag_ref[0]
    out_ref[...] = jnp.zeros_like(out_ref)
    for g in range(2):
        for m in range(MEMBERS):
            both = jnp.concatenate([sums_ref[g, m], jnp.zeros((TESTS, SHARE), F32)], axis=0)
            z_ref[g, :, SHARE * m : SHARE * m + SHARE] = both.astype(BF16)

    def tile(cg, c):
        cols = [pts_ref[cg, k : k + 1, pl.ds(pl.multiple_of(c * BLOCK, BLOCK), BLOCK)] for k in range(3)]

        def body(i, _):
            r0 = pl.multiple_of(i * STRIP, STRIP)
            squared = None
            for k in range(3):
                near = jnp.concatenate([rows_ref[k, pl.ds(r0, STRIP), :]] * (BLOCK // 128), axis=1)
                gap = near - cols[k]
                squared = gap * gap if squared is None else squared + gap * gap
            squared = jnp.maximum(squared, 1e-30)
            dist = squared * lax.rsqrt(squared)
            tile_ref[pl.ds(r0, STRIP), :] = jnp.exp2(-dist).astype(BF16)
            return 0

        lax.fori_loop(0, BLOCK // STRIP, body, 0, unroll=True)

    def phase(rg, _):
        cg = jnp.where(diag == 1, rg, 1)

        def row_block(r, _):
            rs = pl.ds(pl.multiple_of(r * BLOCK, BLOCK), BLOCK)
            for k in range(3):
                rows_ref[k] = jnp.broadcast_to(pts_ref[rg, k : k + 1, rs], (128, BLOCK)).T
            near = z_ref[rg, :, rs]

            def col_block(c, acc):
                tile(cg, c)
                cs = pl.ds(pl.multiple_of(c * BLOCK, BLOCK), BLOCK)
                acc = acc + lax.dot_general(
                    z_ref[cg, :, cs], tile_ref[...], NT, preferred_element_type=F32
                )

                @pl.when(jnp.logical_not((diag == 1) & (c == r)))
                def _():
                    out_ref[cg, :, cs] += jnp.dot(near, tile_ref[...], preferred_element_type=F32)

                return acc

            first = jnp.where(diag == 1, r, 0)
            acc = lax.fori_loop(first, blocks, col_block, jnp.zeros((8, BLOCK), F32))
            out_ref[rg, :, rs] += acc
            return 0

        lax.fori_loop(0, blocks, row_block, 0)
        return 0

    lax.fori_loop(0, 1 + diag, phase, 0)


def cov_call(diag, pts, sums):
    return pl.pallas_call(
        cov_kernel,
        out_shape=jax.ShapeDtypeStruct((2, 8, GROUP), F32),
        in_specs=[pl.BlockSpec(memory_space=pltpu.SMEM), VMEM, VMEM],
        out_specs=VMEM,
        scratch_shapes=[
            pltpu.VMEM((2, 8, GROUP), BF16),
            pltpu.VMEM((3, BLOCK, 128), F32),
            pltpu.VMEM((BLOCK, BLOCK), BF16),
        ],
        compiler_params=pltpu.CompilerParams(vmem_limit_bytes=48 * MIB),
    )(diag, pts, sums)


def reduce_kernel(part_ref, out_ref, send, recv, send_sem, recv_sem):
    me = my_index()
    gx, gy = lax.axis_index("gx"), lax.axis_index("gy")
    low, high, diag = groups_of(gx, gy)
    group, member = me // MEMBERS, me % MEMBERS
    for g in range(2):
        for m in range(MEMBERS):
            send[g, m] = part_ref[g, 0:TESTS, SHARE * m : SHARE * m + SHARE]

    takers = takers_of(group)
    barrier = pltpu.get_barrier_semaphore()
    for place, held in ((0, low), (1, high)):
        for m in range(MEMBERS):
            owner = held * MEMBERS + m

            @pl.when(owner != me)
            def _():
                pl.semaphore_signal(barrier, inc=1, device_id=coords(owner), device_id_type=MESH)

    for dev, _ in takers:

        @pl.when(dev[0] * N_GY + dev[1] != me)
        def _():
            pl.semaphore_signal(barrier, inc=1, device_id=dev, device_id_type=MESH)

    self_here = (low == group) | (high == group)
    pl.semaphore_wait(barrier, 32 - 2 * self_here.astype(jnp.int32))

    def put(place, m, held, slot):
        return pltpu.make_async_remote_copy(
            src_ref=send.at[place, m],
            dst_ref=recv.at[slot],
            send_sem=send_sem.at[place, m],
            recv_sem=recv_sem.at[slot],
            device_id=coords(held * MEMBERS + m),
            device_id_type=MESH,
        )

    sides = (
        (0, low, jnp.where(diag, low, high)),
        (1, high, jnp.where(diag, high, low)),
    )
    for place, held, slot in sides:
        for m in range(MEMBERS):

            @pl.when(held * MEMBERS + m != me)
            def _():
                put(place, m, held, slot).start()

            @pl.when(held * MEMBERS + m == me)
            def _():
                recv[slot] = send[place, m]

    own_slot = jnp.where(
        low == group, jnp.where(diag, low, high), jnp.where(diag, high, low)
    )
    for slot in range(GROUPS):

        @pl.when(jnp.logical_not(self_here & (own_slot == slot)))
        def _():
            pltpu.make_async_copy(recv.at[slot], recv.at[slot], recv_sem.at[slot]).wait()

    total = recv[0]
    for slot in range(1, GROUPS):
        total = total + recv[slot]
    out_ref[...] = total.astype(BF16)
    for place, held, slot in sides:
        for m in range(MEMBERS):

            @pl.when(held * MEMBERS + m != me)
            def _():
                put(place, m, held, slot).wait_send()


def reduce_call(parts):
    return pl.pallas_call(
        reduce_kernel,
        out_shape=jax.ShapeDtypeStruct((TESTS, SHARE), BF16),
        in_specs=[VMEM],
        out_specs=VMEM,
        scratch_shapes=[
            pltpu.VMEM((2, MEMBERS, TESTS, SHARE), F32),
            pltpu.VMEM((GROUPS, TESTS, SHARE), F32),
            pltpu.SemaphoreType.DMA((2, MEMBERS)),
            pltpu.SemaphoreType.DMA((GROUPS,)),
        ],
        compiler_params=pltpu.CompilerParams(
            collective_id=3, has_side_effects=True, vmem_limit_bytes=32 * MIB
        ),
    )(parts)


def per_device(
    well_cell, well_test, well_value, cond_class, class_value, zone_id, drawdown, centroid
):
    gx, gy = lax.axis_index("gx"), lax.axis_index("gy")
    low, high, diag = groups_of(gx, gy)
    pts = jnp.stack(
        [lax.dynamic_slice_in_dim(centroid, held * GROUP, GROUP, 1) for held in (low, high)]
    ) * (LOG2E / corr_len)
    wells, classes, edges = share_call(
        well_cell[None], well_test[None], well_value[None], cond_class
    )
    adjoint = sweeps_call(wells, classes, edges, class_value)
    rows = CX * NZ
    sums = zones_call(
        zone_id.reshape(rows, CY),
        adjoint,
        cond_class.reshape(rows, CY),
        class_value,
        drawdown.reshape(TESTS, rows, CY),
    )
    parts = cov_call(diag.astype(jnp.int32)[None], pts, sums)
    return reduce_call(parts)


def solution(mesh):
    return jax.shard_map(
        per_device,
        mesh=mesh,
        in_specs=(
            P(("gx", "gy")),
            P(("gx", "gy")),
            P(("gx", "gy")),
            P("gx", None, "gy"),
            P(),
            P("gx", None, "gy"),
            P(None, "gx", None, "gy"),
            P(),
        ),
        out_specs=P(None, ("gx", "gy")),
        check_vma=False,
    )
```

time: 318 us -> 252 us (0.79)
  Pallas kernels: 313 us -> 246 us
    pallas_call x2, Pallas kernels: 117 us -> 45.2 us  [the longest x1 26.6 us: share_call(): pl.pallas_call(share_kernel, out_shape=(jax.ShapeDtypeStruct((DEVICES, 4,...]
    pallas_call x1, Pallas kernels: 76 us -> 82.5 us  [zones_call(): pl.pallas_call(zones_kernel, out_shape=jax.ShapeDtypeStruct((2, MEMBERS,...]
where the time goes in v2:
time: 252 us
  Pallas kernels  246 us (98%)
  local copies, waits for them, and re-layouts  5.23 us (2%)
    pallas_call x1, Pallas kernels, cov_call(): pl.pallas_call(cov_kernel, out_shape=jax.ShapeDtypeStruct((2, 8, GROUP),...  91.6 us
    pallas_call x1, Pallas kernels, zones_call(): pl.pallas_call(zones_kernel, out_shape=jax.ShapeDtypeStruct((2, MEMBERS,...  82.5 us
    pallas_call x1, Pallas kernels, reduce_call(): pl.pallas_call(reduce_kernel, out_shape=jax.ShapeDtypeStruct((TESTS, SHAR...  27 us
    pallas_call x1, Pallas kernels, share_call(): pl.pallas_call(share_kernel, out_shape=(jax.ShapeDtypeStruct((DEVICES, 4,...  26.6 us
    pallas_call x1, Pallas kernels, sweeps_call(): pl.pallas_call(sweeps_kernel, out_shape=jax.ShapeDtypeStruct((N_GX, 2 * N...  18.7 us

profile of v2, /device:TPU:1, one launch (start us, length us, event | category | flops | bytes accessed | tf_op | source)
XLA Modules:
  0.0 251.8 jit_solution(2063354519049645521)
XLA Ops:
  0.0 0.0 copy-start.1
  0.0 0.0 copy-start.2
  0.0 0.0 copy-start.3
  0.1 1.0 dynamic-slice_bitcast_fusion.1
  1.1 0.1 maximum_multiply_fusion.pts_ref
  1.2 0.0 copy-start
  1.2 0.9 copy-done
  2.1 0.0 copy-start.5
  2.1 0.7 copy-done.5
  2.8 0.0 copy-start.6
  2.8 0.7 copy-done.6
  3.4 0.0 copy-start.7
  3.4 0.7 copy-done.7
  4.1 26.6 %shard_map.82 = (f32[128,4,128]{2,1,0:T(4,128)S(1)}, bf16[8,256,128]{2,1,0:T(8,128)(2,1)S(1)}, bf16[8,32,128]{2,1,0:T(8,128)(2,1)S(1)}) custom-call(s32[1,512]{1,0:T(1,128)S(1)} %bitcast.14, s32[1,512]{1,0:T(1,128)S(1)} %bitcast.15, f32[1,512]{1,0:T(1,128)S(1)} %bitcast.16, s32[4,64,128]{2,1,0:T(8,128)S(1)} %copy-done), custom_call_target="tpu_custom_call" | custom-call | tf_op jit(solution)/shard_map/pallas_call | solution.py:240
  30.7 0.0 copy-start.4
  30.7 0.6 copy-done.4
  31.4 18.7 %shard_map.83.adj_ref = f32[8,128,128]{2,1,0:T(8,128)S(1)} custom-call(f32[128,4,128]{2,1,0:T(4,128)S(1)} %get-tuple-element.8.wells_ref, bf16[8,256,128]{2,1,0:T(8,128)(2,1)S(1)} %get-tuple-element.9.cls_ref, bf16[8,32,128]{2,1,0:T(8,128)(2,1)S(1)} %get-tuple-element.10.edge_ref, f32[16]{0:T(128)S(1)} %copy-done.4), custom_call_target="tpu_custom_call" | custom-call | tf_op jit(solution)/shard_map/pallas_call | solution.py:521
  50.0 0.0 copy-done.1
  50.0 0.0 copy-done.2
  50.0 0.0 copy-done.3
  50.1 82.5 %shard_map.84.sums_ref = f32[2,8,4,768]{3,2,1,0:T(4,128)S(1)} custom-call(s32[256,128]{1,0:T(8,128)S(1)} %bitcast.13, f32[8,128,128]{2,1,0:T(8,128)S(1)} %shard_map.83.adj_ref, s32[256,128]{1,0:T(8,128)S(1)} %bitcast.11, f32[16]{0:T(128)S(1)} %copy-done.4, bf16[4,256,128]{2,1,0:T(8,128)(2,1)S(1)} %bitcast.12), custom_call_target="tpu_custom_call" | custom-call | tf_op jit(solution)/shard_map/pallas_call | solution.py:721
  132.6 91.6 %shard_map.85.part_ref = f32[2,8,6144]{2,1,0:T(8,128)S(1)} custom-call(s32[1]{0:T(128)} %bitcast.diag_ref, f32[2,3,6144]{2,1,0:T(4,128)S(1)} %maximum_multiply_fusion.pts_ref, f32[2,8,4,768]{3,2,1,0:T(4,128)S(1)} %shard_map.84.sums_ref), custom_call_target="tpu_custom_call" | custom-call | tf_op jit(solution)/shard_map/pallas_call | solution.py:811
  224.2 27.0 %shard_map.86 = bf16[4,768]{1,0:T(4,128)(2,1)S(1)} custom-call(f32[2,8,6144]{2,1,0:T(8,128)S(1)} %shard_map.85.part_ref), custom_call_target="tpu_custom_call" | custom-call | tf_op jit(solution)/shard_map/pallas_call | solution.py:900
  251.2 0.6 copy.10
Async XLA Ops:
  0.0 50.0 %copy-start.1 = (s32[4,64,128]{2,1,0:T(8,128)S(1)}, s32[4,64,128]{2,1,0:T(8,128)}, u32[]{:S(2)}) copy-start(s32[4,64,128]{2,1,0:T(8,128)} %class_ref.1) | copy-start | bytes 393220
  0.0 50.0 %copy-start.2 = (bf16[4,4,64,128]{3,2,1,0:T(8,128)(2,1)S(1)}, bf16[4,4,64,128]{3,2,1,0:T(8,128)(2,1)}, u32[]{:S(2)}) copy-start(bf16[4,4,64,128]{3,2,1,0:T(8,128)(2,1)} %param.14) | copy-start | bytes 786436
  0.0 50.0 %copy-start.3 = (s32[4,64,128]{2,1,0:T(8,128)S(1)}, s32[4,64,128]{2,1,0:T(8,128)}, u32[]{:S(2)}) copy-start(s32[4,64,128]{2,1,0:T(8,128)} %param.13) | copy-start | bytes 393220
  1.2 0.9 copy-start
  2.1 0.7 copy-start.5
  2.8 0.7 copy-start.6
  3.4 0.7 copy-start.7
  30.7 0.7 copy-start.4

commit v3 on v2

--- a/solution.py
+++ b/solution.py
@@ -266,33 +266,14 @@
     return pltpu.roll(value, shift, 1) if shift else value
 
 
-def sweeps_kernel(
-    wells_ref,
-    cls_ref,
-    edge_ref,
-    class_value_ref,
-    out_ref,
-    rows,
-    plane,
-    cond,
-    face_x,
-    face_y,
-    face_z,
-    extra,
-    dirs,
-    resid,
-    sol,
-    flux,
-    acc,
+def tile(j):
+    return slice(8 * j, 8 * j + 8)
+
+
+def source_kernel(
+    wells_ref, cls_ref, edge_ref, class_value_ref, cond, src_ref, rows, plane, acc
 ):
-    gx, gy = lax.axis_index("gx"), lax.axis_index("gy")
-    half = gx // 4
-    lane = lax.broadcasted_iota(jnp.int32, (8, 128), 1)
-    sub = lax.broadcasted_iota(jnp.int32, (8, 128), 0)
-    x_high, y_high = lane // 32, lane % 32
-
-    def tile(j):
-        return slice(8 * j, 8 * j + 8)
+    half = lax.axis_index("gx") // 4
 
     from_lane = lax.broadcasted_iota(jnp.int32, (128, 128), 0)
     to_lane = lax.broadcasted_iota(jnp.int32, (128, 128), 1)
@@ -328,6 +309,203 @@
             plane[...] = value
             for j in range(8):
                 cond[x_low, y_low, tile(j), :] = plane[pl.ds(j, 8, stride=8), :]
+
+    for dev in range(DEVICES):
+        for k in range(4):
+            rows[k, dev : dev + 1, :] = wells_ref[dev, k : k + 1, :]
+    lane16 = lax.broadcasted_iota(jnp.int32, (16, 128), 1)
+    row_high = lax.broadcasted_iota(jnp.int32, (HIGHS, 128), 0)
+    row_low = lax.broadcasted_iota(jnp.int32, (256, 128), 0)
+    acc[...] = jnp.zeros_like(acc)
+
+    def level(n, _):
+        row, at = n // 8, n % 8 * CAP
+        codes = jnp.zeros((16, 128), F32)
+        values = jnp.zeros((16, 128), F32)
+        for g in range(8):
+            here = lane16 // CAP == g
+            turn = lax.rem(CAP * g + 128 - at, 128)
+            block = rows[row, 16 * g : 16 * g + 16, :]
+            codes = jnp.where(here, pltpu.roll(block, turn, 1), codes)
+            block = rows[2 + row, 16 * g : 16 * g + 16, :]
+            values = jnp.where(here, pltpu.roll(block, turn, 1), values)
+
+        @pl.when(jnp.max(jnp.abs(values)) > 0.0)
+        def _():
+            whole_codes = codes.astype(jnp.int32)
+            highs, lows = whole_codes // 256, whole_codes % 256
+            first = values.astype(BF16).astype(F32)
+            second = values - first
+            left, right_a, right_b = [], [], []
+            for r in range(16):
+                left.append(jnp.where(row_high == highs[r : r + 1], 1.0, 0.0).astype(BF16))
+                same = row_low == lows[r : r + 1]
+                right_a.append(jnp.where(same, first[r : r + 1], 0.0).astype(BF16))
+                right_b.append(jnp.where(same, second[r : r + 1], 0.0).astype(BF16))
+            left = jnp.concatenate(left, axis=1)
+            acc[...] += lax.dot_general(
+                left, jnp.concatenate(right_a, axis=1), NT, preferred_element_type=F32
+            ) + lax.dot_general(
+                left, jnp.concatenate(right_b, axis=1), NT, preferred_element_type=F32
+            )
+
+        return 0
+
+    lax.fori_loop(0, SLOTS // CAP, level, 0)
+
+    for x_low in range(XL):
+        for y_low in range(YL):
+            at = NZ * (x_low % 4 * YL + y_low)
+            src_ref[x_low, y_low] = acc[at : at + NZ, x_low // 4 * 128 : x_low // 4 * 128 + 128]
+
+
+FIELD = (XL, YL, NZ, 128)
+
+
+def source_call(wells, classes, edges, class_value):
+    return pl.pallas_call(
+        source_kernel,
+        out_shape=(jax.ShapeDtypeStruct(FIELD, F32),) * 2,
+        in_specs=[VMEM] * 3 + [pl.BlockSpec(memory_space=pltpu.SMEM)],
+        out_specs=(VMEM,) * 2,
+        scratch_shapes=[
+            pltpu.VMEM((4, DEVICES, 128), F32),
+            pltpu.VMEM((NZ, 128), F32),
+            pltpu.VMEM((HIGHS, 256), F32),
+        ],
+        compiler_params=pltpu.CompilerParams(vmem_limit_bytes=48 * MIB),
+    )(wells, classes, edges, class_value)
+
+
+def groups_of(gx, gy):
+    tail = gx == N_GX - 1
+    low = jnp.where(tail, gy % 8, gy)
+    high = jnp.where(tail, gy % 8 + 8, (gy + gx + 1) % GROUPS)
+    return low, high, tail & (gy >= 8)
+
+
+def takers_of(group):
+    out = []
+    for k in range(N_GX - 1):
+        out.append(((k, group), 0))
+        out.append(((k, (group + GROUPS - k - 1) % GROUPS), 1))
+    place = group // 8
+    out.append(((N_GX - 1, group % 8), place))
+    out.append(((N_GX - 1, group % 8 + 8), place))
+    return out
+
+
+STEP = 16
+INNER = SHARE // 2
+
+
+def main_kernel(
+    cond,
+    src_ref,
+    zone_ref,
+    draw_ref,
+    out_ref,
+    face_x,
+    face_y,
+    face_z,
+    extra,
+    dirs,
+    resid,
+    sol,
+    flux,
+    zone_out,
+    draw_out,
+    zone_in,
+    draw_in,
+    sens,
+    left_a,
+    right_a,
+    left_b,
+    right_b,
+    acc,
+    send_a,
+    recv_a,
+    send_b,
+    recv_b,
+    mine,
+    zone_sem,
+    draw_sem,
+    a_sem,
+    b_sem,
+    got_sem,
+    put_sem,
+):
+    me = my_index()
+    gx, gy = lax.axis_index("gx"), lax.axis_index("gy")
+    half = gx // 4
+    lane = lax.broadcasted_iota(jnp.int32, (8, 128), 1)
+    sub = lax.broadcasted_iota(jnp.int32, (8, 128), 0)
+    x_high, y_high = lane // 32, lane % 32
+    left_half = lax.broadcasted_iota(jnp.int32, (NZ, 128), 1) < HALF
+
+    group, member = me // MEMBERS, me % MEMBERS
+    low_group, high_group, _ = groups_of(gx, gy)
+    takers = takers_of(group)
+    barrier = pltpu.get_barrier_semaphore()
+    for k in range(1, N_GX):
+        pl.semaphore_signal(
+            barrier, inc=1, device_id=(lax.rem(gx + k, N_GX), gy), device_id_type=MESH
+        )
+    for k in range(1, N_GY):
+        pl.semaphore_signal(
+            barrier, inc=1, device_id=(gx, lax.rem(gy + k, N_GY)), device_id_type=MESH
+        )
+    for held in (low_group, high_group):
+        for m in range(MEMBERS):
+            owner = held * MEMBERS + m
+
+            @pl.when(owner != me)
+            def _():
+                pl.semaphore_signal(barrier, inc=1, device_id=coords(owner), device_id_type=MESH)
+
+    for dev, _ in takers:
+
+        @pl.when(dev[0] * N_GY + dev[1] != me)
+        def _():
+            pl.semaphore_signal(barrier, inc=1, device_id=dev, device_id_type=MESH)
+
+    def packed(fields, side, n):
+        a, b = fields[n], fields[n + 2]
+        if side == 0:
+            return jnp.where(left_half, a, pltpu.roll(b, HALF, 1))
+        return jnp.where(left_half, pltpu.roll(a, HALF, 1), b)
+
+    zones = [zone_ref[NZ * x : NZ * x + NZ, :].astype(F32) for x in range(CX)]
+    for side in range(2):
+        for n in range(2):
+            zone_out[side, NZ * n : NZ * n + NZ, :] = packed(zones, side, n)
+    for t in range(TESTS):
+        draws = [draw_ref[t, NZ * x : NZ * x + NZ, :].astype(F32) for x in range(CX)]
+        for side in range(2):
+            for n in range(2):
+                draw_out[TESTS * side + t, NZ * n : NZ * n + NZ, :] = packed(
+                    draws, side, n
+                ).astype(BF16)
+
+    self_here = (low_group == group) | (high_group == group)
+    pl.semaphore_wait(barrier, N_GX + N_GY - 2 + 32 - 2 * self_here.astype(jnp.int32))
+
+    def to_column(k, src, dst, sems):
+        dev = lax.rem(gx + k, N_GX)
+        return pltpu.make_async_remote_copy(
+            src_ref=src(dev),
+            dst_ref=dst,
+            send_sem=sems.at[0],
+            recv_sem=sems.at[1],
+            device_id=(dev, gy),
+            device_id_type=MESH,
+        )
+
+    for k in range(1, N_GX):
+        to_column(k, lambda dev: zone_out.at[dev // TESTS], zone_in.at[gx], zone_sem).start()
+        to_column(k, lambda dev: draw_out.at[dev], draw_in.at[gx], draw_sem).start()
+    zone_in[gx] = zone_out[half]
+    draw_in[gx] = draw_out[gx]
 
     zero = jnp.zeros((8, 128), F32)
     first_y = jnp.where((gy == 0) & (half == 0), RIM, -1)
@@ -368,54 +546,10 @@
 
     lax.fori_loop(0, XL, faces, 0)
 
-    for dev in range(DEVICES):
-        for k in range(4):
-            rows[k, dev : dev + 1, :] = wells_ref[dev, k : k + 1, :]
-    lane16 = lax.broadcasted_iota(jnp.int32, (16, 128), 1)
-    row_high = lax.broadcasted_iota(jnp.int32, (HIGHS, 128), 0)
-    row_low = lax.broadcasted_iota(jnp.int32, (256, 128), 0)
-    acc[...] = jnp.zeros_like(acc)
-
-    def level(n, _):
-        row, at = n // 8, n % 8 * CAP
-        codes = jnp.zeros((16, 128), F32)
-        values = jnp.zeros((16, 128), F32)
-        for g in range(8):
-            here = lane16 // CAP == g
-            turn = lax.rem(CAP * g + 128 - at, 128)
-            block = rows[row, 16 * g : 16 * g + 16, :]
-            codes = jnp.where(here, pltpu.roll(block, turn, 1), codes)
-            block = rows[2 + row, 16 * g : 16 * g + 16, :]
-            values = jnp.where(here, pltpu.roll(block, turn, 1), values)
-
-        @pl.when(jnp.max(jnp.abs(values)) > 0.0)
-        def _():
-            whole_codes = codes.astype(jnp.int32)
-            highs, lows = whole_codes // 256, whole_codes % 256
-            first = values.astype(BF16).astype(F32)
-            second = values - first
-            left, right_a, right_b = [], [], []
-            for r in range(16):
-                left.append(jnp.where(row_high == highs[r : r + 1], 1.0, 0.0).astype(BF16))
-                same = row_low == lows[r : r + 1]
-                right_a.append(jnp.where(same, first[r : r + 1], 0.0).astype(BF16))
-                right_b.append(jnp.where(same, second[r : r + 1], 0.0).astype(BF16))
-            left = jnp.concatenate(left, axis=1)
-            acc[...] += lax.dot_general(
-                left, jnp.concatenate(right_a, axis=1), NT, preferred_element_type=F32
-            ) + lax.dot_general(
-                left, jnp.concatenate(right_b, axis=1), NT, preferred_element_type=F32
-            )
-
-        return 0
-
-    lax.fori_loop(0, SLOTS // CAP, level, 0)
-
     middle, factors = cheb_setup()
     for x_low in range(XL):
         for y_low in range(YL):
-            at = NZ * (x_low % 4 * YL + y_low)
-            value = acc[at : at + NZ, x_low // 4 * 128 : x_low // 4 * 128 + 128]
+            value = src_ref[x_low, y_low]
             resid[x_low, y_low] = value
             dirs[0, x_low, y_low] = value / middle
             sol[x_low, y_low] = jnp.zeros((NZ, 128), F32)
@@ -491,12 +625,14 @@
         1.0,
         0.0,
     ).astype(BF16)
-    left_half = lax.broadcasted_iota(jnp.int32, (NZ, 128), 1) < HALF
     for odd in range(2):
         wide = []
         for x_low in range(4 * odd, 4 * odd + 4):
             field = jnp.concatenate(
-                [sol[x_low, y_low] + dirs[last, x_low, y_low] for y_low in range(YL)], axis=1
+                [
+                    cond[x_low, y_low] * (sol[x_low, y_low] + dirs[last, x_low, y_low])
+                    for y_low in range(YL)
+                ], axis=1
             )
             first = field.astype(BF16)
             second = (field - first.astype(F32)).astype(BF16)
@@ -513,170 +649,92 @@
                 else:
                     both = jnp.where(left_half, pltpu.roll(a, 64, 1), b)
                 for j in range(8):
-                    out_ref[2 * h + odd, pl.ds(NZ * n + j, 8, stride=8), :] = both[tile(j)]
-
-
-def sweeps_call(wells, classes, edges, class_value):
-    block = (XL, YL, NZ, 128)
-    return pl.pallas_call(
-        sweeps_kernel,
-        out_shape=jax.ShapeDtypeStruct((N_GX, 2 * NZ, 128), F32),
-        in_specs=[VMEM] * 3 + [pl.BlockSpec(memory_space=pltpu.SMEM)],
-        out_specs=VMEM,
-        scratch_shapes=[
-            pltpu.VMEM((4, DEVICES, 128), F32),
-            pltpu.VMEM((NZ, 128), F32),
-            pltpu.VMEM(block, F32),
-            pltpu.VMEM(block, F32),
-            pltpu.VMEM(block, F32),
-            pltpu.VMEM(block, F32),
-            pltpu.VMEM(block, F32),
-            pltpu.VMEM((2,) + block, F32),
-            pltpu.VMEM(block, F32),
-            pltpu.VMEM(block, F32),
-            pltpu.VMEM((XL + 1, YL, NZ, 128), F32),
-            pltpu.VMEM((HIGHS, 256), F32),
-        ],
-        compiler_params=pltpu.CompilerParams(vmem_limit_bytes=48 * MIB),
-    )(wells, classes, edges, class_value)
-
-
-def groups_of(gx, gy):
-    tail = gx == N_GX - 1
-    low = jnp.where(tail, gy % 8, gy)
-    high = jnp.where(tail, gy % 8 + 8, (gy + gx + 1) % GROUPS)
-    return low, high, tail & (gy >= 8)
-
-
-def takers_of(group):
-    out = []
-    for k in range(N_GX - 1):
-        out.append(((k, group), 0))
-        out.append(((k, (group + GROUPS - k - 1) % GROUPS), 1))
-    place = group // 8
-    out.append(((N_GX - 1, group % 8), place))
-    out.append(((N_GX - 1, group % 8 + 8), place))
-    return out
-
-
-ROWS_STEP = 8
-
-
-def zones_kernel(
-    zone_ref,
-    adj_ref,
-    class_ref,
-    class_value_ref,
-    draw_ref,
-    out_ref,
-    adj,
-    sens_ref,
-    owner_of,
-    left,
-    right,
-    acc,
-    send,
-    recv,
-    mine,
-    sem,
-    got_sem,
-    put_sem,
-    adj_sem,
-):
-    me = my_index()
-    gx, gy = lax.axis_index("gx"), lax.axis_index("gy")
-    greet_all(me)
-
-    def back(k):
-        dev = lax.rem(gx + k, N_GX)
+                    sens[2 * h + odd, pl.ds(NZ * n + j, 8, stride=8), :] = both[tile(j)]
+
+
+    seven = pl.ds(0, N_GX - 1)
+    for ref, sems in ((zone_in, zone_sem), (draw_in, draw_sem)):
+        pltpu.make_async_copy(ref.at[seven], ref.at[seven], sems.at[1]).wait()
+        pltpu.make_async_copy(ref.at[seven], ref.at[seven], sems.at[0]).wait()
+
+    inner = lax.broadcasted_iota(jnp.int32, (256, 128), 0).astype(F32).astype(BF16)
+    one, nil = jnp.ones((), BF16), jnp.zeros((), BF16)
+
+    def spread(row, times):
+        return jnp.concatenate([jnp.broadcast_to(row, (16, 128)).astype(BF16)] * times, axis=0)
+
+    per = 2 * NZ // STEP
+
+    def build(i, left, right):
+        o, at = i // per, pl.ds(pl.multiple_of(i % per * STEP, STEP), STEP)
+        zone = zone_in[o, at, :]
+        value = sens[o, at, :] * draw_in[o, at, :].astype(F32)
+        outer = ((zone + 0.5) * (1.0 / INNER)).astype(jnp.int32).astype(F32)
+        place = zone - outer * INNER
+        for r in range(STEP):
+            row = slice(r, r + 1)
+            cols = slice(128 * r, 128 * r + 128)
+            right[:, cols] = jnp.where(inner == spread(outer[row], 16), spread(value[row], 16), nil)
+            left[0:256, cols] = jnp.where(inner == spread(place[row], 16), one, nil)
+            left[256:INNER, cols] = jnp.where(
+                inner[0 : INNER - 256] == spread(place[row] - 256.0, (INNER - 256) // 16), one, nil
+            )
+
+    def add(left, right):
+        for n in range(2):
+            cols = slice(64 * STEP * n, 64 * STEP * n + 64 * STEP)
+            acc[n] += lax.dot_general(
+                left[:, cols], right[:, cols], NT, preferred_element_type=F32
+            )
+
+    steps = N_GX * per
+    acc[...] = jnp.zeros_like(acc)
+    build(0, left_a, right_a)
+
+    def two(i, _):
+        build(2 * i + 1, left_b, right_b)
+        add(left_a, right_a)
+        build(jnp.minimum(2 * i + 2, steps - 1), left_a, right_a)
+        add(left_b, right_b)
+        return 0
+
+    lax.fori_loop(0, steps // 2, two, 0)
+
+    turned = (acc[0] + acc[1]).T
+    for dev in range(DEVICES):
+        send_a[dev % N_GY, dev // N_GY] = turned[2 * dev : 2 * dev + 2, :]
+
+    def row_copy(k):
+        dev = lax.rem(gy + k, N_GY)
         return pltpu.make_async_remote_copy(
-            src_ref=adj_ref.at[dev],
-            dst_ref=adj.at[gx],
-            send_sem=adj_sem.at[0],
-            recv_sem=adj_sem.at[1],
-            device_id=(dev, gy),
+            src_ref=send_a.at[dev],
+            dst_ref=recv_a.at[gy],
+            send_sem=a_sem.at[0],
+            recv_sem=a_sem.at[1],
+            device_id=(gx, dev),
             device_id_type=MESH,
         )
 
+    for k in range(1, N_GY):
+        row_copy(k).start()
+    recv_a[gy] = send_a[gy]
+    rest = pl.ds(0, N_GY - 1)
+    pltpu.make_async_copy(recv_a.at[rest], recv_a.at[rest], a_sem.at[1]).wait()
+    for o in range(N_GX):
+        total = recv_a[0, o]
+        for n in range(1, N_GY):
+            total = total + recv_a[n, o]
+        send_b[o] = total
     for k in range(1, N_GX):
-        back(k).start()
-    adj[gx] = adj_ref[gx]
-    left_half = lax.broadcasted_iota(jnp.int32, (NZ, 128), 1) < HALF
-    owner_of[...] = (
-        (lax.broadcasted_iota(jnp.int32, (TESTS * DEVICES, 128), 0) // TESTS)
-        .astype(F32)
-        .astype(BF16)
-    )
-    acc[...] = jnp.zeros_like(acc)
-    inner = lax.broadcasted_iota(jnp.int32, (256, 128), 0).astype(F32).astype(BF16)
-    sub = lax.broadcasted_iota(jnp.int32, (8, 128), 0) % TESTS
-    conduct = []
-    for x in range(CX):
-        cls = class_ref[NZ * x : NZ * x + NZ, :]
-        value = jnp.zeros((NZ, CY), F32)
-        for k in range(NCLASS):
-            value = jnp.where(cls == k, class_value_ref[k], value)
-        conduct.append(value)
-    seven = pl.ds(0, N_GX - 1)
-    pltpu.make_async_copy(adj.at[seven], adj.at[seven], adj_sem.at[1]).wait()
+        to_column(k, lambda dev: send_b.at[dev], recv_b.at[gx], b_sem).start()
+    recv_b[gx] = send_b[gx]
+    pltpu.make_async_copy(recv_b.at[seven], recv_b.at[seven], b_sem.at[1]).wait()
     for t in range(TESTS):
+        total = (recv_b[t] + recv_b[TESTS + t]).astype(BF16).astype(F32)
         for n in range(2):
-            a, b = adj[t, NZ * n : NZ * n + NZ, :], adj[4 + t, NZ * n : NZ * n + NZ, :]
-            for x, field in (
-                (n, jnp.where(left_half, a, pltpu.roll(b, 64, 1))),
-                (n + 2, jnp.where(left_half, pltpu.roll(a, 64, 1), b)),
-            ):
-                at = slice(NZ * x, NZ * x + NZ)
-                sens_ref[t, at, :] = conduct[x] * draw_ref[t, at, :].astype(F32) * field
-
-    def spread(row, times):
-        return jnp.concatenate([jnp.broadcast_to(row, (16, 128)).astype(BF16)] * times, axis=0)
-
-    def step(i, _):
-        at = pl.ds(pl.multiple_of(i * ROWS_STEP, ROWS_STEP), ROWS_STEP)
-        zone = zone_ref[at, :].astype(F32)
-        owner = ((zone + 0.5) * (1.0 / SHARE)).astype(jnp.int32).astype(F32)
-        place = zone - owner * SHARE
-        values = [sens_ref[t, at, :] for t in range(TESTS)]
-        for r in range(ROWS_STEP):
-            row = slice(r, r + 1)
-            four = jnp.broadcast_to(values[0][row], (8, 128))
-            for t in range(1, TESTS):
-                four = jnp.where(sub == t, jnp.broadcast_to(values[t][row], (8, 128)), four)
-            four = jnp.concatenate([four, four], axis=0).astype(BF16)
-            cols = slice(128 * r, 128 * r + 128)
-            left[:, cols] = jnp.where(
-                owner_of[...] == spread(owner[row], TESTS * DEVICES // 16),
-                jnp.concatenate([four] * (TESTS * DEVICES // 16), axis=0),
-                jnp.zeros((), BF16),
-            )
-            for part in range(SHARE // 256):
-                right[256 * part : 256 * part + 256, cols] = jnp.where(
-                    inner == spread(place[row] - 256.0 * part, 16),
-                    jnp.ones((), BF16),
-                    jnp.zeros((), BF16),
-                )
-        acc[...] += lax.dot_general(left[...], right[...], NT, preferred_element_type=F32)
-        return 0
-
-    lax.fori_loop(0, CX * NZ // ROWS_STEP, step, 0)
-    for dev in range(DEVICES):
-        send[dev] = acc[TESTS * dev : TESTS * dev + TESTS, :]
-
-    send_to_all(me, send, recv, sem.at[0], sem.at[1])
-    pltpu.make_async_copy(adj.at[seven], adj.at[seven], adj_sem.at[0]).wait()
-
-    def add(s, total):
-        for n in range(8):
-            total = total + recv[8 * s + n]
-        return total
-
-    total = lax.fori_loop(0, DEVICES // 8, add, jnp.zeros((TESTS, SHARE), F32))
-    mine[...] = total.astype(BF16).astype(F32)
-
-    group, member = me // MEMBERS, me % MEMBERS
-
-    def put(n, dev, place):
+            mine[t : t + 1, INNER * n : INNER * n + INNER] = total[n : n + 1]
+
+    def put_out(n, dev, place):
         return pltpu.make_async_remote_copy(
             src_ref=mine,
             dst_ref=out_ref.at[place, member],
@@ -686,20 +744,20 @@
             device_id_type=MESH,
         )
 
-    takers = takers_of(group)
     for n, (dev, place) in enumerate(takers):
-        self_here = dev[0] * N_GY + dev[1] == me
-
-        @pl.when(jnp.logical_not(self_here))
+        taker_is_me = dev[0] * N_GY + dev[1] == me
+
+        @pl.when(jnp.logical_not(taker_is_me))
         def _():
-            put(n, dev, place).start()
-
-        @pl.when(self_here)
+            put_out(n, dev, place).start()
+
+        @pl.when(taker_is_me)
         def _():
             out_ref[place, member] = mine[...]
 
-    low, high, _ = groups_of(gx, gy)
-    for place, held in ((0, low), (1, high)):
+    pltpu.make_async_copy(send_a.at[rest], send_a.at[rest], a_sem.at[0]).wait()
+    pltpu.make_async_copy(send_b.at[seven], send_b.at[seven], b_sem.at[0]).wait()
+    for place, held in ((0, low_group), (1, high_group)):
         for m in range(MEMBERS):
 
             @pl.when(held * MEMBERS + m != me)
@@ -712,44 +770,83 @@
 
         @pl.when(dev[0] * N_GY + dev[1] != me)
         def _():
-            put(n, dev, place).wait_send()
-
-
-def zones_call(zone, adjoint, classes, class_value, drawdown):
-    rows = TESTS * DEVICES
-    width = ROWS_STEP * 128
+            put_out(n, dev, place).wait_send()
+
+
+def main_call(cond, source, zone, drawdown):
+    width = STEP * 128
     return pl.pallas_call(
-        zones_kernel,
+        main_kernel,
         out_shape=jax.ShapeDtypeStruct((2, MEMBERS, TESTS, SHARE), F32),
-        in_specs=[VMEM] * 3 + [pl.BlockSpec(memory_space=pltpu.SMEM), VMEM],
+        in_specs=[VMEM] * 4,
         out_specs=VMEM,
         scratch_shapes=[
+            pltpu.VMEM(FIELD, F32),
+            pltpu.VMEM(FIELD, F32),
+            pltpu.VMEM(FIELD, F32),
+            pltpu.VMEM(FIELD, F32),
+            pltpu.VMEM((2,) + FIELD, F32),
+            pltpu.VMEM(FIELD, F32),
+            pltpu.VMEM(FIELD, F32),
+            pltpu.VMEM((XL + 1, YL, NZ, 128), F32),
+            pltpu.VMEM((2, 2 * NZ, 128), F32),
+            pltpu.VMEM((N_GX, 2 * NZ, 128), BF16),
             pltpu.VMEM((N_GX, 2 * NZ, 128), F32),
-            pltpu.VMEM((TESTS, CX * NZ, CY), F32),
-            pltpu.VMEM((rows, 128), BF16),
-            pltpu.VMEM((rows, width), BF16),
-            pltpu.VMEM((SHARE, width), BF16),
-            pltpu.VMEM((rows, SHARE), F32),
-            pltpu.VMEM((DEVICES, TESTS, SHARE), F32),
-            pltpu.VMEM((DEVICES, TESTS, SHARE), F32),
+            pltpu.VMEM((N_GX, 2 * NZ, 128), BF16),
+            pltpu.VMEM((N_GX, 2 * NZ, 128), F32),
+            pltpu.VMEM((INNER, width), BF16),
+            pltpu.VMEM((256, width), BF16),
+            pltpu.VMEM((INNER, width), BF16),
+            pltpu.VMEM((256, width), BF16),
+            pltpu.VMEM((2, INNER, 256), F32),
+            pltpu.VMEM((N_GY, N_GX, 2, INNER), F32),
+            pltpu.VMEM((N_GY, N_GX, 2, INNER), F32),
+            pltpu.VMEM((N_GX, 2, INNER), F32),
+            pltpu.VMEM((N_GX, 2, INNER), F32),
             pltpu.VMEM((TESTS, SHARE), F32),
+            pltpu.SemaphoreType.DMA((2,)),
+            pltpu.SemaphoreType.DMA((2,)),
+            pltpu.SemaphoreType.DMA((2,)),
             pltpu.SemaphoreType.DMA((2,)),
             pltpu.SemaphoreType.DMA((2, MEMBERS)),
             pltpu.SemaphoreType.DMA((16,)),
-            pltpu.SemaphoreType.DMA((2,)),
         ],
         compiler_params=pltpu.CompilerParams(
-            collective_id=2, has_side_effects=True, vmem_limit_bytes=48 * MIB
+            collective_id=1, has_side_effects=True, vmem_limit_bytes=48 * MIB
         ),
-    )(zone, adjoint, classes, class_value, drawdown)
-
-
-BLOCK = 1024
-STRIP = 64
-
-
-def cov_kernel(diag_ref, pts_ref, sums_ref, out_ref, z_ref, rows_ref, tile_ref):
-    blocks = GROUP // BLOCK
+    )(cond, source, zone, drawdown)
+
+
+ROWS, COLS, STRIP = 1024, 512, 256
+TERMS = 128
+
+
+def pieces(value):
+    out = []
+    for _ in range(3):
+        piece = value.astype(BF16).astype(F32)
+        out.append(piece)
+        value = value - piece
+    return out
+
+
+def terms(pts, as_rows):
+    sub = lax.broadcasted_iota(jnp.int32, pts.shape, 0)
+    norm = pieces(jnp.broadcast_to(jnp.sum(pts * pts, axis=0, keepdims=True), pts.shape))
+    parts = pieces(pts)
+    first = 0 if as_rows else 3
+    rest = jnp.where((sub < 6) & ((sub >= 3) if as_rows else (sub < 3)), 1.0, 0.0)
+    for n in range(3):
+        rest = jnp.where(sub == first + n, norm[n], rest)
+    blocks = [
+        -2.0 * parts[i] if as_rows else parts[j] for i in range(3) for j in range(3)
+    ]
+    return jnp.concatenate(blocks + [rest], axis=0)
+
+
+def cov_kernel(
+    diag_ref, pts_ref, sums_ref, out_ref, z_ref, z_turned, row_terms, col_terms, near, total, ta, tb
+):
     diag = diag_ref[0]
     out_ref[...] = jnp.zeros_like(out_ref)
     for g in range(2):
@@ -757,51 +854,77 @@
             both = jnp.concatenate([sums_ref[g, m], jnp.zeros((TESTS, SHARE), F32)], axis=0)
             z_ref[g, :, SHARE * m : SHARE * m + SHARE] = both.astype(BF16)
 
-    def tile(cg, c):
-        cols = [pts_ref[cg, k : k + 1, pl.ds(pl.multiple_of(c * BLOCK, BLOCK), BLOCK)] for k in range(3)]
-
-        def body(i, _):
-            r0 = pl.multiple_of(i * STRIP, STRIP)
-            squared = None
-            for k in range(3):
-                near = jnp.concatenate([rows_ref[k, pl.ds(r0, STRIP), :]] * (BLOCK // 128), axis=1)
-                gap = near - cols[k]
-                squared = gap * gap if squared is None else squared + gap * gap
-            squared = jnp.maximum(squared, 1e-30)
-            dist = squared * lax.rsqrt(squared)
-            tile_ref[pl.ds(r0, STRIP), :] = jnp.exp2(-dist).astype(BF16)
-            return 0
-
-        lax.fori_loop(0, BLOCK // STRIP, body, 0, unroll=True)
-
     def phase(rg, _):
         cg = jnp.where(diag == 1, rg, 1)
+        for i in range(GROUP // ROWS):
+            at = slice(ROWS * i, ROWS * i + ROWS)
+            row_terms[0:80, at] = terms(pts_ref[rg, :, at], True)
+            row_terms[80:TERMS, at] = jnp.zeros((TERMS - 80, ROWS), F32)
+            col_terms[0:80, at] = terms(pts_ref[cg, :, at], False).astype(BF16)
+            col_terms[80:TERMS, at] = jnp.zeros((TERMS - 80, ROWS), BF16)
+            wide = jnp.concatenate(
+                [z_ref[cg, :, at].astype(F32), jnp.zeros((120, ROWS), F32)], axis=0
+            )
+            z_turned[at, :] = wide.T.astype(BF16)
 
         def row_block(r, _):
-            rs = pl.ds(pl.multiple_of(r * BLOCK, BLOCK), BLOCK)
-            for k in range(3):
-                rows_ref[k] = jnp.broadcast_to(pts_ref[rg, k : k + 1, rs], (128, BLOCK)).T
-            near = z_ref[rg, :, rs]
-
-            def col_block(c, acc):
-                tile(cg, c)
-                cs = pl.ds(pl.multiple_of(c * BLOCK, BLOCK), BLOCK)
-                acc = acc + lax.dot_general(
-                    z_ref[cg, :, cs], tile_ref[...], NT, preferred_element_type=F32
+            rs = pl.ds(pl.multiple_of(r * ROWS, ROWS), ROWS)
+            near[...] = row_terms[:, rs].T.astype(BF16)
+            total[...] = jnp.zeros_like(total)
+            z_row = z_ref[rg, :, rs]
+
+            def at_cols(c):
+                return pl.ds(pl.multiple_of(c * COLS, COLS), COLS)
+
+            def tile(c, out):
+                cols = col_terms[:, at_cols(c)]
+                for i in range(ROWS // STRIP):
+                    at = slice(STRIP * i, STRIP * i + STRIP)
+                    squared = jnp.dot(near[at, :], cols, preferred_element_type=F32)
+                    squared = jnp.maximum(squared, 1e-30)
+                    out[at, :] = jnp.exp2(squared * (-lax.rsqrt(squared))).astype(BF16)
+
+            def for_rows(c, held):
+                total[...] += jnp.dot(
+                    held[...], z_turned[at_cols(c), :], preferred_element_type=F32
                 )
 
-                @pl.when(jnp.logical_not((diag == 1) & (c == r)))
-                def _():
-                    out_ref[cg, :, cs] += jnp.dot(near, tile_ref[...], preferred_element_type=F32)
-
-                return acc
-
-            first = jnp.where(diag == 1, r, 0)
-            acc = lax.fori_loop(first, blocks, col_block, jnp.zeros((8, BLOCK), F32))
-            out_ref[rg, :, rs] += acc
+            def both_ways(c, held):
+                out_ref[cg, :, at_cols(c)] += jnp.dot(
+                    z_row, held[...], preferred_element_type=F32
+                )
+                for_rows(c, held)
+
+            last = GROUP // COLS // 2 - 1
+            first = jnp.where(diag == 1, r + 1, 0)
+
+            @pl.when(diag == 1)
+            def _():
+                tile(2 * r, ta)
+                tile(2 * r + 1, tb)
+                for_rows(2 * r, ta)
+                for_rows(2 * r + 1, tb)
+
+            @pl.when(first <= last)
+            def _():
+                tile(2 * first, ta)
+
+                def two(p, _):
+                    tile(2 * p + 1, tb)
+                    both_ways(2 * p, ta)
+                    tile(2 * p + 2, ta)
+                    both_ways(2 * p + 1, tb)
+                    return 0
+
+                lax.fori_loop(first, last, two, 0)
+                tile(2 * last + 1, tb)
+                both_ways(2 * last, ta)
+                both_ways(2 * last + 1, tb)
+
+            out_ref[rg, :, rs] += total[...].T[0:8]
             return 0
 
-        lax.fori_loop(0, blocks, row_block, 0)
+        lax.fori_loop(0, GROUP // ROWS, row_block, 0)
         return 0
 
     lax.fori_loop(0, 1 + diag, phase, 0)
@@ -815,8 +938,13 @@
         out_specs=VMEM,
         scratch_shapes=[
             pltpu.VMEM((2, 8, GROUP), BF16),
-            pltpu.VMEM((3, BLOCK, 128), F32),
-            pltpu.VMEM((BLOCK, BLOCK), BF16),
+            pltpu.VMEM((GROUP, 128), BF16),
+            pltpu.VMEM((TERMS, GROUP), F32),
+            pltpu.VMEM((TERMS, GROUP), BF16),
+            pltpu.VMEM((ROWS, TERMS), BF16),
+            pltpu.VMEM((ROWS, 128), F32),
+            pltpu.VMEM((ROWS, COLS), BF16),
+            pltpu.VMEM((ROWS, COLS), BF16),
         ],
         compiler_params=pltpu.CompilerParams(vmem_limit_bytes=48 * MIB),
     )(diag, pts, sums)
@@ -909,7 +1037,7 @@
             pltpu.SemaphoreType.DMA((GROUPS,)),
         ],
         compiler_params=pltpu.CompilerParams(
-            collective_id=3, has_side_effects=True, vmem_limit_bytes=32 * MIB
+            collective_id=2, has_side_effects=True, vmem_limit_bytes=32 * MIB
         ),
     )(parts)
 
@@ -921,18 +1049,15 @@
     low, high, diag = groups_of(gx, gy)
     pts = jnp.stack(
         [lax.dynamic_slice_in_dim(centroid, held * GROUP, GROUP, 1) for held in (low, high)]
-    ) * (LOG2E / corr_len)
+    )
+    pts = jnp.pad((pts - 0.5) * (LOG2E / corr_len), ((0, 0), (0, 5), (0, 0)))
     wells, classes, edges = share_call(
         well_cell[None], well_test[None], well_value[None], cond_class
     )
-    adjoint = sweeps_call(wells, classes, edges, class_value)
+    cond, source = source_call(wells, classes, edges, class_value)
     rows = CX * NZ
-    sums = zones_call(
-        zone_id.reshape(rows, CY),
-        adjoint,
-        cond_class.reshape(rows, CY),
-        class_value,
-        drawdown.reshape(TESTS, rows, CY),
+    sums = main_call(
+        cond, source, zone_id.reshape(rows, CY), drawdown.reshape(TESTS, rows, CY)
     )
     parts = cov_call(diag.astype(jnp.int32)[None], pts, sums)
     return reduce_call(parts)

time: 252 us -> 213 us (0.85)
  Pallas kernels: 246 us -> 208 us
    pallas_call x1, Pallas kernels: 91.6 us -> 68.7 us  [cov_call(): pl.pallas_call(cov_kernel, out_shape=jax.ShapeDtypeStruct((2, 8, GROUP),...]
    pallas_call x2, Pallas kernels: 101 us -> 86 us  [the longest x1 76.5 us: main_call(): pl.pallas_call(main_kernel, out_shape=jax.ShapeDtypeStruct((2, MEMBERS, T...]
where the time goes in v3:
time: 213 us
  Pallas kernels  208 us (98%)
  local copies, waits for them, and re-layouts  4.61 us (2%)
    pallas_call x1, Pallas kernels, main_call(): pl.pallas_call(main_kernel, out_shape=jax.ShapeDtypeStruct((2, MEMBERS, T...  76.5 us
    pallas_call x1, Pallas kernels, cov_call(): pl.pallas_call(cov_kernel, out_shape=jax.ShapeDtypeStruct((2, 8, GROUP),...  68.7 us
    pallas_call x1, Pallas kernels, reduce_call(): pl.pallas_call(reduce_kernel, out_shape=jax.ShapeDtypeStruct((TESTS, SHAR...  26.8 us
    pallas_call x1, Pallas kernels, share_call(): pl.pallas_call(share_kernel, out_shape=(jax.ShapeDtypeStruct((DEVICES, 4,...  26.6 us
    pallas_call x1, Pallas kernels, source_call(): pl.pallas_call(source_kernel, out_shape=(jax.ShapeDtypeStruct(FIELD, F32)...  9.45 us

profile of v3, /device:TPU:1, one launch (start us, length us, event | category | flops | bytes accessed | tf_op | source)
XLA Modules:
  0.0 212.9 jit_solution(13902537462118220174)
XLA Ops:
  0.0 0.0 copy-start
  0.0 0.0 copy-start.1
  0.0 0.0 copy-start.6
  0.1 1.0 dynamic-slice_bitcast_fusion.1
  1.1 0.1 fusion
  1.2 0.0 copy-start.2
  1.2 0.9 copy-done.2
  2.1 0.0 copy-start.3
  2.1 0.7 copy-done.3
  2.8 0.0 copy-start.4
  2.8 0.7 copy-done.4
  3.5 0.0 copy-start.5
  3.5 0.7 copy-done.5
  4.2 26.6 %shard_map.82 = (f32[128,4,128]{2,1,0:T(4,128)S(1)}, bf16[8,256,128]{2,1,0:T(8,128)(2,1)S(1)}, bf16[8,32,128]{2,1,0:T(8,128)(2,1)S(1)}) custom-call(s32[1,512]{1,0:T(1,128)S(1)} %bitcast.12, s32[1,512]{1,0:T(1,128)S(1)} %bitcast.13, f32[1,512]{1,0:T(1,128)S(1)} %bitcast.14, s32[4,64,128]{2,1,0:T(8,128)S(1)} %copy-done.2), custom_call_target="tpu_custom_call" | custom-call | tf_op jit(solution)/shard_map/pallas_call | solution.py:240
  30.7 0.0 copy-done.6
  30.7 9.5 %shard_map.83 = (f32[8,3,64,128]{3,2,1,0:T(8,128)S(1)}, f32[8,3,64,128]{3,2,1,0:T(8,128)S(1)}) custom-call(f32[128,4,128]{2,1,0:T(4,128)S(1)} %get-tuple-element.10.wells_ref, bf16[8,256,128]{2,1,0:T(8,128)(2,1)S(1)} %get-tuple-element.11.cls_ref, bf16[8,32,128]{2,1,0:T(8,128)(2,1)S(1)} %get-tuple-element.12.edge_ref, f32[16]{0:T(128)S(1)} %copy-done.6), custom_call_target="tpu_custom_call" | custom-call | tf_op jit(solution)/shard_map/pallas_call | solution.py:366
  40.2 0.0 copy-done
  40.2 0.0 copy-done.1
  40.2 76.5 %shard_map.84.sums_ref = f32[2,8,4,768]{3,2,1,0:T(4,128)S(1)} custom-call(f32[8,3,64,128]{3,2,1,0:T(8,128)S(1)} %get-tuple-element.13.cond, f32[8,3,64,128]{3,2,1,0:T(8,128)S(1)} %get-tuple-element.14.src_ref, s32[256,128]{1,0:T(8,128)S(1)} %bitcast.11, bf16[4,256,128]{2,1,0:T(8,128)(2,1)S(1)} %bitcast.10), custom_call_target="tpu_custom_call" | custom-call | tf_op jit(solution)/shard_map/pallas_call | solution.py:778
  116.7 68.7 %shard_map.85.part_ref = f32[2,8,6144]{2,1,0:T(8,128)S(1)} custom-call(s32[1]{0:T(128)} %bitcast.diag_ref, f32[2,8,6144]{2,1,0:T(8,128)S(1)} %pad.4.pts_ref, f32[2,8,4,768]{3,2,1,0:T(4,128)S(1)} %shard_map.84.sums_ref), custom_call_target="tpu_custom_call" | custom-call | tf_op jit(solution)/shard_map/pallas_call | solution.py:934
  185.5 26.8 %shard_map.86 = bf16[4,768]{1,0:T(4,128)(2,1)S(1)} custom-call(f32[2,8,6144]{2,1,0:T(8,128)S(1)} %shard_map.85.part_ref), custom_call_target="tpu_custom_call" | custom-call | tf_op jit(solution)/shard_map/pallas_call | solution.py:1028
  212.3 0.6 copy.10
  (1 shorter events, 0.0 us)
Async XLA Ops:
  0.0 40.2 %copy-start = (bf16[4,4,64,128]{3,2,1,0:T(8,128)(2,1)S(1)}, bf16[4,4,64,128]{3,2,1,0:T(8,128)(2,1)}, u32[]{:S(2)}) copy-start(bf16[4,4,64,128]{3,2,1,0:T(8,128)(2,1)} %param.14) | copy-start | bytes 786436
  0.0 40.2 %copy-start.1 = (s32[4,64,128]{2,1,0:T(8,128)S(1)}, s32[4,64,128]{2,1,0:T(8,128)}, u32[]{:S(2)}) copy-start(s32[4,64,128]{2,1,0:T(8,128)} %param.13) | copy-start | bytes 393220
  0.0 30.7 %copy-start.6 = (f32[16]{0:T(128)S(1)}, f32[16]{0:T(128)}, u32[]{:S(2)}) copy-start(f32[16]{0:T(128)} %class_value_ref.1) | copy-start | bytes 196
  1.2 0.9 copy-start.2
  2.1 0.7 copy-start.3
  2.8 0.7 copy-start.4
  3.5 0.7 copy-start.5

commit v4 on v3

--- a/solution.py
+++ b/solution.py
@@ -395,7 +395,6 @@
     return out
 
 
-STEP = 16
 INNER = SHARE // 2
 
 
@@ -418,10 +417,6 @@
     zone_in,
     draw_in,
     sens,
-    left_a,
-    right_a,
-    left_b,
-    right_b,
     acc,
     send_a,
     recv_a,
@@ -663,44 +658,41 @@
     def spread(row, times):
         return jnp.concatenate([jnp.broadcast_to(row, (16, 128)).astype(BF16)] * times, axis=0)
 
-    per = 2 * NZ // STEP
-
-    def build(i, left, right):
-        o, at = i // per, pl.ds(pl.multiple_of(i % per * STEP, STEP), STEP)
-        zone = zone_in[o, at, :]
-        value = sens[o, at, :] * draw_in[o, at, :].astype(F32)
+    def step(o, _):
+        zone = zone_in[o]
+        value = sens[o] * draw_in[o].astype(F32)
         outer = ((zone + 0.5) * (1.0 / INNER)).astype(jnp.int32).astype(F32)
         place = zone - outer * INNER
-        for r in range(STEP):
+        left, right = [], []
+        for r in range(2 * NZ):
             row = slice(r, r + 1)
-            cols = slice(128 * r, 128 * r + 128)
-            right[:, cols] = jnp.where(inner == spread(outer[row], 16), spread(value[row], 16), nil)
-            left[0:256, cols] = jnp.where(inner == spread(place[row], 16), one, nil)
-            left[256:INNER, cols] = jnp.where(
-                inner[0 : INNER - 256] == spread(place[row] - 256.0, (INNER - 256) // 16), one, nil
+            right.append(jnp.where(inner == spread(outer[row], 16), spread(value[row], 16), nil))
+            left.append(
+                jnp.concatenate(
+                    [
+                        jnp.where(inner == spread(place[row], 16), one, nil),
+                        jnp.where(
+                            inner[0 : INNER - 256]
+                            == spread(place[row] - 256.0, (INNER - 256) // 16),
+                            one,
+                            nil,
+                        ),
+                    ],
+                    axis=0,
+                )
             )
-
-    def add(left, right):
-        for n in range(2):
-            cols = slice(64 * STEP * n, 64 * STEP * n + 64 * STEP)
-            acc[n] += lax.dot_general(
-                left[:, cols], right[:, cols], NT, preferred_element_type=F32
-            )
-
-    steps = N_GX * per
+        acc[...] += lax.dot_general(
+            jnp.concatenate(left, axis=1),
+            jnp.concatenate(right, axis=1),
+            NT,
+            preferred_element_type=F32,
+        )
+        return 0
+
     acc[...] = jnp.zeros_like(acc)
-    build(0, left_a, right_a)
-
-    def two(i, _):
-        build(2 * i + 1, left_b, right_b)
-        add(left_a, right_a)
-        build(jnp.minimum(2 * i + 2, steps - 1), left_a, right_a)
-        add(left_b, right_b)
-        return 0
-
-    lax.fori_loop(0, steps // 2, two, 0)
-
-    turned = (acc[0] + acc[1]).T
+    lax.fori_loop(0, N_GX, step, 0)
+
+    turned = acc[...].T
     for dev in range(DEVICES):
         send_a[dev % N_GY, dev // N_GY] = turned[2 * dev : 2 * dev + 2, :]
 
@@ -774,7 +766,6 @@
 
 
 def main_call(cond, source, zone, drawdown):
-    width = STEP * 128
     return pl.pallas_call(
         main_kernel,
         out_shape=jax.ShapeDtypeStruct((2, MEMBERS, TESTS, SHARE), F32),
@@ -794,11 +785,7 @@
             pltpu.VMEM((N_GX, 2 * NZ, 128), F32),
             pltpu.VMEM((N_GX, 2 * NZ, 128), BF16),
             pltpu.VMEM((N_GX, 2 * NZ, 128), F32),
-            pltpu.VMEM((INNER, width), BF16),
-            pltpu.VMEM((256, width), BF16),
-            pltpu.VMEM((INNER, width), BF16),
-            pltpu.VMEM((256, width), BF16),
-            pltpu.VMEM((2, INNER, 256), F32),
+            pltpu.VMEM((INNER, 256), F32),
             pltpu.VMEM((N_GY, N_GX, 2, INNER), F32),
             pltpu.VMEM((N_GY, N_GX, 2, INNER), F32),
             pltpu.VMEM((N_GX, 2, INNER), F32),
@@ -817,7 +804,7 @@
     )(cond, source, zone, drawdown)
 
 
-ROWS, COLS, STRIP = 1024, 512, 256
+ROWS, COLS = 1024, 512
 TERMS = 128
 
 
@@ -845,7 +832,7 @@
 
 
 def cov_kernel(
-    diag_ref, pts_ref, sums_ref, out_ref, z_ref, z_turned, row_terms, col_terms, near, total, ta, tb
+    diag_ref, pts_ref, sums_ref, out_ref, z_ref, z_turned, row_terms, col_terms, near, total
 ):
     diag = diag_ref[0]
     out_ref[...] = jnp.zeros_like(out_ref)
@@ -876,51 +863,40 @@
             def at_cols(c):
                 return pl.ds(pl.multiple_of(c * COLS, COLS), COLS)
 
-            def tile(c, out):
-                cols = col_terms[:, at_cols(c)]
-                for i in range(ROWS // STRIP):
-                    at = slice(STRIP * i, STRIP * i + STRIP)
-                    squared = jnp.dot(near[at, :], cols, preferred_element_type=F32)
-                    squared = jnp.maximum(squared, 1e-30)
-                    out[at, :] = jnp.exp2(squared * (-lax.rsqrt(squared))).astype(BF16)
-
-            def for_rows(c, held):
-                total[...] += jnp.dot(
-                    held[...], z_turned[at_cols(c), :], preferred_element_type=F32
+            def tile(c, rows):
+                squared = jnp.dot(
+                    near[rows, :], col_terms[:, at_cols(c)], preferred_element_type=F32
                 )
-
-            def both_ways(c, held):
+                squared = jnp.maximum(squared, 1e-30)
+                return jnp.exp2(squared * (-lax.rsqrt(squared))).astype(BF16)
+
+            def for_rows(c, rows, held):
+                total[rows, :] += jnp.dot(
+                    held, z_turned[at_cols(c), :], preferred_element_type=F32
+                )
+
+            def for_cols(c, weights, held):
                 out_ref[cg, :, at_cols(c)] += jnp.dot(
-                    z_row, held[...], preferred_element_type=F32
+                    weights, held, preferred_element_type=F32
                 )
-                for_rows(c, held)
-
-            last = GROUP // COLS // 2 - 1
-            first = jnp.where(diag == 1, r + 1, 0)
+
+            every, lower = slice(0, ROWS), slice(COLS, ROWS)
 
             @pl.when(diag == 1)
             def _():
-                tile(2 * r, ta)
-                tile(2 * r + 1, tb)
-                for_rows(2 * r, ta)
-                for_rows(2 * r + 1, tb)
-
-            @pl.when(first <= last)
-            def _():
-                tile(2 * first, ta)
-
-                def two(p, _):
-                    tile(2 * p + 1, tb)
-                    both_ways(2 * p, ta)
-                    tile(2 * p + 2, ta)
-                    both_ways(2 * p + 1, tb)
-                    return 0
-
-                lax.fori_loop(first, last, two, 0)
-                tile(2 * last + 1, tb)
-                both_ways(2 * last, ta)
-                both_ways(2 * last + 1, tb)
-
+                held = tile(2 * r, every)
+                for_rows(2 * r, every, held)
+                for_cols(2 * r, z_row[:, COLS:], held[COLS:])
+                for_rows(2 * r + 1, lower, tile(2 * r + 1, lower))
+
+            def two(p, _):
+                for c in (2 * p, 2 * p + 1):
+                    held = tile(c, every)
+                    for_rows(c, every, held)
+                    for_cols(c, z_row, held)
+                return 0
+
+            lax.fori_loop(jnp.where(diag == 1, r + 1, 0), GROUP // ROWS, two, 0)
             out_ref[rg, :, rs] += total[...].T[0:8]
             return 0
 
@@ -943,8 +919,6 @@
             pltpu.VMEM((TERMS, GROUP), BF16),
             pltpu.VMEM((ROWS, TERMS), BF16),
             pltpu.VMEM((ROWS, 128), F32),
-            pltpu.VMEM((ROWS, COLS), BF16),
-            pltpu.VMEM((ROWS, COLS), BF16),
         ],
         compiler_params=pltpu.CompilerParams(vmem_limit_bytes=48 * MIB),
     )(diag, pts, sums)

time: 213 us -> 185 us (0.87)
  Pallas kernels: 208 us -> 180 us
    pallas_call x1, Pallas kernels: 76.5 us -> 62.9 us  [main_call(): pl.pallas_call(main_kernel, out_shape=jax.ShapeDtypeStruct((2, MEMBERS, T...]
    pallas_call x1, Pallas kernels: 26.8 us -> 20.1 us  [reduce_call(): pl.pallas_call(reduce_kernel, out_shape=jax.ShapeDtypeStruct((TESTS, SHAR...]
    pallas_call x1, Pallas kernels: 68.7 us -> 62.4 us  [cov_call(): pl.pallas_call(cov_kernel, out_shape=jax.ShapeDtypeStruct((2, 8, GROUP),...]
where the time goes in v4:
time: 185 us; the launch traced here: 184 us
  Pallas kernels  180 us (97%)
  local copies, waits for them, and re-layouts  4.61 us (2%)
    pallas_call x1, Pallas kernels, main_call(): pl.pallas_call(main_kernel, out_shape=jax.ShapeDtypeStruct((2, MEMBERS, T...  62.9 us
    pallas_call x1, Pallas kernels, cov_call(): pl.pallas_call(cov_kernel, out_shape=jax.ShapeDtypeStruct((2, 8, GROUP),...  62.4 us
    pallas_call x1, Pallas kernels, share_call(): pl.pallas_call(share_kernel, out_shape=(jax.ShapeDtypeStruct((DEVICES, 4,...  26.6 us
    pallas_call x1, Pallas kernels, reduce_call(): pl.pallas_call(reduce_kernel, out_shape=jax.ShapeDtypeStruct((TESTS, SHAR...  20.1 us
    pallas_call x1, Pallas kernels, source_call(): pl.pallas_call(source_kernel, out_shape=(jax.ShapeDtypeStruct(FIELD, F32)...  7.63 us

profile of v4, /device:TPU:1, one launch (start us, length us, event | category | flops | bytes accessed | tf_op | source)
XLA Modules:
  0.0 184.4 jit_solution(3891724599548549982)
XLA Ops:
  0.0 0.0 copy-start
  0.0 0.0 copy-start.1
  0.0 0.0 copy-start.6
  0.1 1.0 dynamic-slice_bitcast_fusion.1
  1.1 0.1 fusion
  1.2 0.0 copy-start.2
  1.2 0.9 copy-done.2
  2.1 0.0 copy-start.3
  2.1 0.7 copy-done.3
  2.8 0.0 copy-start.4
  2.8 0.7 copy-done.4
  3.5 0.0 copy-start.5
  3.5 0.7 copy-done.5
  4.2 26.6 %shard_map.82 = (f32[128,4,128]{2,1,0:T(4,128)S(1)}, bf16[8,256,128]{2,1,0:T(8,128)(2,1)S(1)}, bf16[8,32,128]{2,1,0:T(8,128)(2,1)S(1)}) custom-call(s32[1,512]{1,0:T(1,128)S(1)} %bitcast.12, s32[1,512]{1,0:T(1,128)S(1)} %bitcast.13, f32[1,512]{1,0:T(1,128)S(1)} %bitcast.14, s32[4,64,128]{2,1,0:T(8,128)S(1)} %copy-done.2), custom_call_target="tpu_custom_call" | custom-call | tf_op jit(solution)/shard_map/pallas_call | solution.py:240
  30.7 0.0 copy-done.6
  30.7 7.6 %shard_map.83 = (f32[8,3,64,128]{3,2,1,0:T(8,128)S(1)}, f32[8,3,64,128]{3,2,1,0:T(8,128)S(1)}) custom-call(f32[128,4,128]{2,1,0:T(4,128)S(1)} %get-tuple-element.10.wells_ref, bf16[8,256,128]{2,1,0:T(8,128)(2,1)S(1)} %get-tuple-element.11.cls_ref, bf16[8,32,128]{2,1,0:T(8,128)(2,1)S(1)} %get-tuple-element.12.edge_ref, f32[16]{0:T(128)S(1)} %copy-done.6), custom_call_target="tpu_custom_call" | custom-call | tf_op jit(solution)/shard_map/pallas_call | solution.py:366
  38.4 0.0 copy-done
  38.4 0.0 copy-done.1
  38.4 62.9 %shard_map.84.sums_ref = f32[2,8,4,768]{3,2,1,0:T(4,128)S(1)} custom-call(f32[8,3,64,128]{3,2,1,0:T(8,128)S(1)} %get-tuple-element.13.cond, f32[8,3,64,128]{3,2,1,0:T(8,128)S(1)} %get-tuple-element.14.src_ref, s32[256,128]{1,0:T(8,128)S(1)} %bitcast.11, bf16[4,256,128]{2,1,0:T(8,128)(2,1)S(1)} %bitcast.10), custom_call_target="tpu_custom_call" | custom-call | tf_op jit(solution)/shard_map/pallas_call | solution.py:769
  101.3 62.4 %shard_map.85.part_ref = f32[2,8,6144]{2,1,0:T(8,128)S(1)} custom-call(s32[1]{0:T(128)} %bitcast.diag_ref, f32[2,8,6144]{2,1,0:T(8,128)S(1)} %pad.4.pts_ref, f32[2,8,4,768]{3,2,1,0:T(4,128)S(1)} %shard_map.84.sums_ref), custom_call_target="tpu_custom_call" | custom-call | tf_op jit(solution)/shard_map/pallas_call | solution.py:910
  163.7 20.1 %shard_map.86 = bf16[4,768]{1,0:T(4,128)(2,1)S(1)} custom-call(f32[2,8,6144]{2,1,0:T(8,128)S(1)} %shard_map.85.part_ref), custom_call_target="tpu_custom_call" | custom-call | tf_op jit(solution)/shard_map/pallas_call | solution.py:1002
  183.8 0.6 copy.10
  (1 shorter events, 0.0 us)
Async XLA Ops:
  0.0 38.4 %copy-start = (bf16[4,4,64,128]{3,2,1,0:T(8,128)(2,1)S(1)}, bf16[4,4,64,128]{3,2,1,0:T(8,128)(2,1)}, u32[]{:S(2)}) copy-start(bf16[4,4,64,128]{3,2,1,0:T(8,128)(2,1)} %param.14) | copy-start | bytes 786436
  0.0 38.4 %copy-start.1 = (s32[4,64,128]{2,1,0:T(8,128)S(1)}, s32[4,64,128]{2,1,0:T(8,128)}, u32[]{:S(2)}) copy-start(s32[4,64,128]{2,1,0:T(8,128)} %param.13) | copy-start | bytes 393220
  0.0 30.7 %copy-start.6 = (f32[16]{0:T(128)S(1)}, f32[16]{0:T(128)}, u32[]{:S(2)}) copy-start(f32[16]{0:T(128)} %class_value_ref.1) | copy-start | bytes 196
  1.2 0.9 copy-start.2
  2.1 0.7 copy-start.3
  2.8 0.7 copy-start.4
  3.5 0.7 copy-start.5

commit v5 on v4

--- a/solution.py
+++ b/solution.py
@@ -31,6 +31,7 @@
 XL, YL = 8, 3
 HIGHS = 4 * YL * NZ
 SLOTS = 16 * CAP
+FIELD = (XL, YL, NZ, 128)
 
 storage = 0.02
 lam_low = 0.02
@@ -67,36 +68,22 @@
     pl.semaphore_wait(barrier, len(devs))
 
 
-def greet_all(me):
-    barrier = pltpu.get_barrier_semaphore()
-
-    def each(k, _):
-        dev = lax.rem(me + k, DEVICES)
-        pl.semaphore_signal(barrier, inc=1, device_id=coords(dev), device_id_type=MESH)
+def for_others(act):
+    gx, gy = lax.axis_index("gx"), lax.axis_index("gy")
+    for b in range(1, N_GY):
+        act((gx, lax.rem(gy + b, N_GY)))
+
+    def each(a, _):
+        other = lax.rem(gx + a, N_GX)
+        for b in range(N_GY):
+            act((other, lax.rem(gy + b, N_GY)))
         return 0
 
-    lax.fori_loop(1, DEVICES, each, 0)
-    pl.semaphore_wait(barrier, DEVICES - 1)
-
-
-def send_to_all(me, send, recv, send_sem, recv_sem):
-    def each(k, _):
-        dev = lax.rem(me + k, DEVICES)
-        pltpu.make_async_remote_copy(
-            src_ref=send.at[dev],
-            dst_ref=recv.at[me],
-            send_sem=send_sem,
-            recv_sem=recv_sem,
-            device_id=coords(dev),
-            device_id_type=MESH,
-        ).start()
-        return 0
-
-    lax.fori_loop(1, DEVICES, each, 0)
-    recv[me] = send[me]
-    rest = pl.ds(0, DEVICES - 1)
-    pltpu.make_async_copy(recv.at[rest], recv.at[rest], recv_sem).wait()
-    pltpu.make_async_copy(send.at[rest], send.at[rest], send_sem).wait()
+    lax.fori_loop(1, N_GX, each, 0)
+
+
+def tile(j):
+    return slice(8 * j, 8 * j + 8)
 
 
 def share_kernel(
@@ -104,9 +91,12 @@
     test_ref,
     value_ref,
     class_ref,
+    class_value_ref,
     wells_ref,
+    cond,
     cls_ref,
     edge_ref,
+    plane,
     rows,
     send,
     mine,
@@ -117,6 +107,11 @@
 ):
     me = my_index()
     gx, gy = lax.axis_index("gx"), lax.axis_index("gy")
+    edge_ref[...] = jnp.zeros_like(edge_ref)
+    barrier = pltpu.get_barrier_semaphore()
+    for_others(
+        lambda dev: pl.semaphore_signal(barrier, inc=1, device_id=dev, device_id_type=MESH)
+    )
     lane = lax.broadcasted_iota(jnp.int32, (32, 128), 1)
     classes = class_ref[...].reshape(CX * NZ, CY).astype(F32)
     mine[...] = classes.astype(BF16)
@@ -126,7 +121,6 @@
             here = (lane >= RIM * g) & (lane < RIM * g + RIM)
             pack = jnp.where(here, roll_to(classes[32 * g : 32 * g + 32], RIM * g - first), pack)
         edges[side] = pack.astype(BF16)
-    edge_ref[...] = jnp.zeros_like(edge_ref)
 
     cell, test, value = cell_ref[...], test_ref[...], value_ref[...]
     n_rows = 2 * cell.shape[1]
@@ -179,7 +173,7 @@
         for k in range(4):
             send[dev, k : k + 1, :] = rows[k, dev : dev + 1, :]
 
-    greet_all(me)
+    pl.semaphore_wait(barrier, DEVICES - 1)
 
     def cls_copy(k):
         return pltpu.make_async_remote_copy(
@@ -215,65 +209,26 @@
             edge_copy(1, k).start()
 
     cls_ref[gx] = mine[...]
-    send_to_all(me, send, wells_ref, wells_sem.at[0], wells_sem.at[1])
+
+    def send_rows(dev):
+        pltpu.make_async_remote_copy(
+            src_ref=send.at[dev[0] * N_GY + dev[1]],
+            dst_ref=wells_ref.at[me],
+            send_sem=wells_sem.at[0],
+            recv_sem=wells_sem.at[1],
+            device_id=dev,
+            device_id_type=MESH,
+        ).start()
+
+    for_others(send_rows)
+    wells_ref[me] = send[me]
     seven = pl.ds(0, N_GX - 1)
     pltpu.make_async_copy(cls_ref.at[seven], cls_ref.at[seven], cls_sem.at[1]).wait()
-    pltpu.make_async_copy(cls_ref.at[seven], cls_ref.at[seven], cls_sem.at[0]).wait()
-    four = pl.ds(0, 4)
-
-    @pl.when(gy > 0)
-    def _():
-        pltpu.make_async_copy(edge_ref.at[four], edge_ref.at[four], edge_sem.at[0]).wait()
-
-    @pl.when(gy < N_GY - 1)
-    def _():
-        pltpu.make_async_copy(edge_ref.at[four], edge_ref.at[four], edge_sem.at[1]).wait()
-
-    upper = gx >= 4
-
-    @pl.when((upper & (gy < N_GY - 1)) | (jnp.logical_not(upper) & (gy > 0)))
+    half = gx // 4
+
+    @pl.when(((half == 1) & (gy < N_GY - 1)) | ((half == 0) & (gy > 0)))
     def _():
         pltpu.make_async_copy(edge_ref, edge_ref, edge_sem.at[2]).wait()
-
-
-def share_call(cell, test, value, classes):
-    return pl.pallas_call(
-        share_kernel,
-        out_shape=(
-            jax.ShapeDtypeStruct((DEVICES, 4, 128), F32),
-            jax.ShapeDtypeStruct((N_GX, CX * NZ, CY), BF16),
-            jax.ShapeDtypeStruct((N_GX, 32, 128), BF16),
-        ),
-        in_specs=[VMEM] * 4,
-        out_specs=(VMEM,) * 3,
-        scratch_shapes=[
-            pltpu.VMEM((4, DEVICES, 128), F32),
-            pltpu.VMEM((DEVICES, 4, 128), F32),
-            pltpu.VMEM((CX * NZ, CY), BF16),
-            pltpu.VMEM((2, 32, 128), BF16),
-            pltpu.SemaphoreType.DMA((2,)),
-            pltpu.SemaphoreType.DMA((2,)),
-            pltpu.SemaphoreType.DMA((3,)),
-        ],
-        compiler_params=pltpu.CompilerParams(
-            collective_id=0, has_side_effects=True, vmem_limit_bytes=48 * MIB
-        ),
-    )(cell, test, value, classes)
-
-
-def roll_to(value, shift):
-    shift = shift % 128
-    return pltpu.roll(value, shift, 1) if shift else value
-
-
-def tile(j):
-    return slice(8 * j, 8 * j + 8)
-
-
-def source_kernel(
-    wells_ref, cls_ref, edge_ref, class_value_ref, cond, src_ref, rows, plane, acc
-):
-    half = lax.axis_index("gx") // 4
 
     from_lane = lax.broadcasted_iota(jnp.int32, (128, 128), 0)
     to_lane = lax.broadcasted_iota(jnp.int32, (128, 128), 1)
@@ -310,6 +265,54 @@
             for j in range(8):
                 cond[x_low, y_low, tile(j), :] = plane[pl.ds(j, 8, stride=8), :]
 
+    rest = pl.ds(0, DEVICES - 1)
+    pltpu.make_async_copy(wells_ref.at[rest], wells_ref.at[rest], wells_sem.at[1]).wait()
+    pltpu.make_async_copy(send.at[rest], send.at[rest], wells_sem.at[0]).wait()
+    pltpu.make_async_copy(cls_ref.at[seven], cls_ref.at[seven], cls_sem.at[0]).wait()
+    four = pl.ds(0, 4)
+
+    @pl.when(gy > 0)
+    def _():
+        pltpu.make_async_copy(edge_ref.at[four], edge_ref.at[four], edge_sem.at[0]).wait()
+
+    @pl.when(gy < N_GY - 1)
+    def _():
+        pltpu.make_async_copy(edge_ref.at[four], edge_ref.at[four], edge_sem.at[1]).wait()
+
+
+def share_call(cell, test, value, classes, class_value):
+    return pl.pallas_call(
+        share_kernel,
+        out_shape=(
+            jax.ShapeDtypeStruct((DEVICES, 4, 128), F32),
+            jax.ShapeDtypeStruct(FIELD, F32),
+        ),
+        in_specs=[VMEM] * 4 + [pl.BlockSpec(memory_space=pltpu.SMEM)],
+        out_specs=(VMEM,) * 2,
+        scratch_shapes=[
+            pltpu.VMEM((N_GX, CX * NZ, CY), BF16),
+            pltpu.VMEM((N_GX, 32, 128), BF16),
+            pltpu.VMEM((NZ, 128), F32),
+            pltpu.VMEM((4, DEVICES, 128), F32),
+            pltpu.VMEM((DEVICES, 4, 128), F32),
+            pltpu.VMEM((CX * NZ, CY), BF16),
+            pltpu.VMEM((2, 32, 128), BF16),
+            pltpu.SemaphoreType.DMA((2,)),
+            pltpu.SemaphoreType.DMA((2,)),
+            pltpu.SemaphoreType.DMA((3,)),
+        ],
+        compiler_params=pltpu.CompilerParams(
+            collective_id=0, has_side_effects=True, vmem_limit_bytes=48 * MIB
+        ),
+    )(cell, test, value, classes, class_value)
+
+
+def roll_to(value, shift):
+    shift = shift % 128
+    return pltpu.roll(value, shift, 1) if shift else value
+
+
+def source_kernel(wells_ref, src_ref, rows, acc):
     for dev in range(DEVICES):
         for k in range(4):
             rows[k, dev : dev + 1, :] = wells_ref[dev, k : k + 1, :]
@@ -359,22 +362,15 @@
             src_ref[x_low, y_low] = acc[at : at + NZ, x_low // 4 * 128 : x_low // 4 * 128 + 128]
 
 
-FIELD = (XL, YL, NZ, 128)
-
-
-def source_call(wells, classes, edges, class_value):
+def source_call(wells):
     return pl.pallas_call(
         source_kernel,
-        out_shape=(jax.ShapeDtypeStruct(FIELD, F32),) * 2,
-        in_specs=[VMEM] * 3 + [pl.BlockSpec(memory_space=pltpu.SMEM)],
-        out_specs=(VMEM,) * 2,
-        scratch_shapes=[
-            pltpu.VMEM((4, DEVICES, 128), F32),
-            pltpu.VMEM((NZ, 128), F32),
-            pltpu.VMEM((HIGHS, 256), F32),
-        ],
+        out_shape=jax.ShapeDtypeStruct(FIELD, F32),
+        in_specs=[VMEM],
+        out_specs=VMEM,
+        scratch_shapes=[pltpu.VMEM((4, DEVICES, 128), F32), pltpu.VMEM((HIGHS, 256), F32)],
         compiler_params=pltpu.CompilerParams(vmem_limit_bytes=48 * MIB),
-    )(wells, classes, edges, class_value)
+    )(wells)
 
 
 def groups_of(gx, gy):
@@ -490,15 +486,15 @@
         return pltpu.make_async_remote_copy(
             src_ref=src(dev),
             dst_ref=dst,
-            send_sem=sems.at[0],
-            recv_sem=sems.at[1],
+            send_sem=sems[0],
+            recv_sem=sems[1],
             device_id=(dev, gy),
             device_id_type=MESH,
         )
 
     for k in range(1, N_GX):
-        to_column(k, lambda dev: zone_out.at[dev // TESTS], zone_in.at[gx], zone_sem).start()
-        to_column(k, lambda dev: draw_out.at[dev], draw_in.at[gx], draw_sem).start()
+        to_column(k, lambda dev: zone_out.at[dev // TESTS], zone_in.at[gx], (zone_sem.at[N_GX], zone_sem.at[gx])).start()
+        to_column(k, lambda dev: draw_out.at[dev], draw_in.at[gx], (draw_sem.at[N_GX], draw_sem.at[gx])).start()
     zone_in[gx] = zone_out[half]
     draw_in[gx] = draw_out[gx]
 
@@ -648,9 +644,6 @@
 
 
     seven = pl.ds(0, N_GX - 1)
-    for ref, sems in ((zone_in, zone_sem), (draw_in, draw_sem)):
-        pltpu.make_async_copy(ref.at[seven], ref.at[seven], sems.at[1]).wait()
-        pltpu.make_async_copy(ref.at[seven], ref.at[seven], sems.at[0]).wait()
 
     inner = lax.broadcasted_iota(jnp.int32, (256, 128), 0).astype(F32).astype(BF16)
     one, nil = jnp.ones((), BF16), jnp.zeros((), BF16)
@@ -658,11 +651,20 @@
     def spread(row, times):
         return jnp.concatenate([jnp.broadcast_to(row, (16, 128)).astype(BF16)] * times, axis=0)
 
-    def step(o, _):
+    def step(k, _):
+        o = lax.rem(gx + k, N_GX)
+
+        @pl.when(k > 0)
+        def _():
+            for ref, sems in ((zone_in, zone_sem), (draw_in, draw_sem)):
+                pltpu.make_async_copy(ref.at[o], ref.at[o], sems.at[o]).wait()
+
         zone = zone_in[o]
         value = sens[o] * draw_in[o].astype(F32)
-        outer = ((zone + 0.5) * (1.0 / INNER)).astype(jnp.int32).astype(F32)
-        place = zone - outer * INNER
+        outer = ((zone + 0.5) * (1.0 / INNER)).astype(jnp.int32)
+        place = zone - outer.astype(F32) * INNER
+        outer = outer // 2 % N_GY * 16 + outer // 32 * 2 + outer % 2
+        outer = outer.astype(F32)
         left, right = [], []
         for r in range(2 * NZ):
             row = slice(r, r + 1)
@@ -692,9 +694,7 @@
     acc[...] = jnp.zeros_like(acc)
     lax.fori_loop(0, N_GX, step, 0)
 
-    turned = acc[...].T
-    for dev in range(DEVICES):
-        send_a[dev % N_GY, dev // N_GY] = turned[2 * dev : 2 * dev + 2, :]
+    send_a[...] = acc[...].T.astype(BF16).reshape(N_GY, 16, INNER)
 
     def row_copy(k):
         dev = lax.rem(gy + k, N_GY)
@@ -712,13 +712,13 @@
     recv_a[gy] = send_a[gy]
     rest = pl.ds(0, N_GY - 1)
     pltpu.make_async_copy(recv_a.at[rest], recv_a.at[rest], a_sem.at[1]).wait()
+    total = recv_a[0].astype(F32)
+    for n in range(1, N_GY):
+        total = total + recv_a[n].astype(F32)
     for o in range(N_GX):
-        total = recv_a[0, o]
-        for n in range(1, N_GY):
-            total = total + recv_a[n, o]
-        send_b[o] = total
+        send_b[o] = total[2 * o : 2 * o + 2, :]
     for k in range(1, N_GX):
-        to_column(k, lambda dev: send_b.at[dev], recv_b.at[gx], b_sem).start()
+        to_column(k, lambda dev: send_b.at[dev], recv_b.at[gx], (b_sem.at[0], b_sem.at[1])).start()
     recv_b[gx] = send_b[gx]
     pltpu.make_async_copy(recv_b.at[seven], recv_b.at[seven], b_sem.at[1]).wait()
     for t in range(TESTS):
@@ -749,6 +749,8 @@
 
     pltpu.make_async_copy(send_a.at[rest], send_a.at[rest], a_sem.at[0]).wait()
     pltpu.make_async_copy(send_b.at[seven], send_b.at[seven], b_sem.at[0]).wait()
+    pltpu.make_async_copy(zone_in.at[seven], zone_in.at[seven], zone_sem.at[N_GX]).wait()
+    pltpu.make_async_copy(draw_in.at[seven], draw_in.at[seven], draw_sem.at[N_GX]).wait()
     for place, held in ((0, low_group), (1, high_group)):
         for m in range(MEMBERS):
 
@@ -786,13 +788,13 @@
             pltpu.VMEM((N_GX, 2 * NZ, 128), BF16),
             pltpu.VMEM((N_GX, 2 * NZ, 128), F32),
             pltpu.VMEM((INNER, 256), F32),
-            pltpu.VMEM((N_GY, N_GX, 2, INNER), F32),
-            pltpu.VMEM((N_GY, N_GX, 2, INNER), F32),
+            pltpu.VMEM((N_GY, 16, INNER), BF16),
+            pltpu.VMEM((N_GY, 16, INNER), BF16),
             pltpu.VMEM((N_GX, 2, INNER), F32),
             pltpu.VMEM((N_GX, 2, INNER), F32),
             pltpu.VMEM((TESTS, SHARE), F32),
-            pltpu.SemaphoreType.DMA((2,)),
-            pltpu.SemaphoreType.DMA((2,)),
+            pltpu.SemaphoreType.DMA((N_GX + 1,)),
+            pltpu.SemaphoreType.DMA((N_GX + 1,)),
             pltpu.SemaphoreType.DMA((2,)),
             pltpu.SemaphoreType.DMA((2,)),
             pltpu.SemaphoreType.DMA((2, MEMBERS)),
@@ -1025,10 +1027,10 @@
         [lax.dynamic_slice_in_dim(centroid, held * GROUP, GROUP, 1) for held in (low, high)]
     )
     pts = jnp.pad((pts - 0.5) * (LOG2E / corr_len), ((0, 0), (0, 5), (0, 0)))
-    wells, classes, edges = share_call(
-        well_cell[None], well_test[None], well_value[None], cond_class
+    wells, cond = share_call(
+        well_cell[None], well_test[None], well_value[None], cond_class, class_value
     )
-    cond, source = source_call(wells, classes, edges, class_value)
+    source = source_call(wells)
     rows = CX * NZ
     sums = main_call(
         cond, source, zone_id.reshape(rows, CY), drawdown.reshape(TESTS, rows, CY)

time: 185 us -> 178 us (0.962)
  Pallas kernels: 180 us -> 173 us
    pallas_call x1, Pallas kernels: 62.9 us -> 59 us  [main_call(): pl.pallas_call(main_kernel, out_shape=jax.ShapeDtypeStruct((2, MEMBERS, T...]
    pallas_call x1, Pallas kernels: 7.63 us -> 5.62 us  [source_call(): pl.pallas_call(source_kernel, out_shape=jax.ShapeDtypeStruct(FIELD, F32),...]
where the time goes in v5:
time: 178 us
  Pallas kernels  173 us (97%)
  local copies, waits for them, and re-layouts  5.26 us (3%)
    pallas_call x1, Pallas kernels, cov_call(): pl.pallas_call(cov_kernel, out_shape=jax.ShapeDtypeStruct((2, 8, GROUP),...  62.4 us
    pallas_call x1, Pallas kernels, main_call(): pl.pallas_call(main_kernel, out_shape=jax.ShapeDtypeStruct((2, MEMBERS, T...  59 us
    pallas_call x1, Pallas kernels, share_call(): pl.pallas_call(share_kernel, out_shape=(jax.ShapeDtypeStruct((DEVICES, 4,...  24.8 us
    pallas_call x1, Pallas kernels, reduce_call(): pl.pallas_call(reduce_kernel, out_shape=jax.ShapeDtypeStruct((TESTS, SHAR...  20.6 us
    pallas_call x1, Pallas kernels, source_call(): pl.pallas_call(source_kernel, out_shape=jax.ShapeDtypeStruct(FIELD, F32),...  5.62 us
    unnamed x15, local copies, waits for them, and re-layouts  4.2 us

profile of v5, /device:TPU:1, one launch (start us, length us, event | category | flops | bytes accessed | tf_op | source)
XLA Modules:
  0.0 177.9 jit_solution(12839552516937596792)
XLA Ops:
  0.0 0.0 copy-start
  0.0 0.0 copy-start.1
  0.0 1.0 dynamic-slice_bitcast_fusion.1
  1.0 0.1 fusion
  1.2 0.0 copy-start.2
  1.2 0.9 copy-done.2
  2.1 0.0 copy-start.3
  2.1 0.7 copy-done.3
  2.7 0.0 copy-start.4
  2.7 0.7 copy-done.4
  3.4 0.0 copy-start.5
  3.4 0.7 copy-done.5
  4.1 0.0 copy-start.6
  4.1 0.7 copy-done.6
  4.8 24.8 %shard_map.82 = (f32[128,4,128]{2,1,0:T(4,128)S(1)}, f32[8,3,64,128]{3,2,1,0:T(8,128)S(1)}) custom-call(s32[1,512]{1,0:T(1,128)S(1)} %bitcast.12, s32[1,512]{1,0:T(1,128)S(1)} %bitcast.13, f32[1,512]{1,0:T(1,128)S(1)} %bitcast.14, s32[4,64,128]{2,1,0:T(8,128)S(1)} %copy-done.2, f32[16]{0:T(128)S(1)} %copy-done.6), custom_call_target="tpu_custom_call" | custom-call | tf_op jit(solution)/shard_map/pallas_call | solution.py:284
  29.6 5.6 %shard_map.83.src_ref = f32[8,3,64,128]{3,2,1,0:T(8,128)S(1)} custom-call(f32[128,4,128]{2,1,0:T(4,128)S(1)} %get-tuple-element.8.wells_ref), custom_call_target="tpu_custom_call" | custom-call | tf_op jit(solution)/shard_map/pallas_call | solution.py:366
  35.2 0.0 copy-done
  35.2 0.0 copy-done.1
  35.2 59.0 %shard_map.84.sums_ref = f32[2,8,4,768]{3,2,1,0:T(4,128)S(1)} custom-call(f32[8,3,64,128]{3,2,1,0:T(8,128)S(1)} %get-tuple-element.7.cond, f32[8,3,64,128]{3,2,1,0:T(8,128)S(1)} %shard_map.83.src_ref, s32[256,128]{1,0:T(8,128)S(1)} %bitcast.11, bf16[4,256,128]{2,1,0:T(8,128)(2,1)S(1)} %bitcast.10), custom_call_target="tpu_custom_call" | custom-call | tf_op jit(solution)/shard_map/pallas_call | solution.py:771
  94.3 62.4 %shard_map.85.part_ref = f32[2,8,6144]{2,1,0:T(8,128)S(1)} custom-call(s32[1]{0:T(128)} %bitcast.diag_ref, f32[2,8,6144]{2,1,0:T(8,128)S(1)} %pad.4.pts_ref, f32[2,8,4,768]{3,2,1,0:T(4,128)S(1)} %shard_map.84.sums_ref), custom_call_target="tpu_custom_call" | custom-call | tf_op jit(solution)/shard_map/pallas_call | solution.py:912
  156.7 20.6 %shard_map.86 = bf16[4,768]{1,0:T(4,128)(2,1)S(1)} custom-call(f32[2,8,6144]{2,1,0:T(8,128)S(1)} %shard_map.85.part_ref), custom_call_target="tpu_custom_call" | custom-call | tf_op jit(solution)/shard_map/pallas_call | solution.py:1004
  177.3 0.6 copy.10
  (1 shorter events, 0.0 us)
Async XLA Ops:
  0.0 35.2 %copy-start = (bf16[4,4,64,128]{3,2,1,0:T(8,128)(2,1)S(1)}, bf16[4,4,64,128]{3,2,1,0:T(8,128)(2,1)}, u32[]{:S(2)}) copy-start(bf16[4,4,64,128]{3,2,1,0:T(8,128)(2,1)} %param.14) | copy-start | bytes 786436
  0.0 35.2 %copy-start.1 = (s32[4,64,128]{2,1,0:T(8,128)S(1)}, s32[4,64,128]{2,1,0:T(8,128)}, u32[]{:S(2)}) copy-start(s32[4,64,128]{2,1,0:T(8,128)} %param.13) | copy-start | bytes 393220
  1.2 0.9 copy-start.2
  2.1 0.7 copy-start.3
  2.7 0.7 copy-start.4
  3.4 0.7 copy-start.5
  4.1 0.7 copy-start.6

commit v6 on v5

--- a/solution.py
+++ b/solution.py
@@ -59,13 +59,6 @@
 
 def coords(dev):
     return (dev // N_GY, dev % N_GY)
-
-
-def greet(devs):
-    barrier = pltpu.get_barrier_semaphore()
-    for dev in devs:
-        pl.semaphore_signal(barrier, inc=1, device_id=dev, device_id_type=MESH)
-    pl.semaphore_wait(barrier, len(devs))
 
 
 def for_others(act):
@@ -808,6 +801,7 @@
 
 ROWS, COLS = 1024, 512
 TERMS = 128
+HELP = 4
 
 
 def pieces(value):
@@ -834,27 +828,66 @@
 
 
 def cov_kernel(
-    diag_ref, pts_ref, sums_ref, out_ref, z_ref, z_turned, row_terms, col_terms, near, total
+    pts_ref,
+    sums_ref,
+    out_ref,
+    products,
+    z_ref,
+    z_turned,
+    row_terms,
+    col_terms,
+    near,
+    total,
+    send_c,
+    recv_c,
+    give_sem,
+    take_sem,
 ):
-    diag = diag_ref[0]
-    out_ref[...] = jnp.zeros_like(out_ref)
+    me = my_index()
+    gx, gy = lax.axis_index("gx"), lax.axis_index("gy")
+    low_group, high_group, is_diag = groups_of(gx, gy)
+    group, member = me // MEMBERS, me % MEMBERS
+    mode = is_diag.astype(jnp.int32) + 2 * ((gx == N_GX - 1) & (gy < 8)).astype(jnp.int32)
+    takers = takers_of(group)
+    barrier = pltpu.get_barrier_semaphore()
+    for held in (low_group, high_group):
+        for m in range(MEMBERS):
+            owner = held * MEMBERS + m
+
+            @pl.when(owner != me)
+            def _():
+                pl.semaphore_signal(barrier, inc=1, device_id=coords(owner), device_id_type=MESH)
+
+    for dev, _ in takers:
+
+        @pl.when(dev[0] * N_GY + dev[1] != me)
+        def _():
+            pl.semaphore_signal(barrier, inc=1, device_id=dev, device_id_type=MESH)
+
+    products[...] = jnp.zeros_like(products)
     for g in range(2):
         for m in range(MEMBERS):
             both = jnp.concatenate([sums_ref[g, m], jnp.zeros((TESTS, SHARE), F32)], axis=0)
             z_ref[g, :, SHARE * m : SHARE * m + SHARE] = both.astype(BF16)
 
     def phase(rg, _):
-        cg = jnp.where(diag == 1, rg, 1)
+        square = (mode == 1) | (rg == 1)
+        cg = jnp.where(square, rg, 1)
         for i in range(GROUP // ROWS):
             at = slice(ROWS * i, ROWS * i + ROWS)
             row_terms[0:80, at] = terms(pts_ref[rg, :, at], True)
             row_terms[80:TERMS, at] = jnp.zeros((TERMS - 80, ROWS), F32)
-            col_terms[0:80, at] = terms(pts_ref[cg, :, at], False).astype(BF16)
-            col_terms[80:TERMS, at] = jnp.zeros((TERMS - 80, ROWS), BF16)
-            wide = jnp.concatenate(
-                [z_ref[cg, :, at].astype(F32), jnp.zeros((120, ROWS), F32)], axis=0
-            )
-            z_turned[at, :] = wide.T.astype(BF16)
+
+        @pl.when((mode == 1) | (rg == 0))
+        def _():
+            for i in range(GROUP // ROWS):
+                at = slice(ROWS * i, ROWS * i + ROWS)
+                col_terms[0:80, at] = terms(pts_ref[cg, :, at], False).astype(BF16)
+                col_terms[80:TERMS, at] = jnp.zeros((TERMS - 80, ROWS), BF16)
+                wide = jnp.concatenate(
+                    [z_ref[cg, :, at].astype(F32), jnp.zeros((120, ROWS), F32)], axis=0
+                )
+                z_turned[at, :] = wide.T.astype(BF16)
 
         def row_block(r, _):
             rs = pl.ds(pl.multiple_of(r * ROWS, ROWS), ROWS)
@@ -878,13 +911,13 @@
                 )
 
             def for_cols(c, weights, held):
-                out_ref[cg, :, at_cols(c)] += jnp.dot(
+                products[cg, :, at_cols(c)] += jnp.dot(
                     weights, held, preferred_element_type=F32
                 )
 
             every, lower = slice(0, ROWS), slice(COLS, ROWS)
 
-            @pl.when(diag == 1)
+            @pl.when(square)
             def _():
                 held = tile(2 * r, every)
                 for_rows(2 * r, every, held)
@@ -898,131 +931,98 @@
                     for_cols(c, z_row, held)
                 return 0
 
-            lax.fori_loop(jnp.where(diag == 1, r + 1, 0), GROUP // ROWS, two, 0)
-            out_ref[rg, :, rs] += total[...].T[0:8]
+            lax.fori_loop(jnp.where(square, r + 1, 0), GROUP // ROWS, two, 0)
+            products[rg, :, rs] += total[...].T[0:8]
             return 0
 
-        lax.fori_loop(0, GROUP // ROWS, row_block, 0)
+        begin = jnp.where((mode == 2) & (rg == 1), HELP, 0)
+        end = jnp.where((mode == 1) & (rg == 1), HELP, GROUP // ROWS)
+        lax.fori_loop(begin, end, row_block, 0)
         return 0
 
-    lax.fori_loop(0, 1 + diag, phase, 0)
-
-
-def cov_call(diag, pts, sums):
+    lax.fori_loop(0, jnp.where(mode == 0, 1, 2), phase, 0)
+
+    for g in range(2):
+        for m in range(MEMBERS):
+            send_c[g, m] = products[g, 0:TESTS, SHARE * m : SHARE * m + SHARE]
+
+    self_here = (low_group == group) | (high_group == group)
+    pl.semaphore_wait(barrier, 32 - 2 * self_here.astype(jnp.int32))
+
+    def give(place, m, held, slot):
+        return pltpu.make_async_remote_copy(
+            src_ref=send_c.at[place, m],
+            dst_ref=recv_c.at[slot],
+            send_sem=give_sem.at[place, m],
+            recv_sem=take_sem.at[slot],
+            device_id=coords(held * MEMBERS + m),
+            device_id_type=MESH,
+        )
+
+    sides = (
+        (0, low_group, jnp.where(is_diag, low_group, high_group)),
+        (1, high_group, jnp.where(is_diag, high_group, low_group)),
+    )
+    for place, held, slot in sides:
+        for m in range(MEMBERS):
+
+            @pl.when(held * MEMBERS + m != me)
+            def _():
+                give(place, m, held, slot).start()
+
+            @pl.when(held * MEMBERS + m == me)
+            def _():
+                recv_c[slot] = send_c[place, m]
+
+    own_slot = jnp.where(low_group == group, sides[0][2], sides[1][2])
+    for slot in range(GROUPS):
+
+        @pl.when(jnp.logical_not(self_here & (own_slot == slot)))
+        def _():
+            pltpu.make_async_copy(recv_c.at[slot], recv_c.at[slot], take_sem.at[slot]).wait()
+
+    final = recv_c[0]
+    for slot in range(1, GROUPS):
+        final = final + recv_c[slot]
+    out_ref[...] = final.astype(BF16)
+    for place, held, slot in sides:
+        for m in range(MEMBERS):
+
+            @pl.when(held * MEMBERS + m != me)
+            def _():
+                give(place, m, held, slot).wait_send()
+
+
+def cov_call(pts, sums):
     return pl.pallas_call(
         cov_kernel,
-        out_shape=jax.ShapeDtypeStruct((2, 8, GROUP), F32),
-        in_specs=[pl.BlockSpec(memory_space=pltpu.SMEM), VMEM, VMEM],
+        out_shape=jax.ShapeDtypeStruct((TESTS, SHARE), BF16),
+        in_specs=[VMEM, VMEM],
         out_specs=VMEM,
         scratch_shapes=[
+            pltpu.VMEM((2, 8, GROUP), F32),
             pltpu.VMEM((2, 8, GROUP), BF16),
             pltpu.VMEM((GROUP, 128), BF16),
             pltpu.VMEM((TERMS, GROUP), F32),
             pltpu.VMEM((TERMS, GROUP), BF16),
             pltpu.VMEM((ROWS, TERMS), BF16),
             pltpu.VMEM((ROWS, 128), F32),
-        ],
-        compiler_params=pltpu.CompilerParams(vmem_limit_bytes=48 * MIB),
-    )(diag, pts, sums)
-
-
-def reduce_kernel(part_ref, out_ref, send, recv, send_sem, recv_sem):
-    me = my_index()
-    gx, gy = lax.axis_index("gx"), lax.axis_index("gy")
-    low, high, diag = groups_of(gx, gy)
-    group, member = me // MEMBERS, me % MEMBERS
-    for g in range(2):
-        for m in range(MEMBERS):
-            send[g, m] = part_ref[g, 0:TESTS, SHARE * m : SHARE * m + SHARE]
-
-    takers = takers_of(group)
-    barrier = pltpu.get_barrier_semaphore()
-    for place, held in ((0, low), (1, high)):
-        for m in range(MEMBERS):
-            owner = held * MEMBERS + m
-
-            @pl.when(owner != me)
-            def _():
-                pl.semaphore_signal(barrier, inc=1, device_id=coords(owner), device_id_type=MESH)
-
-    for dev, _ in takers:
-
-        @pl.when(dev[0] * N_GY + dev[1] != me)
-        def _():
-            pl.semaphore_signal(barrier, inc=1, device_id=dev, device_id_type=MESH)
-
-    self_here = (low == group) | (high == group)
-    pl.semaphore_wait(barrier, 32 - 2 * self_here.astype(jnp.int32))
-
-    def put(place, m, held, slot):
-        return pltpu.make_async_remote_copy(
-            src_ref=send.at[place, m],
-            dst_ref=recv.at[slot],
-            send_sem=send_sem.at[place, m],
-            recv_sem=recv_sem.at[slot],
-            device_id=coords(held * MEMBERS + m),
-            device_id_type=MESH,
-        )
-
-    sides = (
-        (0, low, jnp.where(diag, low, high)),
-        (1, high, jnp.where(diag, high, low)),
-    )
-    for place, held, slot in sides:
-        for m in range(MEMBERS):
-
-            @pl.when(held * MEMBERS + m != me)
-            def _():
-                put(place, m, held, slot).start()
-
-            @pl.when(held * MEMBERS + m == me)
-            def _():
-                recv[slot] = send[place, m]
-
-    own_slot = jnp.where(
-        low == group, jnp.where(diag, low, high), jnp.where(diag, high, low)
-    )
-    for slot in range(GROUPS):
-
-        @pl.when(jnp.logical_not(self_here & (own_slot == slot)))
-        def _():
-            pltpu.make_async_copy(recv.at[slot], recv.at[slot], recv_sem.at[slot]).wait()
-
-    total = recv[0]
-    for slot in range(1, GROUPS):
-        total = total + recv[slot]
-    out_ref[...] = total.astype(BF16)
-    for place, held, slot in sides:
-        for m in range(MEMBERS):
-
-            @pl.when(held * MEMBERS + m != me)
-            def _():
-                put(place, m, held, slot).wait_send()
-
-
-def reduce_call(parts):
-    return pl.pallas_call(
-        reduce_kernel,
-        out_shape=jax.ShapeDtypeStruct((TESTS, SHARE), BF16),
-        in_specs=[VMEM],
-        out_specs=VMEM,
-        scratch_shapes=[
             pltpu.VMEM((2, MEMBERS, TESTS, SHARE), F32),
             pltpu.VMEM((GROUPS, TESTS, SHARE), F32),
             pltpu.SemaphoreType.DMA((2, MEMBERS)),
             pltpu.SemaphoreType.DMA((GROUPS,)),
         ],
         compiler_params=pltpu.CompilerParams(
-            collective_id=2, has_side_effects=True, vmem_limit_bytes=32 * MIB
+            collective_id=2, has_side_effects=True, vmem_limit_bytes=48 * MIB
         ),
-    )(parts)
+    )(pts, sums)
 
 
 def per_device(
     well_cell, well_test, well_value, cond_class, class_value, zone_id, drawdown, centroid
 ):
     gx, gy = lax.axis_index("gx"), lax.axis_index("gy")
-    low, high, diag = groups_of(gx, gy)
+    low, high, _ = groups_of(gx, gy)
     pts = jnp.stack(
         [lax.dynamic_slice_in_dim(centroid, held * GROUP, GROUP, 1) for held in (low, high)]
     )
@@ -1035,8 +1035,7 @@
     sums = main_call(
         cond, source, zone_id.reshape(rows, CY), drawdown.reshape(TESTS, rows, CY)
     )
-    parts = cov_call(diag.astype(jnp.int32)[None], pts, sums)
-    return reduce_call(parts)
+    return cov_call(pts, sums)
 
 
 def solution(mesh):

time: 178 us -> 174 us (0.978)
  Pallas kernels: 173 us -> 168 us
    pallas_call x2 -> x1, Pallas kernels: 83.1 us -> 79.4 us  [cov_call(): pl.pallas_call(cov_kernel, out_shape=jax.ShapeDtypeStruct((TESTS, SHARE),...]
where the time goes in v6:
time: 174 us
  Pallas kernels  168 us (97%)
  local copies, waits for them, and re-layouts  5.26 us (3%)
    pallas_call x1, Pallas kernels, cov_call(): pl.pallas_call(cov_kernel, out_shape=jax.ShapeDtypeStruct((TESTS, SHARE),...  79.4 us
    pallas_call x1, Pallas kernels, main_call(): pl.pallas_call(main_kernel, out_shape=jax.ShapeDtypeStruct((2, MEMBERS, T...  58.3 us
    pallas_call x1, Pallas kernels, share_call(): pl.pallas_call(share_kernel, out_shape=(jax.ShapeDtypeStruct((DEVICES, 4,...  24.8 us
    pallas_call x1, Pallas kernels, source_call(): pl.pallas_call(source_kernel, out_shape=jax.ShapeDtypeStruct(FIELD, F32),...  5.62 us
    unnamed x15, local copies, waits for them, and re-layouts  4.2 us

profile of v6, /device:TPU:1, one launch (start us, length us, event | category | flops | bytes accessed | tf_op | source)
XLA Modules:
  0.0 173.5 jit_solution(10029617858973060310)
XLA Ops:
  0.0 0.0 copy-start
  0.0 0.0 copy-start.1
  0.0 1.0 dynamic-slice_bitcast_fusion.1
  1.0 0.1 fusion
  1.2 0.0 copy-start.2
  1.2 0.9 copy-done.2
  2.1 0.0 copy-start.3
  2.1 0.7 copy-done.3
  2.7 0.0 copy-start.4
  2.7 0.7 copy-done.4
  3.4 0.0 copy-start.5
  3.4 0.7 copy-done.5
  4.1 0.0 copy-start.6
  4.1 0.7 copy-done.6
  4.8 24.8 %shard_map.82 = (f32[128,4,128]{2,1,0:T(4,128)S(1)}, f32[8,3,64,128]{3,2,1,0:T(8,128)S(1)}) custom-call(s32[1,512]{1,0:T(1,128)S(1)} %bitcast.11, s32[1,512]{1,0:T(1,128)S(1)} %bitcast.12, f32[1,512]{1,0:T(1,128)S(1)} %bitcast.13, s32[4,64,128]{2,1,0:T(8,128)S(1)} %copy-done.2, f32[16]{0:T(128)S(1)} %copy-done.6), custom_call_target="tpu_custom_call" | custom-call | tf_op jit(solution)/shard_map/pallas_call | solution.py:277
  29.6 5.6 %shard_map.83.src_ref = f32[8,3,64,128]{3,2,1,0:T(8,128)S(1)} custom-call(f32[128,4,128]{2,1,0:T(4,128)S(1)} %get-tuple-element.8.wells_ref), custom_call_target="tpu_custom_call" | custom-call | tf_op jit(solution)/shard_map/pallas_call | solution.py:359
  35.2 0.0 copy-done
  35.2 0.0 copy-done.1
  35.2 58.3 %shard_map.84.sums_ref = f32[2,8,4,768]{3,2,1,0:T(4,128)S(1)} custom-call(f32[8,3,64,128]{3,2,1,0:T(8,128)S(1)} %get-tuple-element.7.cond, f32[8,3,64,128]{3,2,1,0:T(8,128)S(1)} %shard_map.83.src_ref, s32[256,128]{1,0:T(8,128)S(1)} %bitcast.10, bf16[4,256,128]{2,1,0:T(8,128)(2,1)S(1)} %bitcast.9), custom_call_target="tpu_custom_call" | custom-call | tf_op jit(solution)/shard_map/pallas_call | solution.py:764
  93.5 79.4 %shard_map.85 = bf16[4,768]{1,0:T(4,128)(2,1)S(1)} custom-call(f32[2,8,6144]{2,1,0:T(8,128)S(1)} %pad.4.pts_ref, f32[2,8,4,768]{3,2,1,0:T(4,128)S(1)} %shard_map.84.sums_ref), custom_call_target="tpu_custom_call" | custom-call | tf_op jit(solution)/shard_map/pallas_call | solution.py:997
  172.9 0.6 copy.10
  (1 shorter events, 0.0 us)
Async XLA Ops:
  0.0 35.2 %copy-start = (bf16[4,4,64,128]{3,2,1,0:T(8,128)(2,1)S(1)}, bf16[4,4,64,128]{3,2,1,0:T(8,128)(2,1)}, u32[]{:S(2)}) copy-start(bf16[4,4,64,128]{3,2,1,0:T(8,128)(2,1)} %param.14) | copy-start | bytes 786436
  0.0 35.2 %copy-start.1 = (s32[4,64,128]{2,1,0:T(8,128)S(1)}, s32[4,64,128]{2,1,0:T(8,128)}, u32[]{:S(2)}) copy-start(s32[4,64,128]{2,1,0:T(8,128)} %param.13) | copy-start | bytes 393220
  1.2 0.9 copy-start.2
  2.1 0.7 copy-start.3
  2.7 0.7 copy-start.4
  3.4 0.7 copy-start.5
  4.1 0.7 copy-start.6

commit v7 on v6

--- a/solution.py
+++ b/solution.py
@@ -80,10 +80,10 @@
 
 
 def share_kernel(
-    cell_ref,
-    test_ref,
-    value_ref,
-    class_ref,
+    cell_in,
+    test_in,
+    value_in,
+    class_in,
     class_value_ref,
     wells_ref,
     cond,
@@ -97,7 +97,25 @@
     wells_sem,
     cls_sem,
     edge_sem,
+    cell_ref,
+    test_ref,
+    value_ref,
+    class_ref,
+    in_sem,
 ):
+    inputs = [
+        pltpu.make_async_copy(src, dst, in_sem.at[n])
+        for n, (src, dst) in enumerate(
+            (
+                (cell_in, cell_ref),
+                (test_in, test_ref),
+                (value_in, value_ref),
+                (class_in, class_ref),
+            )
+        )
+    ]
+    for copy in inputs:
+        copy.start()
     me = my_index()
     gx, gy = lax.axis_index("gx"), lax.axis_index("gy")
     edge_ref[...] = jnp.zeros_like(edge_ref)
@@ -105,6 +123,8 @@
     for_others(
         lambda dev: pl.semaphore_signal(barrier, inc=1, device_id=dev, device_id_type=MESH)
     )
+    for copy in inputs:
+        copy.wait()
     lane = lax.broadcasted_iota(jnp.int32, (32, 128), 1)
     classes = class_ref[...].reshape(CX * NZ, CY).astype(F32)
     mine[...] = classes.astype(BF16)
@@ -280,7 +300,8 @@
             jax.ShapeDtypeStruct((DEVICES, 4, 128), F32),
             jax.ShapeDtypeStruct(FIELD, F32),
         ),
-        in_specs=[VMEM] * 4 + [pl.BlockSpec(memory_space=pltpu.SMEM)],
+        in_specs=[pl.BlockSpec(memory_space=pl.ANY)] * 4
+        + [pl.BlockSpec(memory_space=pltpu.SMEM)],
         out_specs=(VMEM,) * 2,
         scratch_shapes=[
             pltpu.VMEM((N_GX, CX * NZ, CY), BF16),
@@ -293,6 +314,11 @@
             pltpu.SemaphoreType.DMA((2,)),
             pltpu.SemaphoreType.DMA((2,)),
             pltpu.SemaphoreType.DMA((3,)),
+            pltpu.VMEM(cell.shape, jnp.int32),
+            pltpu.VMEM(test.shape, jnp.int32),
+            pltpu.VMEM(value.shape, F32),
+            pltpu.VMEM(classes.shape, jnp.int32),
+            pltpu.SemaphoreType.DMA((4,)),
         ],
         compiler_params=pltpu.CompilerParams(
             collective_id=0, has_side_effects=True, vmem_limit_bytes=48 * MIB

time: 174 us -> 174 us (level)
  no operation moved by 1% of the time
where the time goes in v7:
time: 174 us
  Pallas kernels  169 us (97%)
  local copies, waits for them, and re-layouts  5.26 us (3%)
    pallas_call x1, Pallas kernels, cov_call(): pl.pallas_call(cov_kernel, out_shape=jax.ShapeDtypeStruct((TESTS, SHARE),...  79 us
    pallas_call x1, Pallas kernels, main_call(): pl.pallas_call(main_kernel, out_shape=jax.ShapeDtypeStruct((2, MEMBERS, T...  59 us
    pallas_call x1, Pallas kernels, share_call(): pl.pallas_call(share_kernel, out_shape=(jax.ShapeDtypeStruct((DEVICES, 4,...  25 us
    pallas_call x1, Pallas kernels, source_call(): pl.pallas_call(source_kernel, out_shape=jax.ShapeDtypeStruct(FIELD, F32),...  5.62 us
    unnamed x15, local copies, waits for them, and re-layouts  4.2 us

profile of v7, /device:TPU:1, one launch (start us, length us, event | category | flops | bytes accessed | tf_op | source)
XLA Modules:
  0.0 174.1 jit_solution(10811495543250453366)
XLA Ops:
  0.0 0.0 copy-start
  0.0 0.0 copy-start.1
  0.0 1.0 dynamic-slice_bitcast_fusion.1
  1.0 0.1 fusion
  1.2 0.0 copy-start.2
  1.2 0.9 copy-done.2
  2.1 0.0 copy-start.3
  2.1 0.7 copy-done.3
  2.7 0.0 copy-start.4
  2.7 0.7 copy-done.4
  3.4 0.0 copy-start.5
  3.4 0.7 copy-done.5
  4.1 0.0 copy-start.6
  4.1 0.7 copy-done.6
  4.8 25.0 %shard_map.82 = (f32[128,4,128]{2,1,0:T(4,128)S(1)}, f32[8,3,64,128]{3,2,1,0:T(8,128)S(1)}) custom-call(s32[1,512]{1,0:T(1,128)S(1)} %bitcast.11, s32[1,512]{1,0:T(1,128)S(1)} %bitcast.12, f32[1,512]{1,0:T(1,128)S(1)} %bitcast.13, s32[4,64,128]{2,1,0:T(8,128)S(1)} %copy-done.2, f32[16]{0:T(128)S(1)} %copy-done.6), custom_call_target="tpu_custom_call" | custom-call | tf_op jit(solution)/shard_map/pallas_call | solution.py:297
  29.8 5.6 %shard_map.83.src_ref = f32[8,3,64,128]{3,2,1,0:T(8,128)S(1)} custom-call(f32[128,4,128]{2,1,0:T(4,128)S(1)} %get-tuple-element.8.wells_ref), custom_call_target="tpu_custom_call" | custom-call | tf_op jit(solution)/shard_map/pallas_call | solution.py:385
  35.4 0.0 copy-done
  35.4 0.0 copy-done.1
  35.4 59.0 %shard_map.84.sums_ref = f32[2,8,4,768]{3,2,1,0:T(4,128)S(1)} custom-call(f32[8,3,64,128]{3,2,1,0:T(8,128)S(1)} %get-tuple-element.7.cond, f32[8,3,64,128]{3,2,1,0:T(8,128)S(1)} %shard_map.83.src_ref, s32[256,128]{1,0:T(8,128)S(1)} %bitcast.10, bf16[4,256,128]{2,1,0:T(8,128)(2,1)S(1)} %bitcast.9), custom_call_target="tpu_custom_call" | custom-call | tf_op jit(solution)/shard_map/pallas_call | solution.py:790
  94.5 79.0 %shard_map.85 = bf16[4,768]{1,0:T(4,128)(2,1)S(1)} custom-call(f32[2,8,6144]{2,1,0:T(8,128)S(1)} %pad.4.pts_ref, f32[2,8,4,768]{3,2,1,0:T(4,128)S(1)} %shard_map.84.sums_ref), custom_call_target="tpu_custom_call" | custom-call | tf_op jit(solution)/shard_map/pallas_call | solution.py:1023
  173.5 0.6 copy.10
  (1 shorter events, 0.0 us)
Async XLA Ops:
  0.0 35.4 %copy-start = (bf16[4,4,64,128]{3,2,1,0:T(8,128)(2,1)S(1)}, bf16[4,4,64,128]{3,2,1,0:T(8,128)(2,1)}, u32[]{:S(2)}) copy-start(bf16[4,4,64,128]{3,2,1,0:T(8,128)(2,1)} %param.14) | copy-start | bytes 786436
  0.0 35.4 %copy-start.1 = (s32[4,64,128]{2,1,0:T(8,128)S(1)}, s32[4,64,128]{2,1,0:T(8,128)}, u32[]{:S(2)}) copy-start(s32[4,64,128]{2,1,0:T(8,128)} %param.13) | copy-start | bytes 393220
  1.2 0.9 copy-start.2
  2.1 0.7 copy-start.3
  2.7 0.7 copy-start.4
  3.4 0.7 copy-start.5
  4.1 0.7 copy-start.6
